TPU v7x, 32 devices: a whole 2x2x4 slice. The times are simulated.
32 devices in a mesh: grp: 2 (over x), slc: 8 (over z, y), row: 2 (over core).
Axes of the slice: x: 2, y: 2, z: 4, core: 2. Of those that a mesh axis runs over, the one named last changes fastest.
Arguments:
- intensity: float32 [8, 32, 16, 512], P('grp', 'slc', 'row'), parts along dimension 0, may hold values from -6 to 6
- labels: int32 [8, 32, 16, 512], P('grp', 'slc', 'row'), parts along dimension 0, may hold values from 0 to 2
- strength: float32 [8, 32, 16, 512], P('grp', 'slc', 'row'), parts along dimension 0, may hold values from 0.5 to 8
- partner: int32 [6, 32, 16, 4], P('grp', 'slc', 'row'), parts along dimension 0, may hold values from 0 to 2047, as said below
Outputs:
- solution_field: float32 [8, 32, 16, 512], P('grp', 'slc', 'row'), parts along dimension 0
- residual: float32 [8, 32, 16, 512], P('grp', 'slc', 'row'), parts along dimension 0
There are 2 independent parts, one for each index of `grp`. A program takes and returns all parts, laid end to end along the dimension named above; each array names one. Nothing has to cross between parts.
Inputs may be any that keep to these rules, and one draw needn't show every extreme that they name: `partner`: at each of the 3 steps the ids over the whole grid form a permutation of all 2048 block ids. At one step, the number of a device's blocks whose partners lie on any one device is 0 or exactly 16, and each device owns the partners of blocks from exactly 8 devices, always including the device 16/2 away in the order of slc then row.
All inputs are finite; a program needn't handle non-finite values.
Results may differ from a plain program's by a relative error of at most 0.00011.
Values sent between devices are 32-bit elements; how exact they have to be, the bound alone decides.
No kernel may reach another device: no remote copies, remote signals or barrier semaphores. Data moves between devices by JAX's collectives and lax.ppermute only.
A program may use at most 64 MiB of HBM per device.

v0:
```python
import jax
import jax.numpy as jnp
from jax import lax
from jax.sharding import PartitionSpec as P

ITERS = 2


EDGE_SHARPNESS = 0.5
DIAGONAL_SHIFT = 0.1


def with_halo(cells, sides, width):
    for axis, dim in sides:
        count = lax.axis_size(axis)
        ends = count - 1
        head = lax.slice_in_dim(cells, 0, width, axis=dim)
        tail = lax.slice_in_dim(cells, cells.shape[dim] - width, cells.shape[dim], axis=dim)
        cells = jnp.concatenate(
            [
                lax.ppermute(tail, axis, [(i, (i + 1) % count) for i in range(ends)]),
                cells,
                lax.ppermute(head, axis, [((i + 1) % count, i) for i in range(ends)]),
            ],
            axis=dim,
        )
    return cells


def edge_weight(upper, lower):
    contrast = upper - lower
    return jnp.exp(-EDGE_SHARPNESS * contrast * contrast)


def select_rows(table, values):
    return jnp.einsum("tsb,tbc->tsc", table, values, precision=lax.Precision.HIGHEST)


def place_rows(table, values):
    return jnp.einsum("tsb,tsc->tbc", table, values, precision=lax.Precision.HIGHEST)


def widened(field):
    return with_halo(field, (("slc", 1), ("row", 2)), 1)


def send_out(payload):
    result = lax.all_to_all(payload, ("slc", "row"), split_axis=1, concat_axis=1, tiled=True)
    return result


def send_back(payload):
    result = lax.all_to_all(payload, ("slc", "row"), split_axis=1, concat_axis=1, tiled=True)
    return result


def spatial(field, padded, weight_z, weight_y, weight_x):
    coupled = weight_z[:, 1:] * (field - padded[:, 2:, 1:-1]) + weight_z[:, :-1] * (
        field - padded[:, :-2, 1:-1]
    )
    coupled = (
        coupled
        + weight_y[:, :, 1:] * (field - padded[:, 1:-1, 2:])
        + weight_y[:, :, :-1] * (field - padded[:, 1:-1, :-2])
    )
    right_cell = jnp.pad(field[..., 1:], ((0, 0), (0, 0), (0, 0), (0, 1)))
    left_cell = jnp.pad(field[..., :-1], ((0, 0), (0, 0), (0, 0), (1, 0)))
    weight_left = jnp.pad(weight_x[..., :-1], ((0, 0), (0, 0), (0, 0), (1, 0)))
    return coupled + weight_x * (field - right_cell) + weight_left * (field - left_cell)


def squares(residual):
    return lax.psum(jnp.sum(residual * residual), ("slc", "row"))


def local(intensity, labels, strength, partner):
    frame_count, slice_count, line_count, cell_count = intensity.shape
    time_links = partner.shape[0]
    owners = lax.axis_size("slc") * lax.axis_size("row")
    block_count = slice_count * line_count * (cell_count // 128)
    capacity = 2 * block_count // owners
    slot_total = owners * capacity
    partner_ids = partner.reshape(time_links, block_count)
    owner_of = partner_ids // block_count
    local_target = partner_ids - owner_of * block_count
    matches = (owner_of[:, :, None] == jnp.arange(owners, dtype=jnp.int32)[None, None, :]).astype(
        jnp.int32
    )
    earlier = jnp.cumsum(matches, axis=1) - matches
    ranked = jnp.sum(earlier * matches, axis=2)
    slot_of = owner_of * capacity + ranked
    slot_range = jnp.arange(slot_total, dtype=jnp.int32)
    block_range = jnp.arange(block_count, dtype=jnp.int32)
    chosen_mask = slot_of[:, None, :] == slot_range[None, :, None]
    targets = jnp.sum(jnp.where(chosen_mask, local_target[:, None, :] + 1, 0), axis=2) - 1
    chosen = chosen_mask.astype(jnp.float32)
    arrived = lax.all_to_all(
        targets.reshape(time_links, owners, capacity),
        ("slc", "row"),
        split_axis=1,
        concat_axis=1,
        tiled=True,
    )
    arrived = arrived.reshape(time_links, slot_total)
    landed = (arrived[:, :, None] == block_range[None, None, :]).astype(jnp.float32)

    def displaced(blocks):
        outgoing = select_rows(chosen, blocks[:-1]).reshape(time_links, owners, capacity, 128)
        own_values = select_rows(landed, blocks[1:]).reshape(time_links, owners, capacity, 128)
        incoming = send_out(outgoing).reshape(time_links, slot_total, 128)
        returned = send_back(own_values).reshape(time_links, slot_total, 128)
        return (place_rows(chosen, returned), place_rows(landed, incoming))

    padded_shade = widened(intensity)
    weight_z = edge_weight(padded_shade[:, 1:, 1:-1], padded_shade[:, :-1, 1:-1])
    weight_y = edge_weight(padded_shade[:, 1:-1, 1:], padded_shade[:, 1:-1, :-1])
    slice_index = lax.axis_index("slc")
    line_index = lax.axis_index("row")
    edge_z = jnp.arange(slice_count + 1)
    edge_y = jnp.arange(line_count + 1)
    inside_z = jnp.logical_not(
        (edge_z == 0) & (slice_index == 0)
        | (edge_z == slice_count) & (slice_index == lax.axis_size("slc") - 1)
    )
    inside_y = jnp.logical_not(
        (edge_y == 0) & (line_index == 0)
        | (edge_y == line_count) & (line_index == lax.axis_size("row") - 1)
    )
    weight_z = jnp.where(inside_z[None, :, None, None], weight_z, 0.0)
    weight_y = jnp.where(inside_y[None, None, :, None], weight_y, 0.0)
    weight_x = jnp.pad(
        edge_weight(intensity[..., 1:], intensity[..., :-1]), ((0, 0), (0, 0), (0, 0), (0, 1))
    )
    shade_blocks = intensity.reshape(frame_count, block_count, 128)
    shade_next, shade_prior = displaced(shade_blocks)
    weight_next = edge_weight(shade_blocks[:-1], shade_next)
    weight_prior = edge_weight(shade_prior, shade_blocks[1:])
    diagonal = DIAGONAL_SHIFT + jnp.where(labels > 0, strength, 0.0)
    right_side = jnp.where(labels == 1, strength, 0.0)
    solution_field = jnp.zeros_like(right_side)
    residual = right_side
    direction = right_side
    norm_now = squares(residual)
    for step in range(ITERS):
        padded = widened(direction)
        operate_blocks = direction.reshape(frame_count, block_count, 128)
        value_next, value_prior = displaced(operate_blocks)
        forward = weight_next * (operate_blocks[:-1] - value_next)
        backward = weight_prior * (operate_blocks[1:] - value_prior)
        empty = jnp.zeros_like(operate_blocks[:1])
        linking = jnp.concatenate([forward, empty], 0) + jnp.concatenate([empty, backward], 0)
        image = (
            diagonal * direction
            + spatial(direction, padded, weight_z, weight_y, weight_x)
            + linking.reshape(direction.shape)
        )
        alpha = norm_now / lax.psum(jnp.sum(direction * image), ("slc", "row"))
        solution_field = solution_field + alpha * direction
        residual = residual - alpha * image
        norm_next = squares(residual)
        direction = residual + norm_next / norm_now * direction
        norm_now = norm_next
    return (solution_field, residual)


def solution(mesh):
    return jax.shard_map(
        local,
        mesh=mesh,
        in_specs=(
            P("grp", "slc", "row", None),
            P("grp", "slc", "row", None),
            P("grp", "slc", "row", None),
            P("grp", "slc", "row", None),
        ),
        out_specs=(P("grp", "slc", "row", None), P("grp", "slc", "row", None)),
        check_vma=False,
    )
```

profile of v0, /device:TPU:0, one launch (start us, length us, event | category | flops | bytes accessed | tf_op | source)
XLA Modules:
  0.0 242.4 jit_solution(109477059247601622)
XLA Ops:
  0.6 0.9 copy.38
  3.1 7.4 %all-to-all-start = ((s32[3,16,16]{2,0,1:T(4,128)}), s32[3,16,16]{2,0,1:T(4,128)S(1)}, u32[]{:S(2)}, u32[]{:S(2)}) async-start(s32[3,16,16]{2,0,1:T(4,128)} %copy.39), calls=%async_computation | async-start | bytes 65536 | tf_op jit(solution)/shard_map/all_to_all | solution.py:97
  11.3 1.3 collective-permute-start.2
  12.6 4.5 %collective-permute-start.3 = (f32[4,1,8,512]{3,2,1,0:T(8,128)}, f32[4,1,8,512]{3,2,1,0:T(8,128)S(1)}, u32[]{:S(2)}, u32[]{:S(2)}) collective-permute-start(f32[4,1,8,512]{3,2,1,0:T(8,128)} %get-tuple-element.27), channel_id=1, source_target_pairs={{0,2},{2,4},{4,6},{6,8},{8,10},{10,12},{12,14},{1,3},{3,5},{5,7},{... | collective-permute-start | bytes 196616 | tf_op jit(solution)/shard_map/ppermute | solution.py:21
  17.8 4.7 %collective-permute-start.1 = (f32[4,1,8,512]{3,2,1,0:T(8,128)}, f32[4,1,8,512]{3,2,1,0:T(8,128)S(1)}, u32[]{:S(2)}, u32[]{:S(2)}) collective-permute-start(f32[4,1,8,512]{3,2,1,0:T(8,128)} %get-tuple-element.26), channel_id=1, source_target_pairs={{0,2},{2,4},{4,6},{6,8},{8,10},{10,12},{12,14},{1,3},{3,5},{5,7},{... | collective-permute-start | bytes 196616 | tf_op jit(solution)/shard_map/ppermute | solution.py:21
  22.5 1.3 collective-permute-start
  24.3 0.8 copy.49
  25.1 5.8 %all-to-all-start.3 = ((f32[3,16,16,128]{3,2,0,1:T(8,128)}), f32[3,16,16,128]{3,2,0,1:T(8,128)S(1)}, u32[]{:S(2)}, u32[]{:S(2)}) async-start(f32[3,16,16,128]{3,2,0,1:T(8,128)} %copy.49), calls=%async_computation.3 | async-start | bytes 786432 | tf_op jit(solution)/shard_map/all_to_all | solution.py:48
  31.3 0.8 copy.51
  32.3 0.9 fusion.71
  33.2 9.9 %all-to-all-done.3 = f32[3,16,16,128]{3,2,0,1:T(8,128)S(1)} async-done(((f32[3,16,16,128]{3,2,0,1:T(8,128)}), f32[3,16,16,128]{3,2,0,1:T(8,128)S(1)}, u32[]{:S(2)}, u32[]{:S(2)}) %all-to-all-start.3) | async-done | bytes 393248 | tf_op jit(solution)/shard_map/all_to_all | solution.py:48
  43.1 3.6 %all-to-all-start.4 = ((f32[3,16,16,128]{3,2,0,1:T(8,128)}), f32[3,16,16,128]{3,2,0,1:T(8,128)S(1)}, u32[]{:S(2)}, u32[]{:S(2)}) async-start(f32[3,16,16,128]{3,2,0,1:T(8,128)} %copy.51), calls=%async_computation.4 | async-start | bytes 786432 | tf_op jit(solution)/shard_map/all_to_all | solution.py:48
  48.4 0.8 copy.46
  49.9 2.9 %collective-permute-start.7 = (f32[4,6,1,512]{3,2,1,0:T(1,128)}, f32[4,6,1,512]{3,2,1,0:T(1,128)}, u32[]{:S(2)}, u32[]{:S(2)}) collective-permute-start(f32[4,6,1,512]{3,2,1,0:T(1,128)} %get-tuple-element.14), channel_id=1, source_target_pairs={{0,1},{2,3},{4,5},{6,7},{8,9},{10,11},{12,13},{14,15},{16,17},{18,... | collective-permute-start | bytes 147464 | tf_op jit(solution)/shard_map/ppermute | solution.py:21
  52.8 6.0 %all-to-all-done.4 = f32[3,16,16,128]{3,2,0,1:T(8,128)S(1)} async-done(((f32[3,16,16,128]{3,2,0,1:T(8,128)}), f32[3,16,16,128]{3,2,0,1:T(8,128)S(1)}, u32[]{:S(2)}, u32[]{:S(2)}) %all-to-all-start.4) | async-done | bytes 393248 | tf_op jit(solution)/shard_map/all_to_all | solution.py:48
  59.6 4.2 %all-to-all-start.1 = ((f32[3,16,16,128]{3,2,0,1:T(8,128)}), f32[3,16,16,128]{3,2,0,1:T(8,128)}, u32[]{:S(2)}, u32[]{:S(2)}) async-start(f32[3,16,16,128]{3,2,0,1:T(8,128)} %copy.42), calls=%async_computation.1 | async-start | bytes 786432 | tf_op jit(solution)/shard_map/all_to_all | solution.py:53
  63.9 2.1 collective-permute-start.5
  66.1 1.3 collective-permute-start.4
  67.4 1.3 collective-permute-start.6
  69.2 1.2 fusion.5
  70.4 0.8 copy.50
  71.6 0.8 copy.52
  72.4 3.7 %all-to-all-done.1 = f32[3,16,16,128]{3,2,0,1:T(8,128)} async-done(((f32[3,16,16,128]{3,2,0,1:T(8,128)}), f32[3,16,16,128]{3,2,0,1:T(8,128)}, u32[]{:S(2)}, u32[]{:S(2)}) %all-to-all-start.1) | async-done | bytes 393248 | tf_op jit(solution)/shard_map/all_to_all | solution.py:53
  76.0 4.2 %all-to-all-start.2 = ((f32[3,16,16,128]{3,2,0,1:T(8,128)}), f32[3,16,16,128]{3,2,0,1:T(8,128)}, u32[]{:S(2)}, u32[]{:S(2)}) async-start(f32[3,16,16,128]{3,2,0,1:T(8,128)} %copy.46), calls=%async_computation.2 | async-start | bytes 786432 | tf_op jit(solution)/shard_map/all_to_all | solution.py:53
  80.3 1.4 fusion.15
  82.1 1.0 copy.43
  83.7 8.8 %all-to-all-done.2 = f32[3,16,16,128]{3,2,0,1:T(8,128)} async-done(((f32[3,16,16,128]{3,2,0,1:T(8,128)}), f32[3,16,16,128]{3,2,0,1:T(8,128)}, u32[]{:S(2)}, u32[]{:S(2)}) %all-to-all-start.2) | async-done | bytes 393248 | tf_op jit(solution)/shard_map/all_to_all | solution.py:53
  92.5 1.0 copy.47
  95.2 1.8 multiply_reduce_fusion.2
  96.9 32.1 %all-reduce.10 = (f32[]{:T(128)}, f32[]{:T(128)}) all-reduce(f32[]{:T(128)} %get-tuple-element.3, f32[]{:T(128)} %get-tuple-element.2), channel_id=1, replica_groups=mesh['grp'=2,'slc'=8,'row'=2] {'slc','row'}, use_global_device_ids=true, to_apply=%region_1.2 | all-reduce | flops 2 | bytes 16 | tf_op jit(solution)/shard_map/psum | solution.py:73
  131.0 30.2 %psum.30 = f32[]{:T(128)} all-reduce(f32[]{:T(128)} %multiply_reduce_fusion.1), channel_id=1, replica_groups=mesh['grp'=2,'slc'=8,'row'=2] {'slc','row'}, use_global_device_ids=true, to_apply=%region_8.9 | all-reduce | flops 1 | bytes 8 | tf_op jit(solution)/shard_map/psum | solution.py:73
  162.9 0.8 copy.57
  163.7 4.2 %all-to-all-start.6 = ((f32[3,16,16,128]{3,2,0,1:T(8,128)}), f32[3,16,16,128]{3,2,0,1:T(8,128)}, u32[]{:S(2)}, u32[]{:S(2)}) async-start(f32[3,16,16,128]{3,2,0,1:T(8,128)} %copy.57), calls=%async_computation.6 | async-start | bytes 786432 | tf_op jit(solution)/shard_map/all_to_all | solution.py:48
  169.2 10.9 %all-to-all-done.6 = f32[3,16,16,128]{3,2,0,1:T(8,128)} async-done(((f32[3,16,16,128]{3,2,0,1:T(8,128)}), f32[3,16,16,128]{3,2,0,1:T(8,128)}, u32[]{:S(2)}, u32[]{:S(2)}) %all-to-all-start.6) | async-done | bytes 393248 | tf_op jit(solution)/shard_map/all_to_all | solution.py:48
  180.2 4.2 %all-to-all-start.5 = ((f32[3,16,16,128]{3,2,0,1:T(8,128)}), f32[3,16,16,128]{3,2,0,1:T(8,128)}, u32[]{:S(2)}, u32[]{:S(2)}) async-start(f32[3,16,16,128]{3,2,0,1:T(8,128)} %copy.54), calls=%async_computation.5 | async-start | bytes 786432 | tf_op jit(solution)/shard_map/all_to_all | solution.py:53
  184.4 1.3 collective-permute-start.8
  185.7 4.5 %collective-permute-start.9 = (f32[4,1,8,512]{3,2,1,0:T(8,128)S(1)}, f32[4,1,8,512]{3,2,1,0:T(8,128)S(1)}, u32[]{:S(2)}, u32[]{:S(2)}) collective-permute-start(f32[4,1,8,512]{3,2,1,0:T(8,128)S(1)} %get-tuple-element.19), channel_id=1, source_target_pairs={{0,2},{2,4},{4,6},{6,8},{8,10},{10,12},{12,14},{1,3},{3,5},{5,7},{... | collective-permute-start | bytes 196616 | tf_op jit(solution)/shard_map/ppermute | solution.py:21
  190.3 0.8 fusion.67
  191.3 2.7 %collective-permute-done.9 = f32[4,1,8,512]{3,2,1,0:T(8,128)S(1)} collective-permute-done((f32[4,1,8,512]{3,2,1,0:T(8,128)S(1)}, f32[4,1,8,512]{3,2,1,0:T(8,128)S(1)}, u32[]{:S(2)}, u32[]{:S(2)}) %collective-permute-start.9) | collective-permute-done | bytes 65568 | tf_op jit(solution)/shard_map/ppermute | solution.py:21
  194.7 1.9 collective-permute-start.11
  196.6 1.3 collective-permute-start.10
  197.9 1.0 copy.58
  199.0 1.1 fusion
  200.0 1.0 copy.55
  202.1 0.9 copy-done.8
  203.0 1.8 multiply_reduce_fusion
  204.8 35.4 %psum.31 = f32[]{:T(128)} all-reduce(f32[]{:T(128)} %get-tuple-element.6), channel_id=1, replica_groups=mesh['grp'=2,'slc'=8,'row'=2] {'slc','row'}, use_global_device_ids=true, to_apply=%region_10.11 | all-reduce | flops 1 | bytes 8 | tf_op jit(solution)/shard_map/psum | solution.py:157
  241.4 0.9 multiply_subtract_fusion
  (93 shorter events, 15.0 us)
Async XLA Ops:
  1.8 8.8 %copy-start.2 = (s32[4,4,8,512]{3,2,1,0:T(8,128)S(1)}, s32[4,4,8,512]{3,2,1,0:T(8,128)}, u32[]{:S(2)}) copy-start(s32[4,4,8,512]{3,2,1,0:T(8,128)} %param.5) | copy-start | bytes 786436
  2.0 8.6 %copy-start.1 = (f32[4,4,8,512]{3,2,1,0:T(8,128)S(1)}, f32[4,4,8,512]{3,2,1,0:T(8,128)}, u32[]{:S(2)}) copy-start(f32[4,4,8,512]{3,2,1,0:T(8,128)} %param.6) | copy-start | bytes 786436
  3.1 21.9 %all-to-all-start = ((s32[3,16,16]{2,0,1:T(4,128)}), s32[3,16,16]{2,0,1:T(4,128)S(1)}, u32[]{:S(2)}, u32[]{:S(2)}) async-start(s32[3,16,16]{2,0,1:T(4,128)} %copy.39), calls=%async_computation | async-start | bytes 65536 | tf_op jit(solution)/shard_map/all_to_all | solution.py:97
  10.6 6.5 %copy-start = (f32[4,4,8,512]{3,2,1,0:T(8,128)S(1)}, f32[4,4,8,512]{3,2,1,0:T(8,128)}, u32[]{:S(2)}) copy-start(f32[4,4,8,512]{3,2,1,0:T(8,128)} %param.4) | copy-start | bytes 786436
  11.3 37.9 %collective-permute-start.2 = (f32[4,1,8,512]{3,2,1,0:T(8,128)}, f32[4,1,8,512]{3,2,1,0:T(8,128)S(1)}, u32[]{:S(2)}, u32[]{:S(2)}) collective-permute-start(f32[4,1,8,512]{3,2,1,0:T(8,128)} %get-tuple-element.28), channel_id=1, source_target_pairs={{2,0},{4,2},{6,4},{8,6},{10,8},{12,10},{14,12},{3,1},{5,3},{7,5},{... | collective-permute-start | bytes 196616 | tf_op jit(solution)/shard_map/ppermute | solution.py:23
  12.6 36.6 %collective-permute-start.3 = (f32[4,1,8,512]{3,2,1,0:T(8,128)}, f32[4,1,8,512]{3,2,1,0:T(8,128)S(1)}, u32[]{:S(2)}, u32[]{:S(2)}) collective-permute-start(f32[4,1,8,512]{3,2,1,0:T(8,128)} %get-tuple-element.27), channel_id=1, source_target_pairs={{0,2},{2,4},{4,6},{6,8},{8,10},{10,12},{12,14},{1,3},{3,5},{5,7},{... | collective-permute-start | bytes 196616 | tf_op jit(solution)/shard_map/ppermute | solution.py:21
  17.8 35.0 %collective-permute-start.1 = (f32[4,1,8,512]{3,2,1,0:T(8,128)}, f32[4,1,8,512]{3,2,1,0:T(8,128)S(1)}, u32[]{:S(2)}, u32[]{:S(2)}) collective-permute-start(f32[4,1,8,512]{3,2,1,0:T(8,128)} %get-tuple-element.26), channel_id=1, source_target_pairs={{0,2},{2,4},{4,6},{6,8},{8,10},{10,12},{12,14},{1,3},{3,5},{5,7},{... | collective-permute-start | bytes 196616 | tf_op jit(solution)/shard_map/ppermute | solution.py:21
  22.5 41.3 %collective-permute-start = (f32[4,1,8,512]{3,2,1,0:T(8,128)}, f32[4,1,8,512]{3,2,1,0:T(8,128)S(1)}, u32[]{:S(2)}, u32[]{:S(2)}) collective-permute-start(f32[4,1,8,512]{3,2,1,0:T(8,128)} %get-tuple-element.25), channel_id=1, source_target_pairs={{2,0},{4,2},{6,4},{8,6},{10,8},{12,10},{14,12},{3,1},{5,3},{7,5},{... | collective-permute-start | bytes 196616 | tf_op jit(solution)/shard_map/ppermute | solution.py:23
  25.1 18.0 %all-to-all-start.3 = ((f32[3,16,16,128]{3,2,0,1:T(8,128)}), f32[3,16,16,128]{3,2,0,1:T(8,128)S(1)}, u32[]{:S(2)}, u32[]{:S(2)}) async-start(f32[3,16,16,128]{3,2,0,1:T(8,128)} %copy.49), calls=%async_computation.3 | async-start | bytes 786432 | tf_op jit(solution)/shard_map/all_to_all | solution.py:48
  43.1 15.7 %all-to-all-start.4 = ((f32[3,16,16,128]{3,2,0,1:T(8,128)}), f32[3,16,16,128]{3,2,0,1:T(8,128)S(1)}, u32[]{:S(2)}, u32[]{:S(2)}) async-start(f32[3,16,16,128]{3,2,0,1:T(8,128)} %copy.51), calls=%async_computation.4 | async-start | bytes 786432 | tf_op jit(solution)/shard_map/all_to_all | solution.py:48
  49.2 0.7 copy-start.11
  49.9 44.3 %collective-permute-start.7 = (f32[4,6,1,512]{3,2,1,0:T(1,128)}, f32[4,6,1,512]{3,2,1,0:T(1,128)}, u32[]{:S(2)}, u32[]{:S(2)}) collective-permute-start(f32[4,6,1,512]{3,2,1,0:T(1,128)} %get-tuple-element.14), channel_id=1, source_target_pairs={{0,1},{2,3},{4,5},{6,7},{8,9},{10,11},{12,13},{14,15},{16,17},{18,... | collective-permute-start | bytes 147464 | tf_op jit(solution)/shard_map/ppermute | solution.py:21
  58.8 0.8 copy-start.3
  59.6 16.4 %all-to-all-start.1 = ((f32[3,16,16,128]{3,2,0,1:T(8,128)}), f32[3,16,16,128]{3,2,0,1:T(8,128)}, u32[]{:S(2)}, u32[]{:S(2)}) async-start(f32[3,16,16,128]{3,2,0,1:T(8,128)} %copy.42), calls=%async_computation.1 | async-start | bytes 786432 | tf_op jit(solution)/shard_map/all_to_all | solution.py:53
  63.9 4.9 %copy-start.9 = (f32[4,6,8,512]{3,2,1,0:T(8,128)}, f32[4,6,8,512]{3,2,1,0:T(8,128)S(1)}, u32[]{:S(2)}) copy-start(f32[4,6,8,512]{3,2,1,0:T(8,128)S(1)} %constant_dynamic-update-slice_fusion) | copy-start | bytes 1179652
  63.9 4.8 %collective-permute-start.5 = (f32[4,6,1,512]{3,2,1,0:T(1,128)S(1)}, f32[4,6,1,512]{3,2,1,0:T(1,128)S(1)}, u32[]{:S(2)}, u32[]{:S(2)}) collective-permute-start(f32[4,6,1,512]{3,2,1,0:T(1,128)S(1)} %get-tuple-element.16), channel_id=1, source_target_pairs={{0,1},{2,3},{4,5},{6,7},{8,9},{10,11},{12,13},{14,15},{16,17},{18,... | collective-permute-start | bytes 147464 | tf_op jit(solution)/shard_map/ppermute | solution.py:21
  66.1 3.1 %collective-permute-start.4 = (f32[4,6,1,512]{3,2,1,0:T(1,128)S(1)}, f32[4,6,1,512]{3,2,1,0:T(1,128)S(1)}, u32[]{:S(2)}, u32[]{:S(2)}) collective-permute-start(f32[4,6,1,512]{3,2,1,0:T(1,128)S(1)} %get-tuple-element.15), channel_id=1, source_target_pairs={{1,0},{3,2},{5,4},{7,6},{9,8},{11,10},{13,12},{15,14},{17,16},{19,... | collective-permute-start | bytes 147464 | tf_op jit(solution)/shard_map/ppermute | solution.py:23
  67.4 26.8 %collective-permute-start.6 = (f32[4,6,1,512]{3,2,1,0:T(1,128)}, f32[4,6,1,512]{3,2,1,0:T(1,128)}, u32[]{:S(2)}, u32[]{:S(2)}) collective-permute-start(f32[4,6,1,512]{3,2,1,0:T(1,128)} %get-tuple-element.13), channel_id=1, source_target_pairs={{1,0},{3,2},{5,4},{7,6},{9,8},{11,10},{13,12},{15,14},{17,16},{19,... | collective-permute-start | bytes 147464 | tf_op jit(solution)/shard_map/ppermute | solution.py:23
  70.4 1.1 copy-start.4
  76.0 16.4 %all-to-all-start.2 = ((f32[3,16,16,128]{3,2,0,1:T(8,128)}), f32[3,16,16,128]{3,2,0,1:T(8,128)}, u32[]{:S(2)}, u32[]{:S(2)}) async-start(f32[3,16,16,128]{3,2,0,1:T(8,128)} %copy.46), calls=%async_computation.2 | async-start | bytes 786432 | tf_op jit(solution)/shard_map/all_to_all | solution.py:53
  80.3 1.4 copy-start.5
  94.1 0.8 copy-start.12
  94.1 1.0 copy-start.6
  94.1 1.0 copy-start.7
  163.7 16.4 %all-to-all-start.6 = ((f32[3,16,16,128]{3,2,0,1:T(8,128)}), f32[3,16,16,128]{3,2,0,1:T(8,128)}, u32[]{:S(2)}, u32[]{:S(2)}) async-start(f32[3,16,16,128]{3,2,0,1:T(8,128)} %copy.57), calls=%async_computation.6 | async-start | bytes 786432 | tf_op jit(solution)/shard_map/all_to_all | solution.py:48
  180.2 19.9 %all-to-all-start.5 = ((f32[3,16,16,128]{3,2,0,1:T(8,128)}), f32[3,16,16,128]{3,2,0,1:T(8,128)}, u32[]{:S(2)}, u32[]{:S(2)}) async-start(f32[3,16,16,128]{3,2,0,1:T(8,128)} %copy.54), calls=%async_computation.5 | async-start | bytes 786432 | tf_op jit(solution)/shard_map/all_to_all | solution.py:53
  184.4 6.9 %collective-permute-start.8 = (f32[4,1,8,512]{3,2,1,0:T(8,128)S(1)}, f32[4,1,8,512]{3,2,1,0:T(8,128)S(1)}, u32[]{:S(2)}, u32[]{:S(2)}) collective-permute-start(f32[4,1,8,512]{3,2,1,0:T(8,128)S(1)} %get-tuple-element.20), channel_id=1, source_target_pairs={{2,0},{4,2},{6,4},{8,6},{10,8},{12,10},{14,12},{3,1},{5,3},{7,5},{... | collective-permute-start | bytes 196616 | tf_op jit(solution)/shard_map/ppermute | solution.py:23
  185.7 8.3 %collective-permute-start.9 = (f32[4,1,8,512]{3,2,1,0:T(8,128)S(1)}, f32[4,1,8,512]{3,2,1,0:T(8,128)S(1)}, u32[]{:S(2)}, u32[]{:S(2)}) collective-permute-start(f32[4,1,8,512]{3,2,1,0:T(8,128)S(1)} %get-tuple-element.19), channel_id=1, source_target_pairs={{0,2},{2,4},{4,6},{6,8},{8,10},{10,12},{12,14},{1,3},{3,5},{5,7},{... | collective-permute-start | bytes 196616 | tf_op jit(solution)/shard_map/ppermute | solution.py:21
  194.0 0.7 copy-start.13
  194.7 7.3 %collective-permute-start.11 = (f32[4,6,1,512]{3,2,1,0:T(1,128)}, f32[4,6,1,512]{3,2,1,0:T(1,128)}, u32[]{:S(2)}, u32[]{:S(2)}) collective-permute-start(f32[4,6,1,512]{3,2,1,0:T(1,128)} %get-tuple-element.12), channel_id=1, source_target_pairs={{0,1},{2,3},{4,5},{6,7},{8,9},{10,11},{12,13},{14,15},{16,17},{18,... | collective-permute-start | bytes 147464 | tf_op jit(solution)/shard_map/ppermute | solution.py:21
  196.6 5.4 %collective-permute-start.10 = (f32[4,6,1,512]{3,2,1,0:T(1,128)}, f32[4,6,1,512]{3,2,1,0:T(1,128)}, u32[]{:S(2)}, u32[]{:S(2)}) collective-permute-start(f32[4,6,1,512]{3,2,1,0:T(1,128)} %get-tuple-element.11), channel_id=1, source_target_pairs={{1,0},{3,2},{5,4},{7,6},{9,8},{11,10},{13,12},{15,14},{17,16},{19,... | collective-permute-start | bytes 147464 | tf_op jit(solution)/shard_map/ppermute | solution.py:23
  201.0 0.9 copy-start.10
  202.0 1.0 copy-start.8
where the time goes:
time: 244 us; the launch traced here: 242 us
  blocking collectives  97.6 us (40%)
  starting transfers between devices  62.1 us (25%)
  waiting for transfers between devices  42.7 us (18%)
  local copies, waits for them, and re-layouts  18.8 us (8%)
  other arithmetic  8.96 us (4%)
  matrix products  7.01 us (3%)
  between operations  5.22 us (2%)
    psum x2, blocking collectives, squares(): return lax.psum(jnp.sum(residual * residual), ('slc', 'row'))  62.2 us
    psum x1, blocking collectives, local(): alpha = norm_now / lax.psum(jnp.sum(direction * image), ('slc', 'row'))  35.4 us
    all_to_all x3, waiting for transfers between devices, send_out(): lax.all_to_all(payload, ('slc', 'row'), split_axis=1, concat_axis=1, tile...  26.8 us
    ppermute x6, starting transfers between devices, with_halo(): lax.ppermute(tail, axis, [(i, (i + 1) % count) for i in range(ends)])  20.7 us
    all_to_all x3, starting transfers between devices, send_out(): lax.all_to_all(payload, ('slc', 'row'), split_axis=1, concat_axis=1, tile...  13.6 us
    all_to_all x3, starting transfers between devices, send_back(): lax.all_to_all(payload, ('slc', 'row'), split_axis=1, concat_axis=1, tile...  12.7 us
    all_to_all x3, waiting for transfers between devices, send_back(): lax.all_to_all(payload, ('slc', 'row'), split_axis=1, concat_axis=1, tile...  12.5 us
    ppermute x6, starting transfers between devices, with_halo(): lax.ppermute(head, axis, [((i + 1) % count, i) for i in range(ends)])  7.73 us
  transfers between devices with their start and end apart: 19, of which 8 were waited for; matrix products, arithmetic and copies ran while one was open for 9% of the time, Pallas kernels for 0%

commit v1 on v0

v1 whole, which is shorter than its diff:
```python
import jax
import jax.numpy as jnp
from jax import lax
from jax.experimental import pallas as pl
from jax.experimental.pallas import tpu as pltpu
from jax.sharding import PartitionSpec as P

EDGE_SHARPNESS = 0.5
DIAGONAL_SHIFT = 0.1
LANES = 128
SUBLANES = 8
AXES = ("slc", "row")
F32 = jnp.float32
VMEM_LIMIT = 40 * 1024 * 1024


def edge_weight(upper, lower):
    contrast = upper - lower
    return jnp.exp(-EDGE_SHARPNESS * contrast * contrast)


def to_blocks(cells):
    slices, _, width = cells.shape
    return jnp.concatenate(
        [cells[z, :, x : x + LANES] for z in range(slices) for x in range(0, width, LANES)],
        axis=0,
    )


def store_cells(ref, frame, blocks):
    _, slices, lines, width = ref.shape
    per_slice = width // LANES
    for z in range(slices):
        for x in range(per_slice):
            first = (z * per_slice + x) * lines
            ref[frame, z, :, x * LANES : (x + 1) * LANES] = blocks[first : first + lines]


def pick(one_hot, values):
    high = values.astype(jnp.bfloat16)
    rest = values - high.astype(F32)
    middle = rest.astype(jnp.bfloat16)
    low = (rest - middle.astype(F32)).astype(jnp.bfloat16)
    width = values.shape[1]
    out = jnp.dot(one_hot, jnp.concatenate([high, middle, low], axis=1), preferred_element_type=F32)
    return out[:, :width] + out[:, width : 2 * width] + out[:, 2 * width :]


def iota(shape, dim):
    return lax.broadcasted_iota(jnp.int32, shape, dim).astype(F32)


def same(one, other):
    return jnp.where(one == other, 1.0, 0.0).astype(jnp.bfloat16)


def gather_matrix(slot_row, slots):
    return same(iota((slots, LANES), 0), slot_row)


def scatter_matrix(slot_column, slots):
    return same(iota((LANES, slots), 1), slot_column)


def landing_gather(target_columns, frame):
    both = jnp.concatenate([target_columns[:, 2 * frame : 2 * frame + 1], target_columns[:, 2 * frame + 1 : 2 * frame + 2]], axis=0)
    return same(iota((2 * LANES, LANES), 1) + 1.0, both)


def landing_scatter(target_rows, frame):
    both = jnp.concatenate([target_rows[2 * frame : 2 * frame + 1], target_rows[2 * frame + 1 : 2 * frame + 2]], axis=1)
    return same(iota((LANES, 2 * LANES), 0) + 1.0, both)


class Payload:
    def __init__(self, owners, capacity, pieces):
        self.owners, self.capacity, self.pieces = owners, capacity, pieces
        self.fused = capacity % SUBLANES == 0
        self.rows = pieces * capacity
        if self.fused:
            self.shapes = [jax.ShapeDtypeStruct((owners, self.rows + SUBLANES, LANES), F32)]
        else:
            self.shapes = [
                jax.ShapeDtypeStruct((pieces, owners * capacity, LANES), F32),
                jax.ShapeDtypeStruct((owners, SUBLANES, LANES), F32),
            ]
        self.count = len(self.shapes)

    def put(self, refs, piece, values):
        if self.fused:
            first = piece * self.capacity
            refs[0][:, first : first + self.capacity, :] = values.reshape(self.owners, self.capacity, LANES)
        else:
            refs[0][piece] = values

    def get(self, refs, piece):
        if self.fused:
            first = piece * self.capacity
            return refs[0][:, first : first + self.capacity, :].reshape(self.owners * self.capacity, LANES)
        return refs[0][piece]

    def put_spare(self, refs, row, values):
        if self.fused:
            refs[0][:, self.rows + row, :] = values
        else:
            refs[1][:, row, :] = values

    def put_spares(self, refs, tile):
        tile = jnp.broadcast_to(tile[None], (self.owners, SUBLANES, LANES))
        if self.fused:
            refs[0][:, self.rows :, :] = tile
        else:
            refs[1][...] = tile

    def sum_spares(self, refs):
        spares = refs[0][:, self.rows :, :] if self.fused else refs[1][...]
        return jnp.sum(spares, axis=0)

    def exchange(self, arrays):
        if self.fused:
            packed = arrays[0]
        else:
            rows = arrays[0].reshape(self.pieces, self.owners, self.capacity, LANES)
            rows = rows.transpose(1, 0, 2, 3).reshape(self.owners, self.rows, LANES)
            packed = jnp.concatenate([rows, arrays[1]], axis=1)
        packed = lax.all_to_all(packed, AXES, split_axis=0, concat_axis=0, tiled=True)
        if self.fused:
            return [packed]
        rows = packed[:, : self.rows].reshape(self.owners, self.pieces, self.capacity, LANES)
        rows = rows.transpose(1, 0, 2, 3).reshape(self.pieces, self.owners * self.capacity, LANES)
        return [rows, packed[:, self.rows :]]


def call(kernel, inputs, outputs, name):
    def spec(leaf):
        small = leaf.dtype == jnp.int32 and leaf.ndim == 1
        return pl.BlockSpec(memory_space=pltpu.SMEM if small else pltpu.VMEM)

    return pl.pallas_call(
        kernel,
        out_shape=outputs,
        in_specs=[spec(leaf) for leaf in inputs],
        out_specs=[pl.BlockSpec(memory_space=pltpu.VMEM) for _ in outputs],
        compiler_params=pltpu.CompilerParams(vmem_limit_bytes=VMEM_LIMIT),
        name=name,
    )(*inputs)


def right_of(labels, strength):
    return jnp.where(labels == 1, strength, 0.0)


def diagonal_of(labels, strength):
    return DIAGONAL_SHIFT + jnp.where(labels > 0, strength, 0.0)


def tile_rows(rows):
    zero = jnp.zeros((1, LANES), F32)
    return jnp.concatenate(list(rows) + [zero] * (SUBLANES - len(rows)), axis=0)


def row_sum(cells):
    while cells.ndim > 2:
        cells = jnp.sum(cells, axis=0)
    total = cells[:, :LANES]
    for first in range(LANES, cells.shape[1], LANES):
        total = total + cells[:, first : first + LANES]
    return jnp.sum(total, axis=0, keepdims=True)


def frame_edges(shade, first, last, side, place, slice_count):
    slices, lines, width = shade.shape
    line = lax.broadcasted_iota(jnp.int32, shade.shape, 1)
    cell = lax.broadcasted_iota(jnp.int32, shade.shape, 2)
    low = jnp.where(place[0] > 0, edge_weight(shade[0], first), 0.0)
    high = jnp.where(place[0] < slice_count - 1, edge_weight(last, shade[slices - 1]), 0.0)
    along_z = [low] + [edge_weight(shade[z], shade[z - 1]) for z in range(1, slices)] + [high]
    outer = edge_weight(side, shade)
    along_y = edge_weight(pltpu.roll(shade, lines - 1, 1), shade)
    along_y = jnp.where(line == lines - 1, jnp.where(place[1] == 0, outer, 0.0), along_y)
    below = jnp.where(place[1] == 0, 0.0, outer)
    along_x = jnp.where(cell == width - 1, 0.0, edge_weight(pltpu.roll(shade, width - 1, 2), shade))
    return along_z, along_y, below, along_x


def frame_spatial(field, first, last, side, edges):
    along_z, along_y, below, along_x = edges
    slices, lines, width = field.shape
    line = lax.broadcasted_iota(jnp.int32, field.shape, 1)
    layers = [first] + [field[z] for z in range(slices)] + [last]
    flow_z = [along_z[k] * (layers[k + 1] - layers[k]) for k in range(slices + 1)]
    coupled = jnp.stack([flow_z[z] - flow_z[z + 1] for z in range(slices)])
    above = jnp.where(line == lines - 1, side, pltpu.roll(field, lines - 1, 1))
    flow_y = along_y * (above - field)
    coupled = coupled - flow_y + jnp.where(line == 0, below * (field - side), pltpu.roll(flow_y, 1, 1))
    flow_x = along_x * (pltpu.roll(field, width - 1, 2) - field)
    return coupled - flow_x + pltpu.roll(flow_x, 1, 2)


def local_step(mesh):
    slc_count, row_count = mesh.shape["slc"], mesh.shape["row"]
    owners = slc_count * row_count

    def local(intensity, labels, strength, partner):
        frames, slices, lines, width = intensity.shape
        links = frames - 1
        blocks = slices * lines * (width // LANES)
        capacity = 2 * blocks // owners
        slots = owners * capacity
        block_bits, line_bits = blocks.bit_length() - 1, lines.bit_length() - 1
        width_bits = (width // LANES).bit_length() - 1
        field = jax.ShapeDtypeStruct(intensity.shape, F32)
        tile = jax.ShapeDtypeStruct((SUBLANES, LANES), F32)
        by_link = jax.ShapeDtypeStruct((links, blocks, LANES), F32)
        pay1, pay2, pay3 = (Payload(owners, capacity, k * links) for k in (2, 2, 1))
        place = jnp.stack([lax.axis_index("slc"), lax.axis_index("row")]).astype(jnp.int32)
        ids = partner.transpose(0, 1, 3, 2).reshape(links, blocks)

        def face_shapes(count):
            return [
                jax.ShapeDtypeStruct((count, frames, lines, width), F32),
                jax.ShapeDtypeStruct((count, frames, lines, width), F32),
                jax.ShapeDtypeStruct((count, frames, slices, width), F32),
            ]

        def put_faces(refs, k, place, frame, cells):
            refs[0][k, frame] = cells[0]
            refs[1][k, frame] = cells[slices - 1]
            inner = jnp.where(place[1] == 0, cells[:, lines - 1 :], cells[:, :1])
            for z in range(slices):
                refs[2][k, frame, z : z + 1, :] = inner[z]

        def swap_faces(first, last, side):
            below = lax.ppermute(last, "slc", [(i, i + 1) for i in range(slc_count - 1)])
            above = lax.ppermute(first, "slc", [(i + 1, i) for i in range(slc_count - 1)])
            beside = lax.ppermute(side, "row", [(i, i ^ 1) for i in range(row_count)])
            return below, above, beside

        def halos(refs, k, frame):
            return refs[0][k, frame], refs[1][k, frame], refs[2][k, frame][:, None, :]

        def send_kernel(place, shade, labels, strength, ids, *outs):
            pay, (slots_out, *faces) = outs[: pay1.count], outs[pay1.count :]
            me = place[0] * row_count + place[1]
            square = jnp.zeros((1, LANES), F32)
            slot_rows = []
            before = jnp.where(iota((LANES, LANES), 0) < iota((LANES, LANES), 1), 1.0, 0.0).astype(jnp.bfloat16)
            for t in range(frames):
                right = right_of(labels[t], strength[t])
                square = square + row_sum(right * right)
                put_faces(faces, 0, place, t, shade[t])
                put_faces(faces, 1, place, t, right)
                if t == links:
                    continue
                partner_id = ids[t : t + 1]
                owner = (partner_id >> block_bits).astype(F32)
                there = partner_id & (blocks - 1)
                line = (there >> width_bits) & (lines - 1)
                x_block = there & ((1 << width_bits) - 1)
                target = (there >> (width_bits + line_bits) << (width_bits + line_bits)) + (x_block << line_bits) + line
                owned = jnp.where(iota((owners, LANES), 0) == owner, 1.0, 0.0)
                count = jnp.dot(owned.astype(jnp.bfloat16), before, preferred_element_type=F32)
                rank = jnp.sum(owned * count, axis=0, keepdims=True)
                slot = owner * capacity + rank
                slot_rows.append(slot)
                both = jnp.concatenate([to_blocks(shade[t]), to_blocks(right)], axis=1)
                sent = pick(gather_matrix(slot, slots), both)
                pay1.put(pay, t, sent[:, :LANES])
                pay1.put(pay, links + t, sent[:, LANES:])
                here = (me * capacity).astype(F32) + rank
                told = lax.dot_general(
                    (owned * (target.astype(F32) + 1.0)).astype(jnp.bfloat16),
                    gather_matrix(here, slots),
                    (((1,), (1,)), ((), ())),
                    preferred_element_type=F32,
                )
                pay1.put_spare(pay, 2 * t, told[:, :LANES])
                pay1.put_spare(pay, 2 * t + 1, told[:, LANES:])
            pay1.put_spare(pay, 2 * links, jnp.broadcast_to(square, (owners, LANES)))
            for row in range(2 * links + 1, SUBLANES):
                pay1.put_spare(pay, row, jnp.zeros((owners, LANES), F32))
            slots_out[...] = tile_rows(slot_rows)

        *payload, slot_tile, face0, face1, face2 = call(
            send_kernel, [place, intensity, labels, strength, ids], pay1.shapes + [tile] + face_shapes(2), "send_blocks"
        )
        received = pay1.exchange(payload)
        halo = swap_faces(face0, face1, face2)

        def spatial_kernel(place, shade, labels, strength, low, high, side, out):
            for t in range(frames):
                edges = frame_edges(shade[t], *halos((low, high, side), 0, t), place, slc_count)
                right = right_of(labels[t], strength[t])
                out[t] = diagonal_of(labels[t], strength[t]) * right + frame_spatial(
                    right, *halos((low, high, side), 1, t), edges
                )

        (own,) = call(spatial_kernel, [place, intensity, labels, strength, *halo], [field], "spatial_of_right")

        def flux_kernel(shade, labels, strength, own, slot_tile, *refs):
            arrived, refs = refs[: pay1.count], refs[pay1.count :]
            pay, (image, weight, flux, right_in, targets) = refs[: pay2.count], refs[pay2.count :]
            spares = pay1.sum_spares(arrived)
            targets[...] = spares
            columns = spares.T
            power = jnp.zeros((1, LANES), F32)
            for t in range(frames):
                right = to_blocks(right_of(labels[t], strength[t]))
                part = to_blocks(own[t])
                power = power + row_sum(right * part)
                if t > 0:
                    k = t - 1
                    came = jnp.concatenate([pay1.get(arrived, k), pay1.get(arrived, links + k)], axis=1)
                    came = pick(landing_scatter(spares, k), came)
                    weight_t = edge_weight(came[:, :LANES], to_blocks(shade[t]))
                    gap = right - came[:, LANES:]
                    flux_t = weight_t * gap
                    power = power + row_sum(flux_t * gap)
                    part = part + flux_t
                    weight[k], flux[k], right_in[k] = weight_t, flux_t, came[:, LANES:]
                    pay2.put(pay, k, pick(landing_gather(columns, k), flux_t))
                if t < links:
                    pay2.put(pay, links + t, pick(gather_matrix(slot_tile[t : t + 1], slots), part))
                store_cells(image, t, part)
            pay2.put_spares(pay, tile_rows([power]))

        *payload, part, weight, flux, right_in, targets = call(
            flux_kernel,
            [intensity, labels, strength, own, slot_tile, *received],
            pay2.shapes + [field, by_link, by_link, by_link, tile],
            "flux_of_right",
        )
        received = pay2.exchange(payload)

        def residual_kernel(place, labels, strength, part, slot_tile, flux, right_in, weight, targets, *refs):
            arrived, refs = refs[: pay2.count], refs[pay2.count :]
            image, residual, back, scalars, *faces = refs
            power = jnp.sum(pay2.sum_spares(arrived), axis=1, keepdims=True)[:1]
            rows = targets[...]
            square = jnp.sum(rows, axis=1, keepdims=True)[2 * links : 2 * links + 1]
            step = square / power
            columns = slot_tile[...].T
            joined = jnp.zeros((1, LANES), F32)
            for t in range(frames):
                image_t = to_blocks(part[t])
                if t < links:
                    image_t = image_t - pick(scatter_matrix(columns[:, t : t + 1], slots), pay2.get(arrived, t))
                residual_t = to_blocks(right_of(labels[t], strength[t])) - step * image_t
                store_cells(image, t, image_t)
                store_cells(residual, t, residual_t)
                put_faces(faces, 0, place, t, residual[t])
                if t > 0:
                    k = t - 1
                    image_in = pick(landing_scatter(rows, k), pay2.get(arrived, links + k)) - flux[k]
                    gap = residual_t - (right_in[k] - step * image_in)
                    back_t = weight[k] * gap
                    joined = joined + row_sum(back_t * gap)
                    back[k] = back_t
            scalars[...] = tile_rows([jnp.broadcast_to(v, (1, LANES)) for v in (square, power, step)] + [joined])

        image, residual, back, scalars, face0, face1, face2 = call(
            residual_kernel,
            [place, labels, strength, part, slot_tile, flux, right_in, weight, targets, *received],
            [field, field, by_link, tile] + face_shapes(1),
            "first_residual",
        )
        low, high, side = swap_faces(face0, face1, face2)
        low0, high0, side0 = halo

        def second_kernel(
            place, shade, labels, strength, residual, image, back, targets, scalars, low0, high0, side0, low, high, side, *refs
        ):
            pay, (out,) = refs[: pay3.count], refs[pay3.count :]
            columns = targets[...].T
            norm = cross = jnp.zeros((1, LANES), F32)
            power = scalars[3:4]
            for t in range(frames):
                edges = frame_edges(shade[t], *halos((low0, high0, side0), 0, t), place, slc_count)
                residual_t = residual[t]
                part = diagonal_of(labels[t], strength[t]) * residual_t + frame_spatial(
                    residual_t, *halos((low, high, side), 0, t), edges
                )
                norm = norm + row_sum(residual_t * residual_t)
                power = power + row_sum(residual_t * part)
                cross = cross + row_sum(residual_t * image[t])
                part = to_blocks(part)
                if t > 0:
                    k = t - 1
                    part = part + back[k]
                    pay3.put(pay, k, pick(landing_gather(columns, k), back[k]))
                store_cells(out, t, part)
            pay3.put_spares(pay, tile_rows([norm, power, cross]))

        *payload, part = call(
            second_kernel,
            [place, intensity, labels, strength, residual, image, back, targets, scalars, low0, high0, side0, low, high, side],
            pay3.shapes + [field],
            "image_of_residual",
        )
        received = pay3.exchange(payload)

        def final_kernel(labels, strength, residual, image, part, slot_tile, scalars, *refs):
            arrived, (solution_field, out) = refs[: pay3.count], refs[pay3.count :]
            sums = jnp.sum(pay3.sum_spares(arrived), axis=1, keepdims=True)
            square, power, step = scalars[0:1, :1], scalars[1:2, :1], scalars[2:3, :1]
            norm = sums[0:1]
            turn = norm / square
            second = norm / (sums[1:2] + 2.0 * turn * sums[2:3] + turn * turn * power)
            columns = slot_tile[...].T
            for t in range(frames):
                turned = to_blocks(part[t])
                if t < links:
                    turned = turned - pick(scatter_matrix(columns[:, t : t + 1], slots), pay3.get(arrived, t))
                residual_t = to_blocks(residual[t])
                right = to_blocks(right_of(labels[t], strength[t]))
                direction = residual_t + turn * right
                turned = turned + turn * to_blocks(image[t])
                store_cells(solution_field, t, step * right + second * direction)
                store_cells(out, t, residual_t - second * turned)

        return tuple(
            call(
                final_kernel,
                [labels, strength, residual, image, part, slot_tile, scalars, *received],
                [field, field],
                "solution_and_residual",
            )
        )

    return local


def solution(mesh):
    spec = P("grp", "slc", "row", None)
    return jax.shard_map(local_step(mesh), mesh=mesh, in_specs=(spec,) * 4, out_specs=(spec, spec), check_vma=False)
```

time: 244 us -> 97.3 us (0.40)
  blocking collectives: 97.6 us -> 48.5 us
  starting transfers between devices: 62.1 us -> 17.4 us
  waiting for transfers between devices: 42.7 us -> 18 us
  local copies, waits for them, and re-layouts: 18.8 us -> 3.69 us
  other arithmetic: 8.96 us -> 0.08 us
  Pallas kernels: 0 us -> 8.37 us
  matrix products: 7.01 us -> 0 us
  between operations: 5.22 us -> 0.72 us
    psum x3 -> x0, blocking collectives: 97.6 us -> none  [the longest x2 62.2 us: squares(): return lax.psum(jnp.sum(residual * residual), ('slc', 'row'))]
    all_to_all x0 -> x2, blocking collectives: none -> 48.5 us  [exchange(): lax.all_to_all(packed, AXES, split_axis=0, concat_axis=0, tiled=True)]
    all_to_all x7 -> x1, waiting for transfers between devices: 39.3 us -> 5.21 us  [exchange(): lax.all_to_all(packed, AXES, split_axis=0, concat_axis=0, tiled=True)]
    all_to_all x7 -> x1, starting transfers between devices: 33.7 us -> 7.52 us  [exchange(): lax.all_to_all(packed, AXES, split_axis=0, concat_axis=0, tiled=True)]
    ppermute x12 -> x6, starting transfers between devices: 28.5 us -> 9.91 us  [the longest x2 6.74 us: swap_faces(): lax.ppermute(last, 'slc', [(i, i + 1) for i in range(slc_count - 1)])]
    ppermute x12 -> x6, waiting for transfers between devices: 3.42 us -> 12.8 us  [the longest x2 7.55 us: swap_faces(): lax.ppermute(first, 'slc', [(i + 1, i) for i in range(slc_count - 1)])]
    pallas_call x0 -> x6, Pallas kernels: none -> 8.37 us  [call(): pl.pallas_call(kernel, out_shape=outputs, in_specs=[spec(leaf) for leaf i...]
    dot_general x12 -> x0, matrix products: 7.01 us -> none  [the longest x6 4.54 us: place_rows(): jnp.einsum('tsb,tsc->tbc', table, values, precision=lax.Precision.HIGHEST)]
  transfers between devices with their start and end apart: 19 -> 7, of which waited for: 8 -> 6; matrix products, arithmetic and copies ran while one was open for 9% -> 0% of each run, Pallas kernels for 0% -> 1%
where the time goes in v1:
time: 97.3 us; the launch traced here: 96.8 us
  blocking collectives  48.5 us (50%)
  waiting for transfers between devices  18 us (18%)
  starting transfers between devices  17.4 us (18%)
  Pallas kernels  8.37 us (9%)
  local copies, waits for them, and re-layouts  3.69 us (4%)
    all_to_all x2, blocking collectives, exchange(): lax.all_to_all(packed, AXES, split_axis=0, concat_axis=0, tiled=True)  48.5 us
    pallas_call x6, Pallas kernels, call(): pl.pallas_call(kernel, out_shape=outputs, in_specs=[spec(leaf) for leaf i...  8.37 us
    ppermute x2, waiting for transfers between devices, swap_faces(): lax.ppermute(first, 'slc', [(i + 1, i) for i in range(slc_count - 1)])  7.55 us
    all_to_all x1, starting transfers between devices, exchange(): lax.all_to_all(packed, AXES, split_axis=0, concat_axis=0, tiled=True)  7.52 us
    ppermute x2, starting transfers between devices, swap_faces(): lax.ppermute(last, 'slc', [(i, i + 1) for i in range(slc_count - 1)])  6.74 us
    all_to_all x1, waiting for transfers between devices, exchange(): lax.all_to_all(packed, AXES, split_axis=0, concat_axis=0, tiled=True)  5.21 us
    ppermute x2, waiting for transfers between devices, swap_faces(): lax.ppermute(last, 'slc', [(i, i + 1) for i in range(slc_count - 1)])  3.15 us
    unnamed x12, local copies, waits for them, and re-layouts  2.86 us
  transfers between devices with their start and end apart: 7, of which 6 were waited for; matrix products, arithmetic and copies ran while one was open for 0% of the time, Pallas kernels for 1%

profile of v1, /device:TPU:0, one launch (start us, length us, event | category | flops | bytes accessed | tf_op | source)
XLA Modules:
  0.0 96.8 jit_solution(13371253286548674622)
XLA Ops:
  0.6 0.8 reshape.7.ids
  1.5 0.1 pad_add_fusion.place
  1.5 0.0 copy-start
  1.5 0.9 copy-done
  2.5 0.0 copy-start.2
  2.5 0.9 copy-done.2
  3.4 0.0 copy-start.4
  3.4 0.9 copy-done.4
  4.4 2.4 %send_blocks.1 = (f32[16,104,128]{2,1,0:T(8,128)}, f32[8,128]{1,0:T(8,128)S(1)}, f32[2,4,8,512]{3,2,1,0:T(8,128)S(1)}, f32[2,4,8,512]{3,2,1,0:T(8,128)S(1)}, f32[2,4,4,512]{3,2,1,0:T(4,128)S(1)}) custom-call(s32[2]{0:T(128)S(1)} %pad_add_fusion.place, f32[4,4,8,512]{3,2,1,0:T(8,128)S(1)} %copy-done.4, s32[4,4,8,512]{3,2,1,0:T(8,128)S(1)} %copy-done, ...), custom_call_target="tpu_custom_call" | custom-call | tf_op jit(solution)/shard_map/send_blocks/pallas_call | solution.py:139
  6.8 0.0 copy-start.1
  6.8 0.0 copy-start.3
  6.8 0.0 copy-start.5
  6.8 7.5 %all-to-all-start = ((f32[16,104,128]{2,1,0:T(8,128)}), f32[16,104,128]{2,1,0:T(8,128)S(1)}, u32[]{:S(2)}, u32[]{:S(2)}) async-start(f32[16,104,128]{2,1,0:T(8,128)} %get-tuple-element.26), calls=%async_computation | async-start | bytes 1703936 | tf_op jit(solution)/shard_map/all_to_all | solution.py:126
  14.3 3.8 %collective-permute-start = (f32[2,4,8,512]{3,2,1,0:T(8,128)S(1)}, f32[2,4,8,512]{3,2,1,0:T(8,128)S(1)}, u32[]{:S(2)}, u32[]{:S(2)}) collective-permute-start(f32[2,4,8,512]{3,2,1,0:T(8,128)S(1)} %get-tuple-element.22), channel_id=1, source_target_pairs={{0,2},{2,4},{4,6},{6,8},{8,10},{10,12},{12,14},{1,3},{3,5},{5,7},{... | collective-permute-start | bytes 393224 | tf_op jit(solution)/shard_map/ppermute | solution.py:234
  18.1 1.3 %collective-permute-start.1 = (f32[2,4,8,512]{3,2,1,0:T(8,128)S(1)}, f32[2,4,8,512]{3,2,1,0:T(8,128)S(1)}, u32[]{:S(2)}, u32[]{:S(2)}) collective-permute-start(f32[2,4,8,512]{3,2,1,0:T(8,128)S(1)} %get-tuple-element.23), channel_id=1, source_target_pairs={{2,0},{4,2},{6,4},{8,6},{10,8},{12,10},{14,12},{3,1},{5,3},{7,5},{... | collective-permute-start | bytes 393224 | tf_op jit(solution)/shard_map/ppermute | solution.py:235
  19.4 0.1 collective-permute-start.2
  19.5 1.2 %collective-permute-done.2.side.side0 = f32[2,4,4,512]{3,2,1,0:T(4,128)S(1)} collective-permute-done((f32[2,4,4,512]{3,2,1,0:T(4,128)S(1)}, f32[2,4,4,512]{3,2,1,0:T(4,128)S(1)}, u32[]{:S(2)}, u32[]{:S(2)}) %collective-permute-start.2) | collective-permute-done | bytes 65568 | tf_op jit(solution)/shard_map/ppermute | solution.py:236
  20.8 3.1 %collective-permute-done.low.low0 = f32[2,4,8,512]{3,2,1,0:T(8,128)S(1)} collective-permute-done((f32[2,4,8,512]{3,2,1,0:T(8,128)S(1)}, f32[2,4,8,512]{3,2,1,0:T(8,128)S(1)}, u32[]{:S(2)}, u32[]{:S(2)}) %collective-permute-start) | collective-permute-done | bytes 131104 | tf_op jit(solution)/shard_map/ppermute | solution.py:234
  23.9 3.9 %collective-permute-done.1.high.high0 = f32[2,4,8,512]{3,2,1,0:T(8,128)S(1)} collective-permute-done((f32[2,4,8,512]{3,2,1,0:T(8,128)S(1)}, f32[2,4,8,512]{3,2,1,0:T(8,128)S(1)}, u32[]{:S(2)}, u32[]{:S(2)}) %collective-permute-start.1) | collective-permute-done | bytes 131104 | tf_op jit(solution)/shard_map/ppermute | solution.py:235
  27.8 0.0 copy-done.1
  27.8 0.0 copy-done.3
  27.8 0.0 copy-done.5
  27.8 1.1 %spatial_of_right.1.own = f32[4,4,8,512]{3,2,1,0:T(8,128)S(1)} custom-call(s32[2]{0:T(128)S(1)} %pad_add_fusion.place, f32[4,4,8,512]{3,2,1,0:T(8,128)S(1)} %copy-done.5, s32[4,4,8,512]{3,2,1,0:T(8,128)S(1)} %copy-done.1, f32[4,4,8,512]{3,2,1,0:T(8,128)S(1)} %copy-done.3, f32[2,4,8,512]{3,2,1,0:T(8,128)S(1)} %collective-permute-done.low.low0, ...), custom_call_target="tpu_custom_call" | custom-call | tf_op jit(solution)/shard_map/spatial_of_right/pallas_call | solution.py:139
  28.9 5.2 %all-to-all-done.refs_0_ = f32[16,104,128]{2,1,0:T(8,128)S(1)} async-done(((f32[16,104,128]{2,1,0:T(8,128)}), f32[16,104,128]{2,1,0:T(8,128)S(1)}, u32[]{:S(2)}, u32[]{:S(2)}) %all-to-all-start) | async-done | bytes 852000 | tf_op jit(solution)/shard_map/all_to_all | solution.py:126
  34.1 1.3 %flux_of_right.1 = (f32[16,104,128]{2,1,0:T(8,128)S(1)}, f32[4,4,8,512]{3,2,1,0:T(8,128)S(1)}, f32[3,128,128]{2,1,0:T(8,128)S(1)}, f32[3,128,128]{2,1,0:T(8,128)...) custom-call(f32[4,4,8,512]{3,2,1,0:T(8,128)S(1)} %copy-done.5, s32[4,4,8,512]{3,2,1,0:T(8,128)S(1)} %copy-done.1, ...), custom_call_target="tpu_custom_call" | custom-call | tf_op jit(solution)/shard_map/flux_of_right/pallas_call | solution.py:139
  35.4 30.6 %all_to_all.15.refs_0_ = f32[16,104,128]{2,1,0:T(8,128)S(1)} all-to-all(f32[16,104,128]{2,1,0:T(8,128)S(1)} %get-tuple-element.32), channel_id=1, replica_groups=mesh['grp'=2,'slc'=8,'row'=2] {'slc','row'}, dimensions={0} | all-to-all | bytes 1703936 | tf_op jit(solution)/shard_map/all_to_all | solution.py:126
  66.0 1.1 %first_residual.1 = (f32[4,4,8,512]{3,2,1,0:T(8,128)S(1)}, f32[4,4,8,512]{3,2,1,0:T(8,128)S(1)}, f32[3,128,128]{2,1,0:T(8,128)S(1)}, f32[8,128]{1,0:T(8,128)S(1)...) custom-call(s32[2]{0:T(128)S(1)} %pad_add_fusion.place, ...), custom_call_target="tpu_custom_call" | custom-call | tf_op jit(solution)/shard_map/first_residual/pallas_call | solution.py:139
  67.1 2.9 %collective-permute-start.3 = (f32[1,4,8,512]{3,2,1,0:T(8,128)S(1)}, f32[1,4,8,512]{3,2,1,0:T(8,128)S(1)}, u32[]{:S(2)}, u32[]{:S(2)}) collective-permute-start(f32[1,4,8,512]{3,2,1,0:T(8,128)S(1)} %get-tuple-element.37), channel_id=1, source_target_pairs={{0,2},{2,4},{4,6},{6,8},{8,10},{10,12},{12,14},{1,3},{3,5},{5,7},{... | collective-permute-start | bytes 196616 | tf_op jit(solution)/shard_map/ppermute | solution.py:234
  70.0 1.3 %collective-permute-start.4 = (f32[1,4,8,512]{3,2,1,0:T(8,128)S(1)}, f32[1,4,8,512]{3,2,1,0:T(8,128)S(1)}, u32[]{:S(2)}, u32[]{:S(2)}) collective-permute-start(f32[1,4,8,512]{3,2,1,0:T(8,128)S(1)} %get-tuple-element.38), channel_id=1, source_target_pairs={{2,0},{4,2},{6,4},{8,6},{10,8},{12,10},{14,12},{3,1},{5,3},{7,5},{... | collective-permute-start | bytes 196616 | tf_op jit(solution)/shard_map/ppermute | solution.py:235
  71.3 0.5 collective-permute-start.5
  71.8 0.9 collective-permute-done.5.side
  72.7 0.0 collective-permute-done.3.low
  72.7 3.7 %collective-permute-done.4.high = f32[1,4,8,512]{3,2,1,0:T(8,128)S(1)} collective-permute-done((f32[1,4,8,512]{3,2,1,0:T(8,128)S(1)}, f32[1,4,8,512]{3,2,1,0:T(8,128)S(1)}, u32[]{:S(2)}, u32[]{:S(2)}) %collective-permute-start.4) | collective-permute-done | bytes 65568 | tf_op jit(solution)/shard_map/ppermute | solution.py:235
  76.3 1.3 %image_of_residual.1 = (f32[16,56,128]{2,1,0:T(8,128)S(1)}, f32[4,4,8,512]{3,2,1,0:T(8,128)S(1)}) custom-call(s32[2]{0:T(128)S(1)} %pad_add_fusion.place, f32[4,4,8,512]{3,2,1,0:T(8,128)S(1)} %copy-done.5, s32[4,4,8,512]{3,2,1,0:T(8,128)S(1)} %copy-done.1, f32[4,4,8,512]{3,2,1,0:T(8,128)S(1)} %copy-done.3, f32[4,4,8,512]{3,2,1,0:T(8,128)S(1)} %get-tuple-element.33.residual, ...), custom_call_target="tpu_custom_call" | custom-call | tf_op jit(solution)/shard_map/image_of_residual/pallas_call | solution.py:139
  77.7 17.9 %all_to_all.16.refs_0_ = f32[16,56,128]{2,1,0:T(8,128)S(1)} all-to-all(f32[16,56,128]{2,1,0:T(8,128)S(1)} %get-tuple-element.41), channel_id=1, replica_groups=mesh['grp'=2,'slc'=8,'row'=2] {'slc','row'}, dimensions={0} | all-to-all | bytes 917504 | tf_op jit(solution)/shard_map/all_to_all | solution.py:126
  95.6 1.2 %solution_and_residual.1 = (f32[4,4,8,512]{3,2,1,0:T(8,128)}, f32[4,4,8,512]{3,2,1,0:T(8,128)}) custom-call(s32[4,4,8,512]{3,2,1,0:T(8,128)S(1)} %copy-done.1, f32[4,4,8,512]{3,2,1,0:T(8,128)S(1)} %copy-done.3, f32[4,4,8,512]{3,2,1,0:T(8,128)S(1)} %get-tuple-element.33.residual, f32[4,4,8,512]{3,2,1,0:T(8,128)S(1)} %get-tuple-element.34.image, ...), custom_call_target="tpu_custom_call" | custom-call | tf_op jit(solution)/shard_map/solution_and_residual/pallas_call | solution.py:139
Async XLA Ops:
  1.5 1.0 copy-start
  2.5 0.9 copy-start.2
  3.4 0.9 copy-start.4
  6.8 21.0 %copy-start.1 = (s32[4,4,8,512]{3,2,1,0:T(8,128)S(1)}, s32[4,4,8,512]{3,2,1,0:T(8,128)}, u32[]{:S(2)}) copy-start(s32[4,4,8,512]{3,2,1,0:T(8,128)} %labels.11) | copy-start | bytes 786436
  6.8 21.0 %copy-start.3 = (f32[4,4,8,512]{3,2,1,0:T(8,128)S(1)}, f32[4,4,8,512]{3,2,1,0:T(8,128)}, u32[]{:S(2)}) copy-start(f32[4,4,8,512]{3,2,1,0:T(8,128)} %strength.11) | copy-start | bytes 786436
  6.8 21.0 %copy-start.5 = (f32[4,4,8,512]{3,2,1,0:T(8,128)S(1)}, f32[4,4,8,512]{3,2,1,0:T(8,128)}, u32[]{:S(2)}) copy-start(f32[4,4,8,512]{3,2,1,0:T(8,128)} %shade.7) | copy-start | bytes 786436
  6.8 27.3 %all-to-all-start = ((f32[16,104,128]{2,1,0:T(8,128)}), f32[16,104,128]{2,1,0:T(8,128)S(1)}, u32[]{:S(2)}, u32[]{:S(2)}) async-start(f32[16,104,128]{2,1,0:T(8,128)} %get-tuple-element.26), calls=%async_computation | async-start | bytes 1703936 | tf_op jit(solution)/shard_map/all_to_all | solution.py:126
  14.3 9.6 %collective-permute-start = (f32[2,4,8,512]{3,2,1,0:T(8,128)S(1)}, f32[2,4,8,512]{3,2,1,0:T(8,128)S(1)}, u32[]{:S(2)}, u32[]{:S(2)}) collective-permute-start(f32[2,4,8,512]{3,2,1,0:T(8,128)S(1)} %get-tuple-element.22), channel_id=1, source_target_pairs={{0,2},{2,4},{4,6},{6,8},{8,10},{10,12},{12,14},{1,3},{3,5},{5,7},{... | collective-permute-start | bytes 393224 | tf_op jit(solution)/shard_map/ppermute | solution.py:234
  18.1 9.7 %collective-permute-start.1 = (f32[2,4,8,512]{3,2,1,0:T(8,128)S(1)}, f32[2,4,8,512]{3,2,1,0:T(8,128)S(1)}, u32[]{:S(2)}, u32[]{:S(2)}) collective-permute-start(f32[2,4,8,512]{3,2,1,0:T(8,128)S(1)} %get-tuple-element.23), channel_id=1, source_target_pairs={{2,0},{4,2},{6,4},{8,6},{10,8},{12,10},{14,12},{3,1},{5,3},{7,5},{... | collective-permute-start | bytes 393224 | tf_op jit(solution)/shard_map/ppermute | solution.py:235
  19.4 1.3 %collective-permute-start.2 = (f32[2,4,4,512]{3,2,1,0:T(4,128)S(1)}, f32[2,4,4,512]{3,2,1,0:T(4,128)S(1)}, u32[]{:S(2)}, u32[]{:S(2)}) collective-permute-start(f32[2,4,4,512]{3,2,1,0:T(4,128)S(1)} %get-tuple-element.24), channel_id=1, source_target_pairs={{0,1},{1,0},{2,3},{3,2},{4,5},{5,4},{6,7},{7,6},{8,9},{9,8},{10,11... | collective-permute-start | bytes 196616 | tf_op jit(solution)/shard_map/ppermute | solution.py:236
  67.1 5.6 %collective-permute-start.3 = (f32[1,4,8,512]{3,2,1,0:T(8,128)S(1)}, f32[1,4,8,512]{3,2,1,0:T(8,128)S(1)}, u32[]{:S(2)}, u32[]{:S(2)}) collective-permute-start(f32[1,4,8,512]{3,2,1,0:T(8,128)S(1)} %get-tuple-element.37), channel_id=1, source_target_pairs={{0,2},{2,4},{4,6},{6,8},{8,10},{10,12},{12,14},{1,3},{3,5},{5,7},{... | collective-permute-start | bytes 196616 | tf_op jit(solution)/shard_map/ppermute | solution.py:234
  70.0 6.3 %collective-permute-start.4 = (f32[1,4,8,512]{3,2,1,0:T(8,128)S(1)}, f32[1,4,8,512]{3,2,1,0:T(8,128)S(1)}, u32[]{:S(2)}, u32[]{:S(2)}) collective-permute-start(f32[1,4,8,512]{3,2,1,0:T(8,128)S(1)} %get-tuple-element.38), channel_id=1, source_target_pairs={{2,0},{4,2},{6,4},{8,6},{10,8},{12,10},{14,12},{3,1},{5,3},{7,5},{... | collective-permute-start | bytes 196616 | tf_op jit(solution)/shard_map/ppermute | solution.py:235
  71.3 1.4 %collective-permute-start.5 = (f32[1,4,4,512]{3,2,1,0:T(4,128)S(1)}, f32[1,4,4,512]{3,2,1,0:T(4,128)S(1)}, u32[]{:S(2)}, u32[]{:S(2)}) collective-permute-start(f32[1,4,4,512]{3,2,1,0:T(4,128)S(1)} %get-tuple-element.39), channel_id=1, source_target_pairs={{0,1},{1,0},{2,3},{3,2},{4,5},{5,4},{6,7},{7,6},{8,9},{9,8},{10,11... | collective-permute-start | bytes 98312 | tf_op jit(solution)/shard_map/ppermute | solution.py:236

commit v2 on v1

v2 whole, which is shorter than its diff:
```python
import jax
import jax.numpy as jnp
from jax import lax
from jax.experimental import pallas as pl
from jax.experimental.pallas import tpu as pltpu
from jax.sharding import PartitionSpec as P

EDGE_SHARPNESS = 0.5
DIAGONAL_SHIFT = 0.1
LANES = 128
SUBLANES = 8
AXES = ("slc", "row")
F32 = jnp.float32
VMEM_LIMIT = 40 * 1024 * 1024


def edge_weight(upper, lower):
    contrast = upper - lower
    return jnp.exp(-EDGE_SHARPNESS * contrast * contrast)


def to_blocks(cells):
    slices, _, width = cells.shape
    return jnp.concatenate(
        [cells[z, :, x : x + LANES] for z in range(slices) for x in range(0, width, LANES)],
        axis=0,
    )


def store_cells(ref, frame, blocks):
    _, slices, lines, width = ref.shape
    per_slice = width // LANES
    for z in range(slices):
        for x in range(per_slice):
            first = (z * per_slice + x) * lines
            ref[frame, z, :, x * LANES : (x + 1) * LANES] = blocks[first : first + lines]


def pick(one_hot, values):
    high = values.astype(jnp.bfloat16)
    rest = values - high.astype(F32)
    middle = rest.astype(jnp.bfloat16)
    low = (rest - middle.astype(F32)).astype(jnp.bfloat16)
    width = values.shape[1]
    out = jnp.dot(one_hot, jnp.concatenate([high, middle, low], axis=1), preferred_element_type=F32)
    return out[:, :width] + out[:, width : 2 * width] + out[:, 2 * width :]


def iota(shape, dim):
    return lax.broadcasted_iota(jnp.int32, shape, dim).astype(F32)


def same(one, other):
    return jnp.where(one == other, 1.0, 0.0).astype(jnp.bfloat16)


def gather_matrix(slot_row, slots):
    return same(iota((slots, LANES), 0), slot_row)


def scatter_matrix(slot_column, slots):
    return same(iota((LANES, slots), 1), slot_column)


def landing_gather(target_columns, frame):
    both = jnp.concatenate([target_columns[:, 2 * frame : 2 * frame + 1], target_columns[:, 2 * frame + 1 : 2 * frame + 2]], axis=0)
    return same(iota((2 * LANES, LANES), 1) + 1.0, both)


def landing_scatter(target_rows, frame):
    both = jnp.concatenate([target_rows[2 * frame : 2 * frame + 1], target_rows[2 * frame + 1 : 2 * frame + 2]], axis=1)
    return same(iota((LANES, 2 * LANES), 0) + 1.0, both)


class Payload:
    def __init__(self, owners, capacity, pieces):
        self.owners, self.capacity, self.pieces = owners, capacity, pieces
        self.fused = capacity % SUBLANES == 0
        self.rows = pieces * capacity
        if self.fused:
            self.shapes = [jax.ShapeDtypeStruct((owners * (self.rows + 1), LANES), F32)]
        else:
            self.shapes = [
                jax.ShapeDtypeStruct((pieces, owners * capacity, LANES), F32),
                jax.ShapeDtypeStruct((owners, LANES), F32),
            ]
        self.count = len(self.shapes)

    def put(self, refs, piece, values):
        if not self.fused:
            refs[0][piece] = values
            return
        for owner in range(self.owners):
            first = owner * (self.rows + 1) + piece * self.capacity
            refs[0][first : first + self.capacity, :] = values[owner * self.capacity : (owner + 1) * self.capacity]

    def get(self, refs, piece):
        if not self.fused:
            return refs[0][piece]
        first = [owner * (self.rows + 1) + piece * self.capacity for owner in range(self.owners)]
        return jnp.concatenate([refs[0][k : k + self.capacity, :] for k in first], axis=0)

    def put_spare(self, refs, values):
        if not self.fused:
            refs[1][...] = jnp.broadcast_to(values, (self.owners, LANES))
            return
        for owner in range(self.owners):
            at = owner * (self.rows + 1) + self.rows
            refs[0][at : at + 1, :] = values[owner : owner + 1] if values.shape[0] > 1 else values

    def get_spare(self, refs):
        if not self.fused:
            return refs[1][...]
        at = [owner * (self.rows + 1) + self.rows for owner in range(self.owners)]
        return jnp.concatenate([refs[0][k : k + 1, :] for k in at], axis=0)

    def exchange(self, arrays):
        if self.fused:
            packed = arrays[0].reshape(self.owners, self.rows + 1, 1, LANES)
        else:
            rows = arrays[0].reshape(self.pieces, self.owners, self.capacity, LANES)
            rows = rows.transpose(1, 0, 2, 3).reshape(self.owners, self.rows, LANES)
            packed = jnp.concatenate([rows, arrays[1][:, None, :]], axis=1)
        packed = lax.all_to_all(packed, AXES, split_axis=0, concat_axis=0, tiled=True)
        if self.fused:
            return [packed.reshape(self.owners * (self.rows + 1), LANES)]
        rows = packed[:, : self.rows].reshape(self.owners, self.pieces, self.capacity, LANES)
        rows = rows.transpose(1, 0, 2, 3).reshape(self.pieces, self.owners * self.capacity, LANES)
        return [rows, packed[:, self.rows]]


def call(kernel, inputs, outputs, name, far=False, scratch=()):
    def spec(leaf):
        if leaf.dtype == jnp.int32 and leaf.ndim == 1:
            return pl.BlockSpec(memory_space=pltpu.SMEM)
        return pl.BlockSpec(memory_space=pltpu.HBM if far else pltpu.VMEM)

    return pl.pallas_call(
        kernel,
        out_shape=outputs,
        in_specs=[spec(leaf) for leaf in inputs],
        out_specs=[pl.BlockSpec(memory_space=pltpu.VMEM) for _ in outputs],
        scratch_shapes=scratch,
        compiler_params=pltpu.CompilerParams(vmem_limit_bytes=VMEM_LIMIT),
        name=name,
    )(*inputs)


def right_of(labels, strength):
    return jnp.where(labels == 1, strength, 0.0)


def diagonal_of(labels, strength):
    return DIAGONAL_SHIFT + jnp.where(labels > 0, strength, 0.0)


def tile_rows(rows):
    zero = jnp.zeros((1, LANES), F32)
    return jnp.concatenate(list(rows) + [zero] * (SUBLANES - len(rows)), axis=0)


def packed_sums(rows):
    lane = lax.broadcasted_iota(jnp.int32, (1, LANES), 1)
    out = jnp.zeros((1, LANES), F32)
    for k, row in enumerate(rows):
        out = jnp.where(lane == k, jnp.sum(row, axis=1, keepdims=True), out)
    return out


def unpacked_sums(spares, count):
    total = jnp.sum(spares, axis=0, keepdims=True)
    lane = lax.broadcasted_iota(jnp.int32, (1, LANES), 1)
    return [jnp.sum(jnp.where(lane == k, total, 0.0), axis=1, keepdims=True) for k in range(count)]


def row_sum(cells):
    while cells.ndim > 2:
        cells = jnp.sum(cells, axis=0)
    total = cells[:, :LANES]
    for first in range(LANES, cells.shape[1], LANES):
        total = total + cells[:, first : first + LANES]
    return jnp.sum(total, axis=0, keepdims=True)


def frame_edges(shade, first, last, side, place, slice_count):
    slices, lines, width = shade.shape
    line = lax.broadcasted_iota(jnp.int32, shade.shape, 1)
    cell = lax.broadcasted_iota(jnp.int32, shade.shape, 2)
    low = high = below = outer = 0.0
    if place is not None:
        low = jnp.where(place[0] > 0, edge_weight(shade[0], first), 0.0)
        high = jnp.where(place[0] < slice_count - 1, edge_weight(last, shade[slices - 1]), 0.0)
        outer = edge_weight(side, shade)
        below = jnp.where(place[1] == 0, 0.0, outer)
        outer = jnp.where(place[1] == 0, outer, 0.0)
    along_z = [low] + [edge_weight(shade[z], shade[z - 1]) for z in range(1, slices)] + [high]
    along_y = edge_weight(pltpu.roll(shade, lines - 1, 1), shade)
    along_y = jnp.where(line == lines - 1, outer, along_y)
    along_x = jnp.where(cell == width - 1, 0.0, edge_weight(pltpu.roll(shade, width - 1, 2), shade))
    return along_z, along_y, below, along_x


def frame_spatial(field, first, last, side, edges):
    along_z, along_y, below, along_x = edges
    slices, lines, width = field.shape
    line = lax.broadcasted_iota(jnp.int32, field.shape, 1)
    layers = [first] + [field[z] for z in range(slices)] + [last]
    flow_z = [along_z[k] * (layers[k + 1] - layers[k]) for k in range(slices + 1)]
    coupled = jnp.stack([flow_z[z] - flow_z[z + 1] for z in range(slices)])
    above = jnp.where(line == lines - 1, side, pltpu.roll(field, lines - 1, 1))
    flow_y = along_y * (above - field)
    coupled = coupled - flow_y + jnp.where(line == 0, below * (field - side), pltpu.roll(flow_y, 1, 1))
    flow_x = along_x * (pltpu.roll(field, width - 1, 2) - field)
    return coupled - flow_x + pltpu.roll(flow_x, 1, 2)


def local_step(mesh):
    slc_count, row_count = mesh.shape["slc"], mesh.shape["row"]
    owners = slc_count * row_count

    def local(intensity, labels, strength, partner):
        frames, slices, lines, width = intensity.shape
        links = frames - 1
        blocks = slices * lines * (width // LANES)
        capacity = 2 * blocks // owners
        slots = owners * capacity
        block_bits, line_bits = blocks.bit_length() - 1, lines.bit_length() - 1
        capacity_bits = capacity.bit_length() - 1
        width_bits = (width // LANES).bit_length() - 1
        field = jax.ShapeDtypeStruct(intensity.shape, F32)
        tile = jax.ShapeDtypeStruct((SUBLANES, LANES), F32)
        by_link = jax.ShapeDtypeStruct((links, blocks, LANES), F32)
        pay1, pay2, pay3 = (Payload(owners, capacity, k * links) for k in (2, 2, 1))
        place = jnp.stack([lax.axis_index("slc"), lax.axis_index("row")]).astype(jnp.int32)
        def face_shapes(count):
            return [
                jax.ShapeDtypeStruct((count, frames, lines, width), F32),
                jax.ShapeDtypeStruct((count, frames, lines, width), F32),
                jax.ShapeDtypeStruct((count, frames, slices, width), F32),
            ]

        def put_faces(refs, k, place, frame, cells):
            refs[0][k, frame] = cells[0]
            refs[1][k, frame] = cells[slices - 1]
            inner = jnp.where(place[1] == 0, cells[:, lines - 1 :], cells[:, :1])
            for z in range(slices):
                refs[2][k, frame, z : z + 1, :] = inner[z]

        def swap_faces(first, last, side):
            below = lax.ppermute(last, "slc", [(i, i + 1) for i in range(slc_count - 1)])
            above = lax.ppermute(first, "slc", [(i + 1, i) for i in range(slc_count - 1)])
            beside = lax.ppermute(side, "row", [(i, i ^ 1) for i in range(row_count)])
            return below, above, beside

        def halos(refs, k, frame):
            return refs[0][k, frame], refs[1][k, frame], refs[2][k, frame][:, None, :]

        def id_rows(ids):
            per_link = slices * (width // LANES)
            flat = jnp.concatenate([ids[t, z] for t in range(links) for z in range(slices)], axis=0)
            halves = jnp.concatenate([flat >> block_bits, flat & (blocks - 1)], axis=0).astype(F32).astype(jnp.bfloat16)
            line = lax.broadcasted_iota(jnp.int32, (lines, LANES), 0)
            lane = lax.broadcasted_iota(jnp.int32, (lines, LANES), 1)
            spread = jnp.where((lane & (lines - 1)) == line, 1.0, 0.0).astype(jnp.bfloat16)
            wide = jnp.dot(halves, spread, preferred_element_type=F32)
            mine = lax.broadcasted_iota(jnp.int32, (per_link, LANES), 0) == (
                lax.broadcasted_iota(jnp.int32, (per_link, LANES), 1) >> line_bits
            )
            rows = [
                jnp.sum(jnp.where(mine, wide[k * per_link : (k + 1) * per_link], 0.0), axis=0, keepdims=True)
                for k in range(2 * links)
            ]
            return rows[:links], rows[links:]

        def send_kernel(place, *refs):
            sources, refs = refs[:4], refs[4:]
            pay, (slots_out, *faces) = refs[: pay1.count], refs[pay1.count : -5]
            ids, shade, labels, strength, done = refs[-5:]
            copies = [pltpu.make_async_copy(*pair, done.at[k]) for k, pair in enumerate(zip(sources, (ids, shade, labels, strength)))]
            for copy in copies:
                copy.start()
            before = jnp.where(iota((LANES, LANES), 0) < iota((LANES, LANES), 1), 1.0, 0.0).astype(jnp.bfloat16)
            copies[0].wait()
            owner_rows, there_rows = id_rows(ids)
            slot_rows = []
            told = jnp.zeros((owners, LANES), F32)
            for t in range(links):
                owner, there = owner_rows[t], there_rows[t].astype(jnp.int32)
                line = (there >> width_bits) & (lines - 1)
                x_block = there & ((1 << width_bits) - 1)
                target = (there >> (width_bits + line_bits) << (width_bits + line_bits)) + (x_block << line_bits) + line
                owned = jnp.where(iota((owners, LANES), 0) == owner, 1.0, 0.0)
                count = jnp.dot(owned.astype(jnp.bfloat16), before, preferred_element_type=F32)
                rank = jnp.sum(owned * count, axis=0, keepdims=True)
                slot_rows.append(owner * capacity + rank)
                told = told + lax.dot_general(
                    (owned * (target.astype(F32) + 1.0)).astype(jnp.bfloat16),
                    gather_matrix(rank + t * capacity, LANES),
                    (((1,), (1,)), ((), ())),
                    preferred_element_type=F32,
                )
            pay1.put_spare(pay, told)
            slots_out[...] = tile_rows(slot_rows)
            for copy in copies[1:]:
                copy.wait()
            for t in range(frames):
                right = right_of(labels[t], strength[t])
                put_faces(faces, 0, place, t, shade[t])
                put_faces(faces, 1, place, t, right)
                if t < links:
                    both = jnp.concatenate([to_blocks(shade[t]), to_blocks(right)], axis=1)
                    sent = pick(gather_matrix(slot_rows[t], slots), both)
                    pay1.put(pay, t, sent[:, :LANES])
                    pay1.put(pay, links + t, sent[:, LANES:])

        *payload, slot_tile, face0, face1, face2 = call(
            send_kernel,
            [place, partner.transpose(0, 1, 3, 2), intensity, labels, strength],
            pay1.shapes + [tile] + face_shapes(2),
            "send_blocks",
            far=True,
            scratch=[pltpu.VMEM((links, slices, width // LANES, lines), jnp.int32)]
            + [pltpu.VMEM(leaf.shape, leaf.dtype) for leaf in (intensity, labels, strength)]
            + [pltpu.SemaphoreType.DMA((4,))],
        )
        received = pay1.exchange(payload)
        halo = swap_faces(face0, face1, face2)

        def spatial_kernel(place, shade, labels, strength, low, high, side, out):
            for t in range(frames):
                edges = frame_edges(shade[t], *halos((low, high, side), 0, t), place, slc_count)
                right = right_of(labels[t], strength[t])
                out[t] = diagonal_of(labels[t], strength[t]) * right + frame_spatial(
                    right, *halos((low, high, side), 1, t), edges
                )

        (own,) = call(spatial_kernel, [place, intensity, labels, strength, *halo], [field], "spatial_of_right")

        def target_rows(told):
            slot = lax.broadcasted_iota(jnp.int32, (owners, slots), 1)
            source = lax.broadcasted_iota(jnp.int32, (owners, slots), 0)
            spread = jnp.where((slot >> capacity_bits) == source, 1.0, 0.0).astype(jnp.bfloat16)
            wide = jnp.dot(told.T.astype(jnp.bfloat16), spread, preferred_element_type=F32)
            place_in = lax.broadcasted_iota(jnp.int32, (LANES, slots), 1) & (capacity - 1)
            lane = lax.broadcasted_iota(jnp.int32, (LANES, slots), 0)
            rows = []
            for t in range(links):
                row = jnp.sum(jnp.where(lane == place_in + t * capacity, wide, 0.0), axis=0, keepdims=True)
                rows += [row[:, :LANES], row[:, LANES:]]
            return tile_rows(rows)

        def flux_kernel(shade, labels, strength, own, slot_tile, *refs):
            arrived, refs = refs[: pay1.count], refs[pay1.count :]
            pay, (image, weight, flux, right_in, targets) = refs[: pay2.count], refs[pay2.count :]
            spares = target_rows(pay1.get_spare(arrived))
            targets[...] = spares
            columns = spares.T
            square = power = jnp.zeros((1, LANES), F32)
            for t in range(frames):
                right = to_blocks(right_of(labels[t], strength[t]))
                part = to_blocks(own[t])
                square = square + row_sum(right * right)
                power = power + row_sum(right * part)
                if t > 0:
                    k = t - 1
                    came = jnp.concatenate([pay1.get(arrived, k), pay1.get(arrived, links + k)], axis=1)
                    came = pick(landing_scatter(spares, k), came)
                    weight_t = edge_weight(came[:, :LANES], to_blocks(shade[t]))
                    gap = right - came[:, LANES:]
                    flux_t = weight_t * gap
                    power = power + row_sum(flux_t * gap)
                    part = part + flux_t
                    weight[k], flux[k], right_in[k] = weight_t, flux_t, came[:, LANES:]
                    pay2.put(pay, k, pick(landing_gather(columns, k), flux_t))
                if t < links:
                    pay2.put(pay, links + t, pick(gather_matrix(slot_tile[t : t + 1], slots), part))
                store_cells(image, t, part)
            pay2.put_spare(pay, packed_sums([square, power]))

        *payload, part, weight, flux, right_in, targets = call(
            flux_kernel,
            [intensity, labels, strength, own, slot_tile, *received],
            pay2.shapes + [field, by_link, by_link, by_link, tile],
            "flux_of_right",
        )
        received = pay2.exchange(payload)

        def residual_kernel(place, labels, strength, part, slot_tile, *refs):
            arrived, (image, residual, scalars, up, side) = refs[: pay2.count], refs[pay2.count :]
            square, power = unpacked_sums(pay2.get_spare(arrived), 2)
            step = square / power
            scalars[...] = tile_rows([jnp.broadcast_to(v, (1, LANES)) for v in (square, power, step)])
            columns = slot_tile[...].T
            for t in range(frames):
                image_t = to_blocks(part[t])
                if t < links:
                    image_t = image_t - pick(scatter_matrix(columns[:, t : t + 1], slots), pay2.get(arrived, t))
                store_cells(image, t, image_t)
                store_cells(residual, t, to_blocks(right_of(labels[t], strength[t])) - step * image_t)
                up[t] = residual[t, slices - 1]
                for z in range(slices):
                    side[t, z : z + 1, :] = residual[t, z, lines - 1 :, :]

        image, residual, scalars, up, side = call(
            residual_kernel,
            [place, labels, strength, part, slot_tile, *received],
            [
                field,
                field,
                tile,
                jax.ShapeDtypeStruct((frames, lines, width), F32),
                jax.ShapeDtypeStruct((frames, slices, width), F32),
            ],
            "first_residual",
        )
        low = lax.ppermute(up, "slc", [(i, i + 1) for i in range(slc_count - 1)])
        beside = lax.ppermute(side, "row", [(i, i + 1) for i in range(row_count - 1)])

        def inner_kernel(place, shade, labels, strength, residual, image, scalars, flux, right_in, weight, targets, *refs):
            arrived, refs = refs[: pay2.count], refs[pay2.count :]
            pay, (out, sums) = refs[: pay3.count], refs[pay3.count :]
            rows = targets[...]
            columns = rows.T
            step = scalars[2:3, :]
            norm = power = cross = jnp.zeros((1, LANES), F32)
            none = jnp.zeros((lines, width), F32)
            for t in range(frames):
                residual_t = residual[t]
                edges = frame_edges(shade[t], none, none, none[:1], None, slc_count)
                inner = diagonal_of(labels[t], strength[t]) * residual_t + frame_spatial(residual_t, none, none, none[:1], edges)
                norm = norm + row_sum(residual_t * residual_t)
                power = power + row_sum(residual_t * inner)
                cross = cross + row_sum(residual_t * image[t])
                inner = to_blocks(inner)
                if t > 0:
                    k = t - 1
                    image_in = pick(landing_scatter(rows, k), pay2.get(arrived, links + k)) - flux[k]
                    gap = to_blocks(residual_t) - (right_in[k] - step * image_in)
                    back = weight[k] * gap
                    power = power + row_sum(back * gap)
                    inner = inner + back
                    pay3.put(pay, k, pick(landing_gather(columns, k), back))
                store_cells(out, t, inner)
            sums[...] = tile_rows([norm, power, cross])

        *payload, inner, sums = call(
            inner_kernel,
            [place, intensity, labels, strength, residual, image, scalars, flux, right_in, weight, targets, *received],
            pay3.shapes + [field, tile],
            "inner_image_of_residual",
        )
        low0, _, side0 = halo

        def outer_kernel(place, shade, residual, sums, low0, side0, low, beside, *refs):
            pay, (flow_z, flow_y) = refs[pay3.count : 2 * pay3.count], refs[2 * pay3.count :]
            pay[0][...] = refs[0][...]
            norm, power, cross = sums[0:1], sums[1:2], sums[2:3]
            for t in range(frames):
                weight_z = jnp.where(place[0] > 0, edge_weight(shade[t, 0], low0[0, t]), 0.0)
                gap_z = residual[t, 0] - low[t]
                flow = weight_z * gap_z
                flow_z[t] = flow
                power = power + row_sum(flow * gap_z)
                first = [jnp.concatenate([ref[t, z, :1, :] for z in range(slices)], axis=0) for ref in (shade, residual)]
                weight_y = jnp.where(place[1] > 0, edge_weight(first[0], side0[0, t]), 0.0)
                gap_y = first[1] - beside[t]
                flow = weight_y * gap_y
                flow_y[t] = flow
                power = power + row_sum(flow * gap_y)
            pay3.put_spare(pay, packed_sums([norm, power, cross]))

        *payload, flow_z, flow_y = call(
            outer_kernel,
            [place, intensity, residual, sums, low0, side0, low, beside, *payload],
            pay3.shapes
            + [
                jax.ShapeDtypeStruct((frames, lines, width), F32),
                jax.ShapeDtypeStruct((frames, slices, width), F32),
            ],
            "outer_image_of_residual",
        )
        received = pay3.exchange(payload)
        high_z = lax.ppermute(flow_z, "slc", [(i + 1, i) for i in range(slc_count - 1)])
        high_y = lax.ppermute(flow_y, "row", [(i + 1, i) for i in range(row_count - 1)])

        def final_kernel(labels, strength, residual, image, inner, flow_z, flow_y, high_z, high_y, slot_tile, scalars, *refs):
            arrived, (solution_field, out) = refs[: pay3.count], refs[pay3.count :]
            norm, whole, cross = unpacked_sums(pay3.get_spare(arrived), 3)
            square, power, step = scalars[0:1, :1], scalars[1:2, :1], scalars[2:3, :1]
            turn = norm / square
            second = norm / (whole + 2.0 * turn * cross + turn * turn * power)
            columns = slot_tile[...].T
            line = lax.broadcasted_iota(jnp.int32, (lines, width), 0)
            for t in range(frames):
                turned = []
                for z in range(slices):
                    cells = inner[t, z] + jnp.where(line == 0, flow_y[t, z : z + 1, :], 0.0)
                    cells = cells - jnp.where(line == lines - 1, high_y[t, z : z + 1, :], 0.0)
                    if z == 0:
                        cells = cells + flow_z[t]
                    if z == slices - 1:
                        cells = cells - high_z[t]
                    turned.append(cells)
                turned = to_blocks(jnp.stack(turned))
                if t < links:
                    turned = turned - pick(scatter_matrix(columns[:, t : t + 1], slots), pay3.get(arrived, t))
                residual_t = to_blocks(residual[t])
                right = to_blocks(right_of(labels[t], strength[t]))
                direction = residual_t + turn * right
                turned = turned + turn * to_blocks(image[t])
                store_cells(solution_field, t, step * right + second * direction)
                store_cells(out, t, residual_t - second * turned)

        return tuple(
            call(
                final_kernel,
                [labels, strength, residual, image, inner, flow_z, flow_y, high_z, high_y, slot_tile, scalars, *received],
                [field, field],
                "solution_and_residual",
            )
        )

    return local


def solution(mesh):
    spec = P("grp", "slc", "row", None)
    return jax.shard_map(local_step(mesh), mesh=mesh, in_specs=(spec,) * 4, out_specs=(spec, spec), check_vma=False)
```

time: 97.3 us -> 91.4 us (0.939)
  blocking collectives: 48.5 us -> 29.3 us
  starting transfers between devices: 17.4 us -> 24.4 us
  waiting for transfers between devices: 18 us -> 22.3 us
  Pallas kernels: 8.37 us -> 10.4 us
    all_to_all x2 -> x1, blocking collectives: 48.5 us -> 29.3 us  [exchange(): lax.all_to_all(packed, AXES, split_axis=0, concat_axis=0, tiled=True)]
    ppermute x0 -> x4, starting transfers between devices: none -> 7.7 us  [the longest x1 2.83 us: local(): low = lax.ppermute(up, 'slc', [(i, i + 1) for i in range(slc_count - 1)])]
    all_to_all x1 -> x2, waiting for transfers between devices: 5.21 us -> 9.81 us  [exchange(): lax.all_to_all(packed, AXES, split_axis=0, concat_axis=0, tiled=True)]
    ppermute x0 -> x4, waiting for transfers between devices: none -> 4.52 us  [the longest x1 2.71 us: local(): lax.ppermute(flow_z, 'slc', [(i + 1, i) for i in range(slc_count - 1)])]
    ppermute x2 -> x1, waiting for transfers between devices: 7.55 us -> 3.04 us  [swap_faces(): lax.ppermute(first, 'slc', [(i + 1, i) for i in range(slc_count - 1)])]
    all_to_all x1 -> x2, starting transfers between devices: 7.52 us -> 11.5 us  [exchange(): lax.all_to_all(packed, AXES, split_axis=0, concat_axis=0, tiled=True)]
    ppermute x2 -> x1, starting transfers between devices: 6.74 us -> 3.83 us  [swap_faces(): lax.ppermute(last, 'slc', [(i, i + 1) for i in range(slc_count - 1)])]
    pallas_call x6 -> x7, Pallas kernels: 8.37 us -> 10.4 us  [call(): pl.pallas_call(kernel, out_shape=outputs, in_specs=[spec(leaf) for leaf i...]
  transfers between devices with their start and end apart: 7 -> 9, of which waited for: 6 -> 7; matrix products, arithmetic and copies ran while one was open for 0% -> 0% of each run, Pallas kernels for 1% -> 3%
where the time goes in v2:
time: 91.4 us; the launch traced here: 90.8 us
  blocking collectives  29.3 us (32%)
  starting transfers between devices  24.4 us (27%)
  waiting for transfers between devices  22.3 us (24%)
  Pallas kernels  10.4 us (11%)
  local copies, waits for them, and re-layouts  3.6 us (4%)
    all_to_all x1, blocking collectives, exchange(): lax.all_to_all(packed, AXES, split_axis=0, concat_axis=0, tiled=True)  29.3 us
    all_to_all x2, starting transfers between devices, exchange(): lax.all_to_all(packed, AXES, split_axis=0, concat_axis=0, tiled=True)  11.5 us
    pallas_call x7, Pallas kernels, call(): pl.pallas_call(kernel, out_shape=outputs, in_specs=[spec(leaf) for leaf i...  10.4 us
    all_to_all x2, waiting for transfers between devices, exchange(): lax.all_to_all(packed, AXES, split_axis=0, concat_axis=0, tiled=True)  9.81 us
    ppermute x1, starting transfers between devices, swap_faces(): lax.ppermute(last, 'slc', [(i, i + 1) for i in range(slc_count - 1)])  3.83 us
    ppermute x1, waiting for transfers between devices, swap_faces(): lax.ppermute(last, 'slc', [(i, i + 1) for i in range(slc_count - 1)])  3.68 us
    unnamed x14, local copies, waits for them, and re-layouts  3.6 us
    ppermute x1, waiting for transfers between devices, swap_faces(): lax.ppermute(first, 'slc', [(i + 1, i) for i in range(slc_count - 1)])  3.04 us
  transfers between devices with their start and end apart: 9, of which 7 were waited for; matrix products, arithmetic and copies ran while one was open for 0% of the time, Pallas kernels for 3%

profile of v2, /device:TPU:0, one launch (start us, length us, event | category | flops | bytes accessed | tf_op | source)
XLA Modules:
  0.0 90.8 jit_solution(11192595136076102496)
XLA Ops:
  0.6 0.1 pad_add_fusion.place
  0.7 0.0 copy-start
  0.7 0.9 %copy-done = s32[4,4,8,512]{3,2,1,0:T(8,128)S(1)} copy-done((s32[4,4,8,512]{3,2,1,0:T(8,128)S(1)}, s32[4,4,8,512]{3,2,1,0:T(8,128)}, u32[]{:S(2)}) %copy-start) | copy-done | bytes 262168
  1.7 0.0 copy-start.2
  1.7 0.9 %copy-done.2 = f32[4,4,8,512]{3,2,1,0:T(8,128)S(1)} copy-done((f32[4,4,8,512]{3,2,1,0:T(8,128)S(1)}, f32[4,4,8,512]{3,2,1,0:T(8,128)}, u32[]{:S(2)}) %copy-start.2) | copy-done | bytes 262168
  2.6 0.0 copy-start.4
  2.6 0.9 %copy-done.4 = f32[4,4,8,512]{3,2,1,0:T(8,128)S(1)} copy-done((f32[4,4,8,512]{3,2,1,0:T(8,128)S(1)}, f32[4,4,8,512]{3,2,1,0:T(8,128)}, u32[]{:S(2)}) %copy-start.4) | copy-done | bytes 262168
  3.6 0.0 copy-start.6
  3.6 0.7 copy-done.6
  4.3 2.6 %send_blocks.1 = (f32[1552,128]{1,0:T(8,128)}, f32[8,128]{1,0:T(8,128)S(1)}, f32[2,4,8,512]{3,2,1,0:T(8,128)S(1)}, f32[2,4,8,512]{3,2,1,0:T(8,128)S(1)}, f32[2,4,4,512]{3,2,1,0:T(4,128)S(1)}) custom-call(s32[2]{0:T(128)S(1)} %pad_add_fusion.place, s32[3,4,4,8]{3,2,1,0:T(4,128)S(1)} %bitcast.14, f32[4,4,8,512]{3,2,1,0:T(8,128)S(1)} %copy-done.4, ...), custom_call_target="tpu_custom_call" | custom-call | tf_op jit(solution)/shard_map/send_blocks/pallas_call | solution.py:138
  6.9 0.0 copy-start.1
  6.9 0.0 copy-start.3
  6.9 0.0 copy-start.5
  6.9 7.5 %all-to-all-start = ((f32[16,97,1,128]{3,2,1,0:T(1,128)}), f32[16,97,1,128]{3,2,1,0:T(1,128)S(1)}, u32[]{:S(2)}, u32[]{:S(2)}) async-start(f32[16,97,1,128]{3,2,1,0:T(1,128)} %bitcast.3), calls=%async_computation | async-start | bytes 1589248 | tf_op jit(solution)/shard_map/all_to_all | solution.py:124
  14.5 3.8 %collective-permute-start = (f32[2,4,8,512]{3,2,1,0:T(8,128)S(1)}, f32[2,4,8,512]{3,2,1,0:T(8,128)S(1)}, u32[]{:S(2)}, u32[]{:S(2)}) collective-permute-start(f32[2,4,8,512]{3,2,1,0:T(8,128)S(1)} %get-tuple-element.24), channel_id=1, source_target_pairs={{0,2},{2,4},{4,6},{6,8},{8,10},{10,12},{12,14},{1,3},{3,5},{5,7},{... | collective-permute-start | bytes 393224 | tf_op jit(solution)/shard_map/ppermute | solution.py:250
  18.3 1.3 %collective-permute-start.1 = (f32[2,4,8,512]{3,2,1,0:T(8,128)S(1)}, f32[2,4,8,512]{3,2,1,0:T(8,128)S(1)}, u32[]{:S(2)}, u32[]{:S(2)}) collective-permute-start(f32[2,4,8,512]{3,2,1,0:T(8,128)S(1)} %get-tuple-element.25), channel_id=1, source_target_pairs={{2,0},{4,2},{6,4},{8,6},{10,8},{12,10},{14,12},{3,1},{5,3},{7,5},{... | collective-permute-start | bytes 393224 | tf_op jit(solution)/shard_map/ppermute | solution.py:251
  19.6 0.1 collective-permute-start.2
  19.7 1.2 %collective-permute-done.2.side.side0 = f32[2,4,4,512]{3,2,1,0:T(4,128)S(1)} collective-permute-done((f32[2,4,4,512]{3,2,1,0:T(4,128)S(1)}, f32[2,4,4,512]{3,2,1,0:T(4,128)S(1)}, u32[]{:S(2)}, u32[]{:S(2)}) %collective-permute-start.2) | collective-permute-done | bytes 65568 | tf_op jit(solution)/shard_map/ppermute | solution.py:252
  20.9 3.7 %collective-permute-done.low.low0 = f32[2,4,8,512]{3,2,1,0:T(8,128)S(1)} collective-permute-done((f32[2,4,8,512]{3,2,1,0:T(8,128)S(1)}, f32[2,4,8,512]{3,2,1,0:T(8,128)S(1)}, u32[]{:S(2)}, u32[]{:S(2)}) %collective-permute-start) | collective-permute-done | bytes 131104 | tf_op jit(solution)/shard_map/ppermute | solution.py:250
  24.6 3.0 %collective-permute-done.1.high = f32[2,4,8,512]{3,2,1,0:T(8,128)S(1)} collective-permute-done((f32[2,4,8,512]{3,2,1,0:T(8,128)S(1)}, f32[2,4,8,512]{3,2,1,0:T(8,128)S(1)}, u32[]{:S(2)}, u32[]{:S(2)}) %collective-permute-start.1) | collective-permute-done | bytes 131104 | tf_op jit(solution)/shard_map/ppermute | solution.py:251
  27.7 0.0 copy-done.1
  27.7 0.0 copy-done.3
  27.7 0.0 copy-done.5
  27.7 1.1 %spatial_of_right.1.own = f32[4,4,8,512]{3,2,1,0:T(8,128)S(1)} custom-call(s32[2]{0:T(128)S(1)} %pad_add_fusion.place, f32[4,4,8,512]{3,2,1,0:T(8,128)S(1)} %copy-done.5, s32[4,4,8,512]{3,2,1,0:T(8,128)S(1)} %copy-done.1, f32[4,4,8,512]{3,2,1,0:T(8,128)S(1)} %copy-done.3, f32[2,4,8,512]{3,2,1,0:T(8,128)S(1)} %collective-permute-done.low.low0, ...), custom_call_target="tpu_custom_call" | custom-call | tf_op jit(solution)/shard_map/spatial_of_right/pallas_call | solution.py:138
  28.7 4.6 %all-to-all-done = f32[16,97,1,128]{3,2,1,0:T(1,128)S(1)} async-done(((f32[16,97,1,128]{3,2,1,0:T(1,128)}), f32[16,97,1,128]{3,2,1,0:T(1,128)S(1)}, u32[]{:S(2)}, u32[]{:S(2)}) %all-to-all-start) | async-done | bytes 794656 | tf_op jit(solution)/shard_map/all_to_all | solution.py:124
  33.3 1.5 %flux_of_right.1 = (f32[1552,128]{1,0:T(8,128)S(1)}, f32[4,4,8,512]{3,2,1,0:T(8,128)S(1)}, f32[3,128,128]{2,1,0:T(8,128)S(1)}, f32[3,128,128]{2,1,0:T(8,128)S(1)...) custom-call(f32[4,4,8,512]{3,2,1,0:T(8,128)S(1)} %copy-done.5, s32[4,4,8,512]{3,2,1,0:T(8,128)S(1)} %copy-done.1, ...), custom_call_target="tpu_custom_call" | custom-call | tf_op jit(solution)/shard_map/flux_of_right/pallas_call | solution.py:138
  34.8 29.3 %all_to_all.15 = f32[16,97,1,128]{3,2,1,0:T(1,128)S(1)} all-to-all(f32[16,97,1,128]{3,2,1,0:T(1,128)S(1)} %bitcast.13), channel_id=1, replica_groups=mesh['grp'=2,'slc'=8,'row'=2] {'slc','row'}, dimensions={0} | all-to-all | bytes 1589248 | tf_op jit(solution)/shard_map/all_to_all | solution.py:124
  64.1 1.0 %first_residual.1 = (f32[4,4,8,512]{3,2,1,0:T(8,128)S(1)}, f32[4,4,8,512]{3,2,1,0:T(8,128)S(1)}, f32[8,128]{1,0:T(8,128)S(1)}, f32[4,8,512]{2,1,0:T(8,128)S(1)}, f32[4,4,512]{2,1,0:T(4,128)S(1)}) custom-call(s32[2]{0:T(128)S(1)} %pad_add_fusion.place, s32[4,4,8,512]{3,2,1,0:T(8,128)S(1)} %copy-done.1, f32[4,4,8,512]{3,2,1,0:T(8,128)S(1)} %copy-done.3, ...), custom_call_target="tpu_custom_call" | custom-call | tf_op jit(solution)/shard_map/first_residual/pallas_call | solution.py:138
  65.1 2.8 %collective-permute-start.3 = (f32[4,8,512]{2,1,0:T(8,128)S(1)}, f32[4,8,512]{2,1,0:T(8,128)S(1)}, u32[]{:S(2)}, u32[]{:S(2)}) collective-permute-start(f32[4,8,512]{2,1,0:T(8,128)S(1)} %get-tuple-element.40), channel_id=1, source_target_pairs={{0,2},{2,4},{4,6},{6,8},{8,10},{10,12},{12,14},{1,3},{3,5},{5,7},{... | collective-permute-start | bytes 196616 | tf_op jit(solution)/shard_map/ppermute | solution.py:416
  67.9 2.3 %collective-permute-start.4 = (f32[4,4,512]{2,1,0:T(4,128)S(1)}, f32[4,4,512]{2,1,0:T(4,128)S(1)}, u32[]{:S(2)}, u32[]{:S(2)}) collective-permute-start(f32[4,4,512]{2,1,0:T(4,128)S(1)} %get-tuple-element.41), channel_id=1, source_target_pairs={{0,1},{2,3},{4,5},{6,7},{8,9},{10,11},{12,13},{14,15},{16,17},{18,... | collective-permute-start | bytes 98312 | tf_op jit(solution)/shard_map/ppermute | solution.py:417
  70.2 1.5 %inner_image_of_residual.1 = (f32[784,128]{1,0:T(8,128)S(1)}, f32[4,4,8,512]{3,2,1,0:T(8,128)S(1)}, f32[8,128]{1,0:T(8,128)S(1)}) custom-call(s32[2]{0:T(128)S(1)} %pad_add_fusion.place, f32[4,4,8,512]{3,2,1,0:T(8,128)S(1)} %copy-done.5, s32[4,4,8,512]{3,2,1,0:T(8,128)S(1)} %copy-done.1, f32[4,4,8,512]{3,2,1,0:T(8,128)S(1)} %copy-done.3, ...), custom_call_target="tpu_custom_call" | custom-call | tf_op jit(solution)/shard_map/inner_image_of_residual/pallas_call | solution.py:138
  71.7 0.0 collective-permute-done.4.beside
  71.7 0.0 collective-permute-done.3.low
  71.8 1.5 %outer_image_of_residual.1 = (f32[784,128]{1,0:T(8,128)}, f32[4,8,512]{2,1,0:T(8,128)S(1)}, f32[4,4,512]{2,1,0:T(4,128)S(1)}) custom-call(s32[2]{0:T(128)S(1)} %pad_add_fusion.place, f32[4,4,8,512]{3,2,1,0:T(8,128)S(1)} %copy-done.5, f32[4,4,8,512]{3,2,1,0:T(8,128)S(1)} %get-tuple-element.31.residual, f32[8,128]{1,0:T(8,128)S(1)} %get-tuple-element.39.sums, ...), custom_call_target="tpu_custom_call" | custom-call | tf_op jit(solution)/shard_map/outer_image_of_residual/pallas_call | solution.py:138
  73.2 4.0 %all-to-all-start.2 = ((f32[16,49,1,128]{3,2,1,0:T(1,128)}), f32[16,49,1,128]{3,2,1,0:T(1,128)S(1)}, u32[]{:S(2)}, u32[]{:S(2)}) async-start(f32[16,49,1,128]{3,2,1,0:T(1,128)} %bitcast.7), calls=%async_computation.2 | async-start | bytes 802816 | tf_op jit(solution)/shard_map/all_to_all | solution.py:124
  77.2 1.3 %collective-permute-start.5 = (f32[4,8,512]{2,1,0:T(8,128)S(1)}, f32[4,8,512]{2,1,0:T(8,128)S(1)}, u32[]{:S(2)}, u32[]{:S(2)}) collective-permute-start(f32[4,8,512]{2,1,0:T(8,128)S(1)} %get-tuple-element.43.flow_z), channel_id=1, source_target_pairs={{2,0},{4,2},{6,4},{8,6},{10,8},{12,10},{14,12},{3,1},{5,3},{7,5},{... | collective-permute-start | bytes 196616 | tf_op jit(solution)/shard_map/ppermute | solution.py:483
  78.5 1.3 %collective-permute-start.6 = (f32[4,4,512]{2,1,0:T(4,128)S(1)}, f32[4,4,512]{2,1,0:T(4,128)S(1)}, u32[]{:S(2)}, u32[]{:S(2)}) collective-permute-start(f32[4,4,512]{2,1,0:T(4,128)S(1)} %get-tuple-element.44.flow_y), channel_id=1, source_target_pairs={{1,0},{3,2},{5,4},{7,6},{9,8},{11,10},{13,12},{15,14},{17,16},{19,... | collective-permute-start | bytes 98312 | tf_op jit(solution)/shard_map/ppermute | solution.py:484
  79.8 1.8 %collective-permute-done.6.high_y = f32[4,4,512]{2,1,0:T(4,128)S(1)} collective-permute-done((f32[4,4,512]{2,1,0:T(4,128)S(1)}, f32[4,4,512]{2,1,0:T(4,128)S(1)}, u32[]{:S(2)}, u32[]{:S(2)}) %collective-permute-start.6) | collective-permute-done | bytes 32800 | tf_op jit(solution)/shard_map/ppermute | solution.py:484
  81.6 2.7 %collective-permute-done.5.high_z = f32[4,8,512]{2,1,0:T(8,128)S(1)} collective-permute-done((f32[4,8,512]{2,1,0:T(8,128)S(1)}, f32[4,8,512]{2,1,0:T(8,128)S(1)}, u32[]{:S(2)}, u32[]{:S(2)}) %collective-permute-start.5) | collective-permute-done | bytes 65568 | tf_op jit(solution)/shard_map/ppermute | solution.py:483
  84.3 5.2 %all-to-all-done.2 = f32[16,49,1,128]{3,2,1,0:T(1,128)S(1)} async-done(((f32[16,49,1,128]{3,2,1,0:T(1,128)}), f32[16,49,1,128]{3,2,1,0:T(1,128)S(1)}, u32[]{:S(2)}, u32[]{:S(2)}) %all-to-all-start.2) | async-done | bytes 401440 | tf_op jit(solution)/shard_map/all_to_all | solution.py:124
  89.5 1.2 %solution_and_residual.1 = (f32[4,4,8,512]{3,2,1,0:T(8,128)}, f32[4,4,8,512]{3,2,1,0:T(8,128)}) custom-call(s32[4,4,8,512]{3,2,1,0:T(8,128)S(1)} %copy-done.1, f32[4,4,8,512]{3,2,1,0:T(8,128)S(1)} %copy-done.3, f32[4,4,8,512]{3,2,1,0:T(8,128)S(1)} %get-tuple-element.31.residual, f32[4,4,8,512]{3,2,1,0:T(8,128)S(1)} %get-tuple-element.32.image, ...), custom_call_target="tpu_custom_call" | custom-call | tf_op jit(solution)/shard_map/solution_and_residual/pallas_call | solution.py:138
Async XLA Ops:
  0.7 1.0 %copy-start = (s32[4,4,8,512]{3,2,1,0:T(8,128)S(1)}, s32[4,4,8,512]{3,2,1,0:T(8,128)}, u32[]{:S(2)}) copy-start(s32[4,4,8,512]{3,2,1,0:T(8,128)} %labels.9) | copy-start | bytes 786436
  1.7 0.9 %copy-start.2 = (f32[4,4,8,512]{3,2,1,0:T(8,128)S(1)}, f32[4,4,8,512]{3,2,1,0:T(8,128)}, u32[]{:S(2)}) copy-start(f32[4,4,8,512]{3,2,1,0:T(8,128)} %strength.9) | copy-start | bytes 786436
  2.6 0.9 %copy-start.4 = (f32[4,4,8,512]{3,2,1,0:T(8,128)S(1)}, f32[4,4,8,512]{3,2,1,0:T(8,128)}, u32[]{:S(2)}) copy-start(f32[4,4,8,512]{3,2,1,0:T(8,128)} %shade.7) | copy-start | bytes 786436
  3.6 0.7 copy-start.6
  6.9 20.8 %copy-start.1 = (s32[4,4,8,512]{3,2,1,0:T(8,128)S(1)}, s32[4,4,8,512]{3,2,1,0:T(8,128)}, u32[]{:S(2)}) copy-start(s32[4,4,8,512]{3,2,1,0:T(8,128)} %labels.9) | copy-start | bytes 786436
  6.9 20.7 %copy-start.3 = (f32[4,4,8,512]{3,2,1,0:T(8,128)S(1)}, f32[4,4,8,512]{3,2,1,0:T(8,128)}, u32[]{:S(2)}) copy-start(f32[4,4,8,512]{3,2,1,0:T(8,128)} %strength.9) | copy-start | bytes 786436
  6.9 20.7 %copy-start.5 = (f32[4,4,8,512]{3,2,1,0:T(8,128)S(1)}, f32[4,4,8,512]{3,2,1,0:T(8,128)}, u32[]{:S(2)}) copy-start(f32[4,4,8,512]{3,2,1,0:T(8,128)} %shade.7) | copy-start | bytes 786436
  6.9 26.4 %all-to-all-start = ((f32[16,97,1,128]{3,2,1,0:T(1,128)}), f32[16,97,1,128]{3,2,1,0:T(1,128)S(1)}, u32[]{:S(2)}, u32[]{:S(2)}) async-start(f32[16,97,1,128]{3,2,1,0:T(1,128)} %bitcast.3), calls=%async_computation | async-start | bytes 1589248 | tf_op jit(solution)/shard_map/all_to_all | solution.py:124
  14.5 10.1 %collective-permute-start = (f32[2,4,8,512]{3,2,1,0:T(8,128)S(1)}, f32[2,4,8,512]{3,2,1,0:T(8,128)S(1)}, u32[]{:S(2)}, u32[]{:S(2)}) collective-permute-start(f32[2,4,8,512]{3,2,1,0:T(8,128)S(1)} %get-tuple-element.24), channel_id=1, source_target_pairs={{0,2},{2,4},{4,6},{6,8},{8,10},{10,12},{12,14},{1,3},{3,5},{5,7},{... | collective-permute-start | bytes 393224 | tf_op jit(solution)/shard_map/ppermute | solution.py:250
  18.3 9.3 %collective-permute-start.1 = (f32[2,4,8,512]{3,2,1,0:T(8,128)S(1)}, f32[2,4,8,512]{3,2,1,0:T(8,128)S(1)}, u32[]{:S(2)}, u32[]{:S(2)}) collective-permute-start(f32[2,4,8,512]{3,2,1,0:T(8,128)S(1)} %get-tuple-element.25), channel_id=1, source_target_pairs={{2,0},{4,2},{6,4},{8,6},{10,8},{12,10},{14,12},{3,1},{5,3},{7,5},{... | collective-permute-start | bytes 393224 | tf_op jit(solution)/shard_map/ppermute | solution.py:251
  19.6 1.3 %collective-permute-start.2 = (f32[2,4,4,512]{3,2,1,0:T(4,128)S(1)}, f32[2,4,4,512]{3,2,1,0:T(4,128)S(1)}, u32[]{:S(2)}, u32[]{:S(2)}) collective-permute-start(f32[2,4,4,512]{3,2,1,0:T(4,128)S(1)} %get-tuple-element.26), channel_id=1, source_target_pairs={{0,1},{1,0},{2,3},{3,2},{4,5},{5,4},{6,7},{7,6},{8,9},{9,8},{10,11... | collective-permute-start | bytes 196616 | tf_op jit(solution)/shard_map/ppermute | solution.py:252
  65.1 6.7 %collective-permute-start.3 = (f32[4,8,512]{2,1,0:T(8,128)S(1)}, f32[4,8,512]{2,1,0:T(8,128)S(1)}, u32[]{:S(2)}, u32[]{:S(2)}) collective-permute-start(f32[4,8,512]{2,1,0:T(8,128)S(1)} %get-tuple-element.40), channel_id=1, source_target_pairs={{0,2},{2,4},{4,6},{6,8},{8,10},{10,12},{12,14},{1,3},{3,5},{5,7},{... | collective-permute-start | bytes 196616 | tf_op jit(solution)/shard_map/ppermute | solution.py:416
  67.9 3.8 %collective-permute-start.4 = (f32[4,4,512]{2,1,0:T(4,128)S(1)}, f32[4,4,512]{2,1,0:T(4,128)S(1)}, u32[]{:S(2)}, u32[]{:S(2)}) collective-permute-start(f32[4,4,512]{2,1,0:T(4,128)S(1)} %get-tuple-element.41), channel_id=1, source_target_pairs={{0,1},{2,3},{4,5},{6,7},{8,9},{10,11},{12,13},{14,15},{16,17},{18,... | collective-permute-start | bytes 98312 | tf_op jit(solution)/shard_map/ppermute | solution.py:417
  73.2 16.3 %all-to-all-start.2 = ((f32[16,49,1,128]{3,2,1,0:T(1,128)}), f32[16,49,1,128]{3,2,1,0:T(1,128)S(1)}, u32[]{:S(2)}, u32[]{:S(2)}) async-start(f32[16,49,1,128]{3,2,1,0:T(1,128)} %bitcast.7), calls=%async_computation.2 | async-start | bytes 802816 | tf_op jit(solution)/shard_map/all_to_all | solution.py:124
  77.2 7.1 %collective-permute-start.5 = (f32[4,8,512]{2,1,0:T(8,128)S(1)}, f32[4,8,512]{2,1,0:T(8,128)S(1)}, u32[]{:S(2)}, u32[]{:S(2)}) collective-permute-start(f32[4,8,512]{2,1,0:T(8,128)S(1)} %get-tuple-element.43.flow_z), channel_id=1, source_target_pairs={{2,0},{4,2},{6,4},{8,6},{10,8},{12,10},{14,12},{3,1},{5,3},{7,5},{... | collective-permute-start | bytes 196616 | tf_op jit(solution)/shard_map/ppermute | solution.py:483
  78.5 3.1 %collective-permute-start.6 = (f32[4,4,512]{2,1,0:T(4,128)S(1)}, f32[4,4,512]{2,1,0:T(4,128)S(1)}, u32[]{:S(2)}, u32[]{:S(2)}) collective-permute-start(f32[4,4,512]{2,1,0:T(4,128)S(1)} %get-tuple-element.44.flow_y), channel_id=1, source_target_pairs={{1,0},{3,2},{5,4},{7,6},{9,8},{11,10},{13,12},{15,14},{17,16},{19,... | collective-permute-start | bytes 98312 | tf_op jit(solution)/shard_map/ppermute | solution.py:484

commit v3 on v2

--- a/solution.py
+++ b/solution.py
@@ -12,6 +12,7 @@
 AXES = ("slc", "row")
 F32 = jnp.float32
 VMEM_LIMIT = 40 * 1024 * 1024
+VMEM_WHOLE = 54 * 1024 * 1024 + 512 * 1024
 
 
 def edge_weight(upper, lower):
@@ -131,8 +132,6 @@
 
 def call(kernel, inputs, outputs, name, far=False, scratch=()):
     def spec(leaf):
-        if leaf.dtype == jnp.int32 and leaf.ndim == 1:
-            return pl.BlockSpec(memory_space=pltpu.SMEM)
         return pl.BlockSpec(memory_space=pltpu.HBM if far else pltpu.VMEM)
 
     return pl.pallas_call(
@@ -141,7 +140,7 @@
         in_specs=[spec(leaf) for leaf in inputs],
         out_specs=[pl.BlockSpec(memory_space=pltpu.VMEM) for _ in outputs],
         scratch_shapes=scratch,
-        compiler_params=pltpu.CompilerParams(vmem_limit_bytes=VMEM_LIMIT),
+        compiler_params=pltpu.CompilerParams(vmem_limit_bytes=VMEM_WHOLE if far else VMEM_LIMIT),
         name=name,
     )(*inputs)
 
@@ -229,22 +228,19 @@
         width_bits = (width // LANES).bit_length() - 1
         field = jax.ShapeDtypeStruct(intensity.shape, F32)
         tile = jax.ShapeDtypeStruct((SUBLANES, LANES), F32)
+        face_z = jax.ShapeDtypeStruct((frames, lines, width), F32)
+        face_y = jax.ShapeDtypeStruct((frames, slices, width), F32)
         by_link = jax.ShapeDtypeStruct((links, blocks, LANES), F32)
         pay1, pay2, pay3 = (Payload(owners, capacity, k * links) for k in (2, 2, 1))
-        place = jnp.stack([lax.axis_index("slc"), lax.axis_index("row")]).astype(jnp.int32)
-        def face_shapes(count):
-            return [
-                jax.ShapeDtypeStruct((count, frames, lines, width), F32),
-                jax.ShapeDtypeStruct((count, frames, lines, width), F32),
-                jax.ShapeDtypeStruct((count, frames, slices, width), F32),
-            ]
-
-        def put_faces(refs, k, place, frame, cells):
-            refs[0][k, frame] = cells[0]
-            refs[1][k, frame] = cells[slices - 1]
+
+        def whereabouts():
+            return lax.axis_index("slc"), lax.axis_index("row")
+        def put_faces(refs, place, frame, cells):
+            refs[0][frame] = cells[0]
+            refs[1][frame] = cells[slices - 1]
             inner = jnp.where(place[1] == 0, cells[:, lines - 1 :], cells[:, :1])
             for z in range(slices):
-                refs[2][k, frame, z : z + 1, :] = inner[z]
+                refs[2][frame, z : z + 1, :] = inner[z]
 
         def swap_faces(first, last, side):
             below = lax.ppermute(last, "slc", [(i, i + 1) for i in range(slc_count - 1)])
@@ -252,8 +248,8 @@
             beside = lax.ppermute(side, "row", [(i, i ^ 1) for i in range(row_count)])
             return below, above, beside
 
-        def halos(refs, k, frame):
-            return refs[0][k, frame], refs[1][k, frame], refs[2][k, frame][:, None, :]
+        def halos(refs, frame):
+            return refs[0][frame], refs[1][frame], refs[2][frame][:, None, :]
 
         def id_rows(ids):
             per_link = slices * (width // LANES)
@@ -272,7 +268,8 @@
             ]
             return rows[:links], rows[links:]
 
-        def send_kernel(place, *refs):
+        def send_kernel(*refs):
+            place = whereabouts()
             sources, refs = refs[:4], refs[4:]
             pay, (slots_out, *faces) = refs[: pay1.count], refs[pay1.count : -5]
             ids, shade, labels, strength, done = refs[-5:]
@@ -305,36 +302,48 @@
                 copy.wait()
             for t in range(frames):
                 right = right_of(labels[t], strength[t])
-                put_faces(faces, 0, place, t, shade[t])
-                put_faces(faces, 1, place, t, right)
+                put_faces(faces[:3], place, t, shade[t])
+                put_faces(faces[3:], place, t, right)
                 if t < links:
-                    both = jnp.concatenate([to_blocks(shade[t]), to_blocks(right)], axis=1)
-                    sent = pick(gather_matrix(slot_rows[t], slots), both)
+                    sent = pick(gather_matrix(slot_rows[t], slots), jnp.concatenate([to_blocks(shade[t]), to_blocks(right)], axis=1))
                     pay1.put(pay, t, sent[:, :LANES])
                     pay1.put(pay, links + t, sent[:, LANES:])
 
-        *payload, slot_tile, face0, face1, face2 = call(
+        *payload, slot_tile, shade_first, shade_last, shade_side, right_first, right_last, right_side = call(
             send_kernel,
-            [place, partner.transpose(0, 1, 3, 2), intensity, labels, strength],
-            pay1.shapes + [tile] + face_shapes(2),
+            [partner.transpose(0, 1, 3, 2), intensity, labels, strength],
+            pay1.shapes + [tile] + [face_z, face_z, face_y] * 2,
             "send_blocks",
             far=True,
             scratch=[pltpu.VMEM((links, slices, width // LANES, lines), jnp.int32)]
             + [pltpu.VMEM(leaf.shape, leaf.dtype) for leaf in (intensity, labels, strength)]
             + [pltpu.SemaphoreType.DMA((4,))],
         )
+        shade_halo = swap_faces(shade_first, shade_last, shade_side)
+        right_halo = swap_faces(right_first, right_last, right_side)
         received = pay1.exchange(payload)
-        halo = swap_faces(face0, face1, face2)
-
-        def spatial_kernel(place, shade, labels, strength, low, high, side, out):
-            for t in range(frames):
-                edges = frame_edges(shade[t], *halos((low, high, side), 0, t), place, slc_count)
+
+        def spatial_kernel(shade, labels, strength, face, *refs):
+            shade_outer, right_outer, (out, sums, outer_z, outer_y) = refs[:3], refs[3:6], refs[6:]
+            place = whereabouts()
+            square = power = jnp.zeros((1, LANES), F32)
+            for t in range(frames):
+                edges = frame_edges(shade[t], *halos(shade_outer, t), place, slc_count)
                 right = right_of(labels[t], strength[t])
-                out[t] = diagonal_of(labels[t], strength[t]) * right + frame_spatial(
-                    right, *halos((low, high, side), 1, t), edges
-                )
-
-        (own,) = call(spatial_kernel, [place, intensity, labels, strength, *halo], [field], "spatial_of_right")
+                part = diagonal_of(labels[t], strength[t]) * right + frame_spatial(right, *halos(right_outer, t), edges)
+                square = square + row_sum(right * right)
+                power = power + row_sum(right * part)
+                out[t] = part
+                outer_z[t] = edges[0][0]
+                outer_y[t] = jnp.where(place[1] > 0, edge_weight(face[t], shade_outer[2][t]), 0.0)
+            sums[...] = tile_rows([square, power])
+
+        own, sums, outer_z, outer_y = call(
+            spatial_kernel,
+            [intensity, labels, strength, shade_side, *shade_halo, *right_halo],
+            [field, tile, face_z, face_y],
+            "spatial_of_right",
+        )
 
         def target_rows(told):
             slot = lax.broadcasted_iota(jnp.int32, (owners, slots), 1)
@@ -349,24 +358,21 @@
                 rows += [row[:, :LANES], row[:, LANES:]]
             return tile_rows(rows)
 
-        def flux_kernel(shade, labels, strength, own, slot_tile, *refs):
+        def flux_kernel(shade, labels, strength, own, sums, slot_tile, *refs):
             arrived, refs = refs[: pay1.count], refs[pay1.count :]
             pay, (image, weight, flux, right_in, targets) = refs[: pay2.count], refs[pay2.count :]
             spares = target_rows(pay1.get_spare(arrived))
             targets[...] = spares
             columns = spares.T
-            square = power = jnp.zeros((1, LANES), F32)
-            for t in range(frames):
-                right = to_blocks(right_of(labels[t], strength[t]))
+            square, power = sums[0:1, :], sums[1:2, :]
+            for t in range(frames):
                 part = to_blocks(own[t])
-                square = square + row_sum(right * right)
-                power = power + row_sum(right * part)
                 if t > 0:
                     k = t - 1
                     came = jnp.concatenate([pay1.get(arrived, k), pay1.get(arrived, links + k)], axis=1)
                     came = pick(landing_scatter(spares, k), came)
                     weight_t = edge_weight(came[:, :LANES], to_blocks(shade[t]))
-                    gap = right - came[:, LANES:]
+                    gap = to_blocks(right_of(labels[t], strength[t])) - came[:, LANES:]
                     flux_t = weight_t * gap
                     power = power + row_sum(flux_t * gap)
                     part = part + flux_t
@@ -379,13 +385,14 @@
 
         *payload, part, weight, flux, right_in, targets = call(
             flux_kernel,
-            [intensity, labels, strength, own, slot_tile, *received],
+            [intensity, labels, strength, own, sums, slot_tile, *received],
             pay2.shapes + [field, by_link, by_link, by_link, tile],
             "flux_of_right",
         )
         received = pay2.exchange(payload)
 
-        def residual_kernel(place, labels, strength, part, slot_tile, *refs):
+        def residual_kernel(labels, strength, part, slot_tile, *refs):
+            place = whereabouts()
             arrived, (image, residual, scalars, up, side) = refs[: pay2.count], refs[pay2.count :]
             square, power = unpacked_sums(pay2.get_spare(arrived), 2)
             step = square / power
@@ -399,24 +406,19 @@
                 store_cells(residual, t, to_blocks(right_of(labels[t], strength[t])) - step * image_t)
                 up[t] = residual[t, slices - 1]
                 for z in range(slices):
-                    side[t, z : z + 1, :] = residual[t, z, lines - 1 :, :]
+                    row = residual[t, z]
+                    side[t, z : z + 1, :] = jnp.where(place[1] == 0, row[lines - 1 :], row[:1])
 
         image, residual, scalars, up, side = call(
             residual_kernel,
-            [place, labels, strength, part, slot_tile, *received],
-            [
-                field,
-                field,
-                tile,
-                jax.ShapeDtypeStruct((frames, lines, width), F32),
-                jax.ShapeDtypeStruct((frames, slices, width), F32),
-            ],
+            [labels, strength, part, slot_tile, *received],
+            [field, field, tile, face_z, face_y],
             "first_residual",
         )
         low = lax.ppermute(up, "slc", [(i, i + 1) for i in range(slc_count - 1)])
         beside = lax.ppermute(side, "row", [(i, i + 1) for i in range(row_count - 1)])
 
-        def inner_kernel(place, shade, labels, strength, residual, image, scalars, flux, right_in, weight, targets, *refs):
+        def inner_kernel(shade, labels, strength, residual, image, scalars, flux, right_in, weight, targets, *refs):
             arrived, refs = refs[: pay2.count], refs[pay2.count :]
             pay, (out, sums) = refs[: pay3.count], refs[pay3.count :]
             rows = targets[...]
@@ -445,38 +447,29 @@
 
         *payload, inner, sums = call(
             inner_kernel,
-            [place, intensity, labels, strength, residual, image, scalars, flux, right_in, weight, targets, *received],
+            [intensity, labels, strength, residual, image, scalars, flux, right_in, weight, targets, *received],
             pay3.shapes + [field, tile],
             "inner_image_of_residual",
         )
-        low0, _, side0 = halo
-
-        def outer_kernel(place, shade, residual, sums, low0, side0, low, beside, *refs):
+        def outer_kernel(residual, side, sums, outer_z, outer_y, low, beside, *refs):
             pay, (flow_z, flow_y) = refs[pay3.count : 2 * pay3.count], refs[2 * pay3.count :]
             pay[0][...] = refs[0][...]
             norm, power, cross = sums[0:1], sums[1:2], sums[2:3]
             for t in range(frames):
-                weight_z = jnp.where(place[0] > 0, edge_weight(shade[t, 0], low0[0, t]), 0.0)
-                gap_z = residual[t, 0] - low[t]
-                flow = weight_z * gap_z
+                gap = residual[t, 0] - low[t]
+                flow = outer_z[t] * gap
                 flow_z[t] = flow
-                power = power + row_sum(flow * gap_z)
-                first = [jnp.concatenate([ref[t, z, :1, :] for z in range(slices)], axis=0) for ref in (shade, residual)]
-                weight_y = jnp.where(place[1] > 0, edge_weight(first[0], side0[0, t]), 0.0)
-                gap_y = first[1] - beside[t]
-                flow = weight_y * gap_y
-                flow_y[t] = flow
-                power = power + row_sum(flow * gap_y)
+                power = power + row_sum(flow * gap)
+            gap = side[...] - beside[...]
+            flow = outer_y[...] * gap
+            flow_y[...] = flow
+            power = power + row_sum(flow * gap)
             pay3.put_spare(pay, packed_sums([norm, power, cross]))
 
         *payload, flow_z, flow_y = call(
             outer_kernel,
-            [place, intensity, residual, sums, low0, side0, low, beside, *payload],
-            pay3.shapes
-            + [
-                jax.ShapeDtypeStruct((frames, lines, width), F32),
-                jax.ShapeDtypeStruct((frames, slices, width), F32),
-            ],
+            [residual, side, sums, outer_z, outer_y, low, beside, *payload],
+            pay3.shapes + [face_z, face_y],
             "outer_image_of_residual",
         )
         received = pay3.exchange(payload)

time: 91.4 us -> 86.9 us (0.951)
  starting transfers between devices: 24.4 us -> 31 us
  waiting for transfers between devices: 22.3 us -> 16.6 us
  local copies, waits for them, and re-layouts: 3.6 us -> 0.05 us
  Pallas kernels: 10.4 us -> 8.36 us
    ppermute x1 -> x2, starting transfers between devices: 3.83 us -> 8.12 us  [swap_faces(): lax.ppermute(last, 'slc', [(i, i + 1) for i in range(slc_count - 1)])]
    unnamed x14 -> x20, local copies, waits for them, and re-layouts: 3.6 us -> 0.05 us
    all_to_all x2, waiting for transfers between devices: 9.81 us -> 6.75 us  [exchange(): lax.all_to_all(packed, AXES, split_axis=0, concat_axis=0, tiled=True)]
    pallas_call x7, Pallas kernels: 10.4 us -> 8.36 us  [call(): pl.pallas_call(kernel, out_shape=outputs, in_specs=[spec(leaf) for leaf i...]
    ppermute x1 -> x2, waiting for transfers between devices: 3.68 us -> 1.9 us  [swap_faces(): lax.ppermute(last, 'slc', [(i, i + 1) for i in range(slc_count - 1)])]
    ppermute x1 -> x2, starting transfers between devices: 1.29 us -> 2.58 us  [swap_faces(): lax.ppermute(first, 'slc', [(i + 1, i) for i in range(slc_count - 1)])]
    ppermute x1 -> x2, waiting for transfers between devices: 3.04 us -> 2.27 us  [swap_faces(): lax.ppermute(first, 'slc', [(i + 1, i) for i in range(slc_count - 1)])]
  transfers between devices with their start and end apart: 9 -> 12, of which waited for: 7 -> 7; matrix products, arithmetic and copies ran while one was open for 0% -> 0% of each run, Pallas kernels for 3% -> 2%
where the time goes in v3:
time: 86.9 us; the launch traced here: 86.3 us
  starting transfers between devices  31 us (36%)
  blocking collectives  29.4 us (34%)
  waiting for transfers between devices  16.6 us (19%)
  Pallas kernels  8.36 us (10%)
  between operations  0.9 us (1%)
    all_to_all x1, blocking collectives, exchange(): lax.all_to_all(packed, AXES, split_axis=0, concat_axis=0, tiled=True)  29.4 us
    all_to_all x2, starting transfers between devices, exchange(): lax.all_to_all(packed, AXES, split_axis=0, concat_axis=0, tiled=True)  12 us
    pallas_call x7, Pallas kernels, call(): pl.pallas_call(kernel, out_shape=outputs, in_specs=[spec(leaf) for leaf i...  8.36 us
    ppermute x2, starting transfers between devices, swap_faces(): lax.ppermute(last, 'slc', [(i, i + 1) for i in range(slc_count - 1)])  8.12 us
    all_to_all x2, waiting for transfers between devices, exchange(): lax.all_to_all(packed, AXES, split_axis=0, concat_axis=0, tiled=True)  6.75 us
    ppermute x1, starting transfers between devices, local(): low = lax.ppermute(up, 'slc', [(i, i + 1) for i in range(slc_count - 1)])  2.83 us
    ppermute x1, waiting for transfers between devices, local(): lax.ppermute(flow_z, 'slc', [(i + 1, i) for i in range(slc_count - 1)])  2.71 us
    ppermute x2, starting transfers between devices, swap_faces(): lax.ppermute(first, 'slc', [(i + 1, i) for i in range(slc_count - 1)])  2.58 us
  transfers between devices with their start and end apart: 12, of which 7 were waited for; matrix products, arithmetic and copies ran while one was open for 0% of the time, Pallas kernels for 2%

profile of v3, /device:TPU:0, one launch (start us, length us, event | category | flops | bytes accessed | tf_op | source)
XLA Modules:
  0.0 86.3 jit_solution(8809822370117383294)
XLA Ops:
  0.6 2.7 %send_blocks.1 = (f32[1552,128]{1,0:T(8,128)}, f32[8,128]{1,0:T(8,128)}, f32[4,8,512]{2,1,0:T(8,128)}, f32[4,8,512]{2,1,0:T(8,128)}, f32[4,4,512]{2,1,0:T(4,128)...) custom-call(s32[3,4,4,8]{3,2,1,0:T(4,128)} %bitcast.13, f32[4,4,8,512]{3,2,1,0:T(8,128)} %shade.5, ...), custom_call_target="tpu_custom_call" | custom-call | tf_op jit(solution)/shard_map/send_blocks/pallas_call | solution.py:137
  3.4 0.0 copy-start.9
  3.4 0.0 copy-start.8
  3.4 0.0 copy-start.7
  3.4 0.0 copy-start.6
  3.4 0.0 copy-start.5
  3.4 0.0 copy-start.4
  3.4 0.0 copy-start
  3.4 0.0 copy-start.1
  3.4 0.0 copy-start.2
  3.5 7.5 %all-to-all-start = ((f32[16,97,1,128]{3,2,1,0:T(1,128)}), f32[16,97,1,128]{3,2,1,0:T(1,128)S(1)}, u32[]{:S(2)}, u32[]{:S(2)}) async-start(f32[16,97,1,128]{3,2,1,0:T(1,128)} %bitcast.12), calls=%async_computation | async-start | bytes 1589248 | tf_op jit(solution)/shard_map/all_to_all | solution.py:125
  11.0 0.0 copy-done.9
  11.0 0.5 collective-permute-start.5
  11.5 0.0 copy-done.8
  11.5 3.6 %collective-permute-start = (f32[4,8,512]{2,1,0:T(8,128)S(1)}, f32[4,8,512]{2,1,0:T(8,128)S(1)}, u32[]{:S(2)}, u32[]{:S(2)}) collective-permute-start(f32[4,8,512]{2,1,0:T(8,128)S(1)} %copy-done.8), channel_id=1, source_target_pairs={{0,2},{2,4},{4,6},{6,8},{8,10},{10,12},{12,14},{1,3},{3,5},{5,7},{... | collective-permute-start | bytes 196616 | tf_op jit(solution)/shard_map/ppermute | solution.py:246
  15.1 0.0 copy-done.7
  15.1 1.3 %collective-permute-start.1 = (f32[4,8,512]{2,1,0:T(8,128)S(1)}, f32[4,8,512]{2,1,0:T(8,128)S(1)}, u32[]{:S(2)}, u32[]{:S(2)}) collective-permute-start(f32[4,8,512]{2,1,0:T(8,128)S(1)} %copy-done.7), channel_id=1, source_target_pairs={{2,0},{4,2},{6,4},{8,6},{10,8},{12,10},{14,12},{3,1},{5,3},{7,5},{... | collective-permute-start | bytes 196616 | tf_op jit(solution)/shard_map/ppermute | solution.py:247
  16.4 0.0 copy-done.6
  16.4 4.5 %collective-permute-start.3 = (f32[4,8,512]{2,1,0:T(8,128)S(1)}, f32[4,8,512]{2,1,0:T(8,128)S(1)}, u32[]{:S(2)}, u32[]{:S(2)}) collective-permute-start(f32[4,8,512]{2,1,0:T(8,128)S(1)} %copy-done.6), channel_id=1, source_target_pairs={{0,2},{2,4},{4,6},{6,8},{8,10},{10,12},{12,14},{1,3},{3,5},{5,7},{... | collective-permute-start | bytes 196616 | tf_op jit(solution)/shard_map/ppermute | solution.py:246
  20.9 0.0 copy-done.5
  21.0 1.3 %collective-permute-start.4 = (f32[4,8,512]{2,1,0:T(8,128)S(1)}, f32[4,8,512]{2,1,0:T(8,128)S(1)}, u32[]{:S(2)}, u32[]{:S(2)}) collective-permute-start(f32[4,8,512]{2,1,0:T(8,128)S(1)} %copy-done.5), channel_id=1, source_target_pairs={{2,0},{4,2},{6,4},{8,6},{10,8},{12,10},{14,12},{3,1},{5,3},{7,5},{... | collective-permute-start | bytes 196616 | tf_op jit(solution)/shard_map/ppermute | solution.py:247
  22.3 0.0 collective-permute-done.5.refs_5_
  22.3 0.0 copy-done.4
  22.3 0.1 collective-permute-start.2
  22.4 1.2 %collective-permute-done.2.refs_2_ = f32[4,4,512]{2,1,0:T(4,128)S(1)} collective-permute-done((f32[4,4,512]{2,1,0:T(4,128)S(1)}, f32[4,4,512]{2,1,0:T(4,128)S(1)}, u32[]{:S(2)}, u32[]{:S(2)}) %collective-permute-start.2) | collective-permute-done | bytes 32800 | tf_op jit(solution)/shard_map/ppermute | solution.py:248
  23.5 0.0 collective-permute-done.refs_0_
  23.5 0.0 collective-permute-done.1.refs_1_
  23.6 1.9 %collective-permute-done.3.refs_3_ = f32[4,8,512]{2,1,0:T(8,128)S(1)} collective-permute-done((f32[4,8,512]{2,1,0:T(8,128)S(1)}, f32[4,8,512]{2,1,0:T(8,128)S(1)}, u32[]{:S(2)}, u32[]{:S(2)}) %collective-permute-start.3) | collective-permute-done | bytes 65568 | tf_op jit(solution)/shard_map/ppermute | solution.py:246
  25.4 2.3 %collective-permute-done.4.refs_4_ = f32[4,8,512]{2,1,0:T(8,128)S(1)} collective-permute-done((f32[4,8,512]{2,1,0:T(8,128)S(1)}, f32[4,8,512]{2,1,0:T(8,128)S(1)}, u32[]{:S(2)}, u32[]{:S(2)}) %collective-permute-start.4) | collective-permute-done | bytes 65568 | tf_op jit(solution)/shard_map/ppermute | solution.py:247
  27.7 0.0 copy-done
  27.7 0.6 spatial_of_right.1
  28.3 1.5 %all-to-all-done = f32[16,97,1,128]{3,2,1,0:T(1,128)S(1)} async-done(((f32[16,97,1,128]{3,2,1,0:T(1,128)}), f32[16,97,1,128]{3,2,1,0:T(1,128)S(1)}, u32[]{:S(2)}, u32[]{:S(2)}) %all-to-all-start) | async-done | bytes 794656 | tf_op jit(solution)/shard_map/all_to_all | solution.py:125
  29.8 1.5 %flux_of_right.1 = (f32[1552,128]{1,0:T(8,128)S(1)}, f32[4,4,8,512]{3,2,1,0:T(8,128)S(1)}, f32[3,128,128]{2,1,0:T(8,128)S(1)}, f32[3,128,128]{2,1,0:T(8,128)S(1)...) custom-call(f32[4,4,8,512]{3,2,1,0:T(8,128)S(1)} %copy-done.2, s32[4,4,8,512]{3,2,1,0:T(8,128)S(1)} %copy-done, ...), custom_call_target="tpu_custom_call" | custom-call | tf_op jit(solution)/shard_map/flux_of_right/pallas_call | solution.py:137
  31.4 29.4 %all_to_all.15 = f32[16,97,1,128]{3,2,1,0:T(1,128)S(1)} all-to-all(f32[16,97,1,128]{3,2,1,0:T(1,128)S(1)} %bitcast.11), channel_id=1, replica_groups=mesh['grp'=2,'slc'=8,'row'=2] {'slc','row'}, dimensions={0} | all-to-all | bytes 1589248 | tf_op jit(solution)/shard_map/all_to_all | solution.py:125
  60.8 0.4 first_residual.1
  61.2 2.8 %collective-permute-start.6 = (f32[4,8,512]{2,1,0:T(8,128)S(1)}, f32[4,8,512]{2,1,0:T(8,128)S(1)}, u32[]{:S(2)}, u32[]{:S(2)}) collective-permute-start(f32[4,8,512]{2,1,0:T(8,128)S(1)} %get-tuple-element.55), channel_id=1, source_target_pairs={{0,2},{2,4},{4,6},{6,8},{8,10},{10,12},{12,14},{1,3},{3,5},{5,7},{... | collective-permute-start | bytes 196616 | tf_op jit(solution)/shard_map/ppermute | solution.py:418
  64.0 2.3 %collective-permute-start.7 = (f32[4,4,512]{2,1,0:T(4,128)S(1)}, f32[4,4,512]{2,1,0:T(4,128)S(1)}, u32[]{:S(2)}, u32[]{:S(2)}) collective-permute-start(f32[4,4,512]{2,1,0:T(4,128)S(1)} %get-tuple-element.51.side), channel_id=1, source_target_pairs={{0,1},{2,3},{4,5},{6,7},{8,9},{10,11},{12,13},{14,15},{16,17},{18,... | collective-permute-start | bytes 98312 | tf_op jit(solution)/shard_map/ppermute | solution.py:419
  66.3 1.0 %inner_image_of_residual.1 = (f32[784,128]{1,0:T(8,128)S(1)}, f32[4,4,8,512]{3,2,1,0:T(8,128)S(1)}, f32[8,128]{1,0:T(8,128)S(1)}) custom-call(f32[4,4,8,512]{3,2,1,0:T(8,128)S(1)} %copy-done.2, s32[4,4,8,512]{3,2,1,0:T(8,128)S(1)} %copy-done, f32[4,4,8,512]{3,2,1,0:T(8,128)S(1)} %copy-done.1, f32[4,4,8,512]{3,2,1,0:T(8,128)S(1)} %get-tuple-element.43.residual, ...), custom_call_target="tpu_custom_call" | custom-call | tf_op jit(solution)/shard_map/inner_image_of_residual/pallas_call | solution.py:137
  67.3 0.0 collective-permute-done.7.beside
  67.4 0.0 collective-permute-done.6.low
  67.4 0.9 %outer_image_of_residual.1 = (f32[784,128]{1,0:T(8,128)}, f32[4,8,512]{2,1,0:T(8,128)S(1)}, f32[4,4,512]{2,1,0:T(4,128)S(1)}) custom-call(f32[4,4,8,512]{3,2,1,0:T(8,128)S(1)} %get-tuple-element.43.residual, f32[4,4,512]{2,1,0:T(4,128)S(1)} %get-tuple-element.51.side, f32[8,128]{1,0:T(8,128)S(1)} %get-tuple-element.52.sums, ...), custom_call_target="tpu_custom_call" | custom-call | tf_op jit(solution)/shard_map/outer_image_of_residual/pallas_call | solution.py:137
  68.3 4.5 %all-to-all-start.2 = ((f32[16,49,1,128]{3,2,1,0:T(1,128)}), f32[16,49,1,128]{3,2,1,0:T(1,128)S(1)}, u32[]{:S(2)}, u32[]{:S(2)}) async-start(f32[16,49,1,128]{3,2,1,0:T(1,128)} %bitcast.5), calls=%async_computation.2 | async-start | bytes 802816 | tf_op jit(solution)/shard_map/all_to_all | solution.py:125
  72.7 1.3 %collective-permute-start.8 = (f32[4,8,512]{2,1,0:T(8,128)S(1)}, f32[4,8,512]{2,1,0:T(8,128)S(1)}, u32[]{:S(2)}, u32[]{:S(2)}) collective-permute-start(f32[4,8,512]{2,1,0:T(8,128)S(1)} %get-tuple-element.57.flow_z), channel_id=1, source_target_pairs={{2,0},{4,2},{6,4},{8,6},{10,8},{12,10},{14,12},{3,1},{5,3},{7,5},{... | collective-permute-start | bytes 196616 | tf_op jit(solution)/shard_map/ppermute | solution.py:476
  74.0 1.3 %collective-permute-start.9 = (f32[4,4,512]{2,1,0:T(4,128)S(1)}, f32[4,4,512]{2,1,0:T(4,128)S(1)}, u32[]{:S(2)}, u32[]{:S(2)}) collective-permute-start(f32[4,4,512]{2,1,0:T(4,128)S(1)} %get-tuple-element.58.flow_y), channel_id=1, source_target_pairs={{1,0},{3,2},{5,4},{7,6},{9,8},{11,10},{13,12},{15,14},{17,16},{19,... | collective-permute-start | bytes 98312 | tf_op jit(solution)/shard_map/ppermute | solution.py:477
  75.3 1.8 %collective-permute-done.9.high_y = f32[4,4,512]{2,1,0:T(4,128)S(1)} collective-permute-done((f32[4,4,512]{2,1,0:T(4,128)S(1)}, f32[4,4,512]{2,1,0:T(4,128)S(1)}, u32[]{:S(2)}, u32[]{:S(2)}) %collective-permute-start.9) | collective-permute-done | bytes 32800 | tf_op jit(solution)/shard_map/ppermute | solution.py:477
  77.1 2.7 %collective-permute-done.8.high_z = f32[4,8,512]{2,1,0:T(8,128)S(1)} collective-permute-done((f32[4,8,512]{2,1,0:T(8,128)S(1)}, f32[4,8,512]{2,1,0:T(8,128)S(1)}, u32[]{:S(2)}, u32[]{:S(2)}) %collective-permute-start.8) | collective-permute-done | bytes 65568 | tf_op jit(solution)/shard_map/ppermute | solution.py:476
  79.8 5.2 %all-to-all-done.2 = f32[16,49,1,128]{3,2,1,0:T(1,128)S(1)} async-done(((f32[16,49,1,128]{3,2,1,0:T(1,128)}), f32[16,49,1,128]{3,2,1,0:T(1,128)S(1)}, u32[]{:S(2)}, u32[]{:S(2)}) %all-to-all-start.2) | async-done | bytes 401440 | tf_op jit(solution)/shard_map/all_to_all | solution.py:125
  85.1 1.3 %solution_and_residual.1 = (f32[4,4,8,512]{3,2,1,0:T(8,128)}, f32[4,4,8,512]{3,2,1,0:T(8,128)}) custom-call(s32[4,4,8,512]{3,2,1,0:T(8,128)S(1)} %copy-done, f32[4,4,8,512]{3,2,1,0:T(8,128)S(1)} %copy-done.1, f32[4,4,8,512]{3,2,1,0:T(8,128)S(1)} %get-tuple-element.43.residual, f32[4,4,8,512]{3,2,1,0:T(8,128)S(1)} %get-tuple-element.44.image, ...), custom_call_target="tpu_custom_call" | custom-call | tf_op jit(solution)/shard_map/solution_and_residual/pallas_call | solution.py:137
  (4 shorter events, 0.0 us)
Async XLA Ops:
  3.4 7.6 %copy-start.9 = (f32[4,4,512]{2,1,0:T(4,128)S(1)}, f32[4,4,512]{2,1,0:T(4,128)}, u32[]{:S(2)}) copy-start(f32[4,4,512]{2,1,0:T(4,128)} %get-tuple-element.36) | copy-start | bytes 98308
  3.4 8.1 %copy-start.8 = (f32[4,8,512]{2,1,0:T(8,128)S(1)}, f32[4,8,512]{2,1,0:T(8,128)}, u32[]{:S(2)}) copy-start(f32[4,8,512]{2,1,0:T(8,128)} %get-tuple-element.32) | copy-start | bytes 196612
  3.4 11.7 %copy-start.7 = (f32[4,8,512]{2,1,0:T(8,128)S(1)}, f32[4,8,512]{2,1,0:T(8,128)}, u32[]{:S(2)}) copy-start(f32[4,8,512]{2,1,0:T(8,128)} %get-tuple-element.33) | copy-start | bytes 196612
  3.4 13.0 %copy-start.6 = (f32[4,8,512]{2,1,0:T(8,128)S(1)}, f32[4,8,512]{2,1,0:T(8,128)}, u32[]{:S(2)}) copy-start(f32[4,8,512]{2,1,0:T(8,128)} %get-tuple-element.34) | copy-start | bytes 196612
  3.4 17.5 %copy-start.5 = (f32[4,8,512]{2,1,0:T(8,128)S(1)}, f32[4,8,512]{2,1,0:T(8,128)}, u32[]{:S(2)}) copy-start(f32[4,8,512]{2,1,0:T(8,128)} %get-tuple-element.35) | copy-start | bytes 196612
  3.4 18.9 %copy-start.4 = (f32[4,4,512]{2,1,0:T(4,128)S(1)}, f32[4,4,512]{2,1,0:T(4,128)}, u32[]{:S(2)}) copy-start(f32[4,4,512]{2,1,0:T(4,128)} %get-tuple-element.31.face) | copy-start | bytes 98308
  3.4 24.3 %copy-start = (s32[4,4,8,512]{3,2,1,0:T(8,128)S(1)}, s32[4,4,8,512]{3,2,1,0:T(8,128)}, u32[]{:S(2)}) copy-start(s32[4,4,8,512]{3,2,1,0:T(8,128)} %labels.9) | copy-start | bytes 786436
  3.4 24.3 %copy-start.1 = (f32[4,4,8,512]{3,2,1,0:T(8,128)S(1)}, f32[4,4,8,512]{3,2,1,0:T(8,128)}, u32[]{:S(2)}) copy-start(f32[4,4,8,512]{3,2,1,0:T(8,128)} %strength.9) | copy-start | bytes 786436
  3.4 24.3 %copy-start.2 = (f32[4,4,8,512]{3,2,1,0:T(8,128)S(1)}, f32[4,4,8,512]{3,2,1,0:T(8,128)}, u32[]{:S(2)}) copy-start(f32[4,4,8,512]{3,2,1,0:T(8,128)} %shade.5) | copy-start | bytes 786436
  3.5 26.4 %all-to-all-start = ((f32[16,97,1,128]{3,2,1,0:T(1,128)}), f32[16,97,1,128]{3,2,1,0:T(1,128)S(1)}, u32[]{:S(2)}, u32[]{:S(2)}) async-start(f32[16,97,1,128]{3,2,1,0:T(1,128)} %bitcast.12), calls=%async_computation | async-start | bytes 1589248 | tf_op jit(solution)/shard_map/all_to_all | solution.py:125
  11.0 11.2 %collective-permute-start.5 = (f32[4,4,512]{2,1,0:T(4,128)S(1)}, f32[4,4,512]{2,1,0:T(4,128)S(1)}, u32[]{:S(2)}, u32[]{:S(2)}) collective-permute-start(f32[4,4,512]{2,1,0:T(4,128)S(1)} %copy-done.9), channel_id=1, source_target_pairs={{0,1},{1,0},{2,3},{3,2},{4,5},{5,4},{6,7},{7,6},{8,9},{9,8},{10,11... | collective-permute-start | bytes 98312 | tf_op jit(solution)/shard_map/ppermute | solution.py:248
  11.5 12.1 %collective-permute-start = (f32[4,8,512]{2,1,0:T(8,128)S(1)}, f32[4,8,512]{2,1,0:T(8,128)S(1)}, u32[]{:S(2)}, u32[]{:S(2)}) collective-permute-start(f32[4,8,512]{2,1,0:T(8,128)S(1)} %copy-done.8), channel_id=1, source_target_pairs={{0,2},{2,4},{4,6},{6,8},{8,10},{10,12},{12,14},{1,3},{3,5},{5,7},{... | collective-permute-start | bytes 196616 | tf_op jit(solution)/shard_map/ppermute | solution.py:246
  15.1 8.5 %collective-permute-start.1 = (f32[4,8,512]{2,1,0:T(8,128)S(1)}, f32[4,8,512]{2,1,0:T(8,128)S(1)}, u32[]{:S(2)}, u32[]{:S(2)}) collective-permute-start(f32[4,8,512]{2,1,0:T(8,128)S(1)} %copy-done.7), channel_id=1, source_target_pairs={{2,0},{4,2},{6,4},{8,6},{10,8},{12,10},{14,12},{3,1},{5,3},{7,5},{... | collective-permute-start | bytes 196616 | tf_op jit(solution)/shard_map/ppermute | solution.py:247
  16.4 9.1 %collective-permute-start.3 = (f32[4,8,512]{2,1,0:T(8,128)S(1)}, f32[4,8,512]{2,1,0:T(8,128)S(1)}, u32[]{:S(2)}, u32[]{:S(2)}) collective-permute-start(f32[4,8,512]{2,1,0:T(8,128)S(1)} %copy-done.6), channel_id=1, source_target_pairs={{0,2},{2,4},{4,6},{6,8},{8,10},{10,12},{12,14},{1,3},{3,5},{5,7},{... | collective-permute-start | bytes 196616 | tf_op jit(solution)/shard_map/ppermute | solution.py:246
  21.0 6.8 %collective-permute-start.4 = (f32[4,8,512]{2,1,0:T(8,128)S(1)}, f32[4,8,512]{2,1,0:T(8,128)S(1)}, u32[]{:S(2)}, u32[]{:S(2)}) collective-permute-start(f32[4,8,512]{2,1,0:T(8,128)S(1)} %copy-done.5), channel_id=1, source_target_pairs={{2,0},{4,2},{6,4},{8,6},{10,8},{12,10},{14,12},{3,1},{5,3},{7,5},{... | collective-permute-start | bytes 196616 | tf_op jit(solution)/shard_map/ppermute | solution.py:247
  22.3 1.3 %collective-permute-start.2 = (f32[4,4,512]{2,1,0:T(4,128)S(1)}, f32[4,4,512]{2,1,0:T(4,128)S(1)}, u32[]{:S(2)}, u32[]{:S(2)}) collective-permute-start(f32[4,4,512]{2,1,0:T(4,128)S(1)} %copy-done.4), channel_id=1, source_target_pairs={{0,1},{1,0},{2,3},{3,2},{4,5},{5,4},{6,7},{7,6},{8,9},{9,8},{10,11... | collective-permute-start | bytes 98312 | tf_op jit(solution)/shard_map/ppermute | solution.py:248
  28.3 1.5 %copy-start.3 = (f32[8,128]{1,0:T(8,128)S(1)}, f32[8,128]{1,0:T(8,128)}, u32[]{:S(2)}) copy-start(f32[8,128]{1,0:T(8,128)} %get-tuple-element.39.slot_tile) | copy-start | bytes 12292
  61.2 6.1 %collective-permute-start.6 = (f32[4,8,512]{2,1,0:T(8,128)S(1)}, f32[4,8,512]{2,1,0:T(8,128)S(1)}, u32[]{:S(2)}, u32[]{:S(2)}) collective-permute-start(f32[4,8,512]{2,1,0:T(8,128)S(1)} %get-tuple-element.55), channel_id=1, source_target_pairs={{0,2},{2,4},{4,6},{6,8},{8,10},{10,12},{12,14},{1,3},{3,5},{5,7},{... | collective-permute-start | bytes 196616 | tf_op jit(solution)/shard_map/ppermute | solution.py:418
  64.0 3.3 %collective-permute-start.7 = (f32[4,4,512]{2,1,0:T(4,128)S(1)}, f32[4,4,512]{2,1,0:T(4,128)S(1)}, u32[]{:S(2)}, u32[]{:S(2)}) collective-permute-start(f32[4,4,512]{2,1,0:T(4,128)S(1)} %get-tuple-element.51.side), channel_id=1, source_target_pairs={{0,1},{2,3},{4,5},{6,7},{8,9},{10,11},{12,13},{14,15},{16,17},{18,... | collective-permute-start | bytes 98312 | tf_op jit(solution)/shard_map/ppermute | solution.py:419
  68.3 16.8 %all-to-all-start.2 = ((f32[16,49,1,128]{3,2,1,0:T(1,128)}), f32[16,49,1,128]{3,2,1,0:T(1,128)S(1)}, u32[]{:S(2)}, u32[]{:S(2)}) async-start(f32[16,49,1,128]{3,2,1,0:T(1,128)} %bitcast.5), calls=%async_computation.2 | async-start | bytes 802816 | tf_op jit(solution)/shard_map/all_to_all | solution.py:125
  72.7 7.1 %collective-permute-start.8 = (f32[4,8,512]{2,1,0:T(8,128)S(1)}, f32[4,8,512]{2,1,0:T(8,128)S(1)}, u32[]{:S(2)}, u32[]{:S(2)}) collective-permute-start(f32[4,8,512]{2,1,0:T(8,128)S(1)} %get-tuple-element.57.flow_z), channel_id=1, source_target_pairs={{2,0},{4,2},{6,4},{8,6},{10,8},{12,10},{14,12},{3,1},{5,3},{7,5},{... | collective-permute-start | bytes 196616 | tf_op jit(solution)/shard_map/ppermute | solution.py:476
  74.0 3.1 %collective-permute-start.9 = (f32[4,4,512]{2,1,0:T(4,128)S(1)}, f32[4,4,512]{2,1,0:T(4,128)S(1)}, u32[]{:S(2)}, u32[]{:S(2)}) collective-permute-start(f32[4,4,512]{2,1,0:T(4,128)S(1)} %get-tuple-element.58.flow_y), channel_id=1, source_target_pairs={{1,0},{3,2},{5,4},{7,6},{9,8},{11,10},{13,12},{15,14},{17,16},{19,... | collective-permute-start | bytes 98312 | tf_op jit(solution)/shard_map/ppermute | solution.py:477

commit v4 on v3

--- a/solution.py
+++ b/solution.py
@@ -42,7 +42,13 @@
     rest = values - high.astype(F32)
     middle = rest.astype(jnp.bfloat16)
     low = (rest - middle.astype(F32)).astype(jnp.bfloat16)
-    width = values.shape[1]
+    depth, width = values.shape
+    if depth <= LANES:
+        pieces = [jnp.concatenate([high, low], axis=1), jnp.concatenate([middle, jnp.zeros_like(low)], axis=1)]
+        out = jnp.dot(
+            jnp.concatenate([one_hot, one_hot], axis=1), jnp.concatenate(pieces, axis=0), preferred_element_type=F32
+        )
+        return out[:, :width] + out[:, width:]
     out = jnp.dot(one_hot, jnp.concatenate([high, middle, low], axis=1), preferred_element_type=F32)
     return out[:, :width] + out[:, width : 2 * width] + out[:, 2 * width :]
 
@@ -130,19 +136,35 @@
         return [rows, packed[:, self.rows]]
 
 
-def call(kernel, inputs, outputs, name, far=False, scratch=()):
-    def spec(leaf):
-        return pl.BlockSpec(memory_space=pltpu.HBM if far else pltpu.VMEM)
-
+def call(kernel, inputs, outputs, name, far=False, far_outputs=False, scratch=()):
+    near, away = pl.BlockSpec(memory_space=pltpu.VMEM), pl.BlockSpec(memory_space=pltpu.HBM)
     return pl.pallas_call(
         kernel,
         out_shape=outputs,
-        in_specs=[spec(leaf) for leaf in inputs],
-        out_specs=[pl.BlockSpec(memory_space=pltpu.VMEM) for _ in outputs],
+        in_specs=[away if far else near for _ in inputs],
+        out_specs=[away if far_outputs else near for _ in outputs],
         scratch_shapes=scratch,
         compiler_params=pltpu.CompilerParams(vmem_limit_bytes=VMEM_WHOLE if far else VMEM_LIMIT),
         name=name,
     )(*inputs)
+
+
+class Sender:
+    def __init__(self, semaphores):
+        self.semaphores, self.copies = semaphores, []
+
+    def start(self, source, target, parts=1):
+        rows = source.shape[0]
+        step = -(-rows // (parts * SUBLANES)) * SUBLANES if parts > 1 else rows
+        for first in range(0, rows, step):
+            piece = pl.ds(first, min(step, rows - first))
+            copy = pltpu.make_async_copy(source.at[piece], target.at[piece], self.semaphores.at[len(self.copies)])
+            copy.start()
+            self.copies.append(copy)
+
+    def wait(self):
+        for copy in self.copies:
+            copy.wait()
 
 
 def right_of(labels, strength):
@@ -181,34 +203,25 @@
     return jnp.sum(total, axis=0, keepdims=True)
 
 
-def frame_edges(shade, first, last, side, place, slice_count):
+def inner_edges(shade):
     slices, lines, width = shade.shape
     line = lax.broadcasted_iota(jnp.int32, shade.shape, 1)
     cell = lax.broadcasted_iota(jnp.int32, shade.shape, 2)
-    low = high = below = outer = 0.0
-    if place is not None:
-        low = jnp.where(place[0] > 0, edge_weight(shade[0], first), 0.0)
-        high = jnp.where(place[0] < slice_count - 1, edge_weight(last, shade[slices - 1]), 0.0)
-        outer = edge_weight(side, shade)
-        below = jnp.where(place[1] == 0, 0.0, outer)
-        outer = jnp.where(place[1] == 0, outer, 0.0)
-    along_z = [low] + [edge_weight(shade[z], shade[z - 1]) for z in range(1, slices)] + [high]
-    along_y = edge_weight(pltpu.roll(shade, lines - 1, 1), shade)
-    along_y = jnp.where(line == lines - 1, outer, along_y)
+    along_z = [edge_weight(shade[z + 1], shade[z]) for z in range(slices - 1)]
+    along_y = jnp.where(line == lines - 1, 0.0, edge_weight(pltpu.roll(shade, lines - 1, 1), shade))
     along_x = jnp.where(cell == width - 1, 0.0, edge_weight(pltpu.roll(shade, width - 1, 2), shade))
-    return along_z, along_y, below, along_x
-
-
-def frame_spatial(field, first, last, side, edges):
-    along_z, along_y, below, along_x = edges
+    return along_z, along_y, along_x
+
+
+def inner_spatial(field, edges):
+    along_z, along_y, along_x = edges
     slices, lines, width = field.shape
-    line = lax.broadcasted_iota(jnp.int32, field.shape, 1)
-    layers = [first] + [field[z] for z in range(slices)] + [last]
-    flow_z = [along_z[k] * (layers[k + 1] - layers[k]) for k in range(slices + 1)]
+    flow_z = [along_z[z] * (field[z + 1] - field[z]) for z in range(slices - 1)]
+    none = jnp.zeros((lines, width), F32)
+    flow_z = [none] + flow_z + [none]
     coupled = jnp.stack([flow_z[z] - flow_z[z + 1] for z in range(slices)])
-    above = jnp.where(line == lines - 1, side, pltpu.roll(field, lines - 1, 1))
-    flow_y = along_y * (above - field)
-    coupled = coupled - flow_y + jnp.where(line == 0, below * (field - side), pltpu.roll(flow_y, 1, 1))
+    flow_y = along_y * (pltpu.roll(field, lines - 1, 1) - field)
+    coupled = coupled - flow_y + pltpu.roll(flow_y, 1, 1)
     flow_x = along_x * (pltpu.roll(field, width - 1, 2) - field)
     return coupled - flow_x + pltpu.roll(flow_x, 1, 2)
 
@@ -216,6 +229,7 @@
 def local_step(mesh):
     slc_count, row_count = mesh.shape["slc"], mesh.shape["row"]
     owners = slc_count * row_count
+    assert row_count == 2
 
     def local(intensity, labels, strength, partner):
         frames, slices, lines, width = intensity.shape
@@ -236,20 +250,26 @@
         def whereabouts():
             return lax.axis_index("slc"), lax.axis_index("row")
         def put_faces(refs, place, frame, cells):
-            refs[0][frame] = cells[0]
-            refs[1][frame] = cells[slices - 1]
-            inner = jnp.where(place[1] == 0, cells[:, lines - 1 :], cells[:, :1])
+            line = place[1] == 0
+            refs[0][frame] = jnp.where(line, cells[slices - 1], cells[0])
+            refs[1][frame] = jnp.where(line, cells[0], cells[slices - 1])
+            inner = jnp.where(line, cells[:, lines - 1 :], cells[:, :1])
             for z in range(slices):
                 refs[2][frame, z : z + 1, :] = inner[z]
 
-        def swap_faces(first, last, side):
-            below = lax.ppermute(last, "slc", [(i, i + 1) for i in range(slc_count - 1)])
-            above = lax.ppermute(first, "slc", [(i + 1, i) for i in range(slc_count - 1)])
-            beside = lax.ppermute(side, "row", [(i, i ^ 1) for i in range(row_count)])
-            return below, above, beside
-
-        def halos(refs, frame):
-            return refs[0][frame], refs[1][frame], refs[2][frame][:, None, :]
+        up = [(2 * k, 2 * k + 2) for k in range(slc_count - 1)]
+        down = [(2 * k + 3, 2 * k + 1) for k in range(slc_count - 1)]
+        ring = up + [(owners - 2, owners - 1)] + down + [(1, 0)]
+
+        def swap_faces(along, against, side):
+            return (
+                lax.ppermute(along, AXES, ring),
+                lax.ppermute(against, AXES, [(j, i) for i, j in ring]),
+                lax.ppermute(side, "row", [(0, 1), (1, 0)]),
+            )
+
+        def facing(faces):
+            return faces[1], faces[0], faces[2]
 
         def id_rows(ids):
             per_link = slices * (width // LANES)
@@ -269,10 +289,11 @@
             return rows[:links], rows[links:]
 
         def send_kernel(*refs):
+            sources, refs = refs[:4], refs[4:]
+            count = pay1.count + 7
+            targets, held, (ids, shade, labels, strength, done, sent) = refs[:count], refs[count : 2 * count], refs[2 * count :]
+            pay, (slots_out, *faces) = held[: pay1.count], held[pay1.count :]
             place = whereabouts()
-            sources, refs = refs[:4], refs[4:]
-            pay, (slots_out, *faces) = refs[: pay1.count], refs[pay1.count : -5]
-            ids, shade, labels, strength, done = refs[-5:]
             copies = [pltpu.make_async_copy(*pair, done.at[k]) for k, pair in enumerate(zip(sources, (ids, shade, labels, strength)))]
             for copy in copies:
                 copy.start()
@@ -287,8 +308,8 @@
                 x_block = there & ((1 << width_bits) - 1)
                 target = (there >> (width_bits + line_bits) << (width_bits + line_bits)) + (x_block << line_bits) + line
                 owned = jnp.where(iota((owners, LANES), 0) == owner, 1.0, 0.0)
-                count = jnp.dot(owned.astype(jnp.bfloat16), before, preferred_element_type=F32)
-                rank = jnp.sum(owned * count, axis=0, keepdims=True)
+                count_before = jnp.dot(owned.astype(jnp.bfloat16), before, preferred_element_type=F32)
+                rank = jnp.sum(owned * count_before, axis=0, keepdims=True)
                 slot_rows.append(owner * capacity + rank)
                 told = told + lax.dot_general(
                     (owned * (target.astype(F32) + 1.0)).astype(jnp.bfloat16),
@@ -300,50 +321,96 @@
             slots_out[...] = tile_rows(slot_rows)
             for copy in copies[1:]:
                 copy.wait()
+            rights = [right_of(labels[t], strength[t]) for t in range(frames)]
+            for t in range(frames):
+                put_faces(faces[:3], place, t, shade[t])
+                put_faces(faces[3:], place, t, rights[t])
+            gone = Sender(sent)
+            for k in range(pay1.count, count):
+                gone.start(held[k], targets[k])
+            for t in range(links):
+                both = pick(gather_matrix(slot_rows[t], slots), jnp.concatenate([to_blocks(shade[t]), to_blocks(rights[t])], axis=1))
+                pay1.put(pay, t, both[:, :LANES])
+                pay1.put(pay, links + t, both[:, LANES:])
+            for k in range(pay1.count):
+                gone.start(held[k], targets[k], 8)
+            gone.wait()
+
+        send_outputs = pay1.shapes + [tile] + [face_z, face_z, face_y] * 2
+        *payload, slot_tile, faces0, faces1, faces2, faces3, faces4, faces5 = call(
+            send_kernel,
+            [partner.transpose(0, 1, 3, 2), intensity, labels, strength],
+            send_outputs,
+            "send_blocks",
+            far=True,
+            far_outputs=True,
+            scratch=[pltpu.VMEM(leaf.shape, leaf.dtype) for leaf in send_outputs]
+            + [pltpu.VMEM((links, slices, width // LANES, lines), jnp.int32)]
+            + [pltpu.VMEM(leaf.shape, leaf.dtype) for leaf in (intensity, labels, strength)]
+            + [pltpu.SemaphoreType.DMA((4,)), pltpu.SemaphoreType.DMA((32,))],
+        )
+        shade_faces, right_faces = (faces0, faces1, faces2), (faces3, faces4, faces5)
+        shade_halo, right_halo = swap_faces(*shade_faces), swap_faces(*right_faces)
+        received = pay1.exchange(payload)
+
+        def own_kernel(shade, labels, strength, slot_tile, out, sums, slots_out):
+            square = power = jnp.zeros((1, LANES), F32)
             for t in range(frames):
                 right = right_of(labels[t], strength[t])
-                put_faces(faces[:3], place, t, shade[t])
-                put_faces(faces[3:], place, t, right)
-                if t < links:
-                    sent = pick(gather_matrix(slot_rows[t], slots), jnp.concatenate([to_blocks(shade[t]), to_blocks(right)], axis=1))
-                    pay1.put(pay, t, sent[:, :LANES])
-                    pay1.put(pay, links + t, sent[:, LANES:])
-
-        *payload, slot_tile, shade_first, shade_last, shade_side, right_first, right_last, right_side = call(
-            send_kernel,
-            [partner.transpose(0, 1, 3, 2), intensity, labels, strength],
-            pay1.shapes + [tile] + [face_z, face_z, face_y] * 2,
-            "send_blocks",
-            far=True,
-            scratch=[pltpu.VMEM((links, slices, width // LANES, lines), jnp.int32)]
-            + [pltpu.VMEM(leaf.shape, leaf.dtype) for leaf in (intensity, labels, strength)]
-            + [pltpu.SemaphoreType.DMA((4,))],
-        )
-        shade_halo = swap_faces(shade_first, shade_last, shade_side)
-        right_halo = swap_faces(right_first, right_last, right_side)
-        received = pay1.exchange(payload)
-
-        def spatial_kernel(shade, labels, strength, face, *refs):
-            shade_outer, right_outer, (out, sums, outer_z, outer_y) = refs[:3], refs[3:6], refs[6:]
-            place = whereabouts()
-            square = power = jnp.zeros((1, LANES), F32)
-            for t in range(frames):
-                edges = frame_edges(shade[t], *halos(shade_outer, t), place, slc_count)
-                right = right_of(labels[t], strength[t])
-                part = diagonal_of(labels[t], strength[t]) * right + frame_spatial(right, *halos(right_outer, t), edges)
+                part = diagonal_of(labels[t], strength[t]) * right + inner_spatial(right, inner_edges(shade[t]))
                 square = square + row_sum(right * right)
                 power = power + row_sum(right * part)
                 out[t] = part
-                outer_z[t] = edges[0][0]
-                outer_y[t] = jnp.where(place[1] > 0, edge_weight(face[t], shade_outer[2][t]), 0.0)
             sums[...] = tile_rows([square, power])
-
-        own, sums, outer_z, outer_y = call(
-            spatial_kernel,
-            [intensity, labels, strength, shade_side, *shade_halo, *right_halo],
-            [field, tile, face_z, face_y],
-            "spatial_of_right",
-        )
+            slots_out[...] = slot_tile[...]
+
+        own, sums, slot_tile = call(own_kernel, [intensity, labels, strength, slot_tile], [field, tile, tile], "inner_image_of_right")
+
+        edge_shapes = [face_z, face_z, face_y]
+
+        def edge_kernel(sums, *refs):
+            shade, shade_out, right, right_out = (refs[k : k + 3] for k in (0, 3, 6, 9))
+            total, weights, flows = refs[12], refs[13:16], refs[16:]
+            place = whereabouts()
+            line = place[1] == 0
+            ahead, behind = place[0] < slc_count - 1, place[0] > 0
+            inside = jnp.where(line, behind, ahead), jnp.where(line, ahead, behind), None
+            power = sums[1:2, :]
+            for k in range(3):
+                weight = edge_weight(shade[k][...], shade_out[k][...])
+                if inside[k] is not None:
+                    weight = jnp.where(inside[k], weight, 0.0)
+                weights[k][...] = weight
+                power = power + put_flow(flows[k], weight, right[k][...], right_out[k][...])
+            total[...] = tile_rows([sums[0:1, :], power])
+
+        def put_flow(ref, weight, cells, outside):
+            flow = weight * (cells - outside)
+            ref[...] = flow
+            return row_sum(cells * flow)
+
+        def with_flows(cells, flows, place, frame):
+            low, high = place[1] == 0, place[1] != 0
+            line = lax.broadcasted_iota(jnp.int32, (lines, width), 0)
+            outer = line == jnp.where(place[1] == 0, lines - 1, 0)
+            both = flows[0][frame], flows[1][frame]
+            out = []
+            for z in range(slices):
+                layer = cells[z] + jnp.where(outer, flows[2][frame, z : z + 1, :], 0.0)
+                if z == 0:
+                    layer = layer + jnp.where(low, both[0], both[1])
+                if z == slices - 1:
+                    layer = layer + jnp.where(high, both[0], both[1])
+                out.append(layer)
+            return jnp.stack(out)
+
+        sums, *edges = call(
+            edge_kernel,
+            [sums, *facing(shade_faces), *shade_halo, *facing(right_faces), *right_halo],
+            [tile] + edge_shapes * 2,
+            "outer_image_of_right",
+        )
+        weights, flows = edges[:3], edges[3:]
 
         def target_rows(told):
             slot = lax.broadcasted_iota(jnp.int32, (owners, slots), 1)
@@ -358,19 +425,20 @@
                 rows += [row[:, :LANES], row[:, LANES:]]
             return tile_rows(rows)
 
-        def flux_kernel(shade, labels, strength, own, sums, slot_tile, *refs):
+        def flux_kernel(shade, labels, strength, own, flow0, flow1, flow2, sums, slot_tile, *refs):
             arrived, refs = refs[: pay1.count], refs[pay1.count :]
             pay, (image, weight, flux, right_in, targets) = refs[: pay2.count], refs[pay2.count :]
-            spares = target_rows(pay1.get_spare(arrived))
-            targets[...] = spares
-            columns = spares.T
+            place = whereabouts()
+            rows = target_rows(pay1.get_spare(arrived))
+            targets[...] = rows
+            columns = rows.T
             square, power = sums[0:1, :], sums[1:2, :]
             for t in range(frames):
-                part = to_blocks(own[t])
+                part = to_blocks(with_flows(own[t], (flow0, flow1, flow2), place, t))
                 if t > 0:
                     k = t - 1
                     came = jnp.concatenate([pay1.get(arrived, k), pay1.get(arrived, links + k)], axis=1)
-                    came = pick(landing_scatter(spares, k), came)
+                    came = pick(landing_scatter(rows, k), came)
                     weight_t = edge_weight(came[:, :LANES], to_blocks(shade[t]))
                     gap = to_blocks(right_of(labels[t], strength[t])) - came[:, LANES:]
                     flux_t = weight_t * gap
@@ -385,7 +453,7 @@
 
         *payload, part, weight, flux, right_in, targets = call(
             flux_kernel,
-            [intensity, labels, strength, own, sums, slot_tile, *received],
+            [intensity, labels, strength, own, *flows, sums, slot_tile, *received],
             pay2.shapes + [field, by_link, by_link, by_link, tile],
             "flux_of_right",
         )
@@ -393,7 +461,7 @@
 
         def residual_kernel(labels, strength, part, slot_tile, *refs):
             place = whereabouts()
-            arrived, (image, residual, scalars, up, side) = refs[: pay2.count], refs[pay2.count :]
+            arrived, (image, residual, scalars, *faces) = refs[: pay2.count], refs[pay2.count :]
             square, power = unpacked_sums(pay2.get_spare(arrived), 2)
             step = square / power
             scalars[...] = tile_rows([jnp.broadcast_to(v, (1, LANES)) for v in (square, power, step)])
@@ -404,19 +472,15 @@
                     image_t = image_t - pick(scatter_matrix(columns[:, t : t + 1], slots), pay2.get(arrived, t))
                 store_cells(image, t, image_t)
                 store_cells(residual, t, to_blocks(right_of(labels[t], strength[t])) - step * image_t)
-                up[t] = residual[t, slices - 1]
-                for z in range(slices):
-                    row = residual[t, z]
-                    side[t, z : z + 1, :] = jnp.where(place[1] == 0, row[lines - 1 :], row[:1])
-
-        image, residual, scalars, up, side = call(
+                put_faces(faces, place, t, residual[t])
+
+        image, residual, scalars, *faces = call(
             residual_kernel,
             [labels, strength, part, slot_tile, *received],
-            [field, field, tile, face_z, face_y],
+            [field, field, tile] + edge_shapes,
             "first_residual",
         )
-        low = lax.ppermute(up, "slc", [(i, i + 1) for i in range(slc_count - 1)])
-        beside = lax.ppermute(side, "row", [(i, i + 1) for i in range(row_count - 1)])
+        halo = swap_faces(*faces)
 
         def inner_kernel(shade, labels, strength, residual, image, scalars, flux, right_in, weight, targets, *refs):
             arrived, refs = refs[: pay2.count], refs[pay2.count :]
@@ -425,11 +489,9 @@
             columns = rows.T
             step = scalars[2:3, :]
             norm = power = cross = jnp.zeros((1, LANES), F32)
-            none = jnp.zeros((lines, width), F32)
             for t in range(frames):
                 residual_t = residual[t]
-                edges = frame_edges(shade[t], none, none, none[:1], None, slc_count)
-                inner = diagonal_of(labels[t], strength[t]) * residual_t + frame_spatial(residual_t, none, none, none[:1], edges)
+                inner = diagonal_of(labels[t], strength[t]) * residual_t + inner_spatial(residual_t, inner_edges(shade[t]))
                 norm = norm + row_sum(residual_t * residual_t)
                 power = power + row_sum(residual_t * inner)
                 cross = cross + row_sum(residual_t * image[t])
@@ -451,50 +513,34 @@
             pay3.shapes + [field, tile],
             "inner_image_of_residual",
         )
-        def outer_kernel(residual, side, sums, outer_z, outer_y, low, beside, *refs):
-            pay, (flow_z, flow_y) = refs[pay3.count : 2 * pay3.count], refs[2 * pay3.count :]
-            pay[0][...] = refs[0][...]
-            norm, power, cross = sums[0:1], sums[1:2], sums[2:3]
-            for t in range(frames):
-                gap = residual[t, 0] - low[t]
-                flow = outer_z[t] * gap
-                flow_z[t] = flow
-                power = power + row_sum(flow * gap)
-            gap = side[...] - beside[...]
-            flow = outer_y[...] * gap
-            flow_y[...] = flow
-            power = power + row_sum(flow * gap)
-            pay3.put_spare(pay, packed_sums([norm, power, cross]))
-
-        *payload, flow_z, flow_y = call(
+        def outer_kernel(sums, *refs):
+            faces, outside, weights = (refs[k : k + 3] for k in (0, 3, 6))
+            rows, pay, flows = refs[9 : 9 + pay3.count], refs[9 + pay3.count : 9 + 2 * pay3.count], refs[-3:]
+            pay[0][...] = rows[0][...]
+            power = sums[1:2, :]
+            for k in range(3):
+                power = power + put_flow(flows[k], weights[k][...], faces[k][...], outside[k][...])
+            pay3.put_spare(pay, packed_sums([sums[0:1, :], power, sums[2:3, :]]))
+
+        *payload, flow0, flow1, flow2 = call(
             outer_kernel,
-            [residual, side, sums, outer_z, outer_y, low, beside, *payload],
-            pay3.shapes + [face_z, face_y],
+            [sums, *facing(faces), *halo, *weights, *payload],
+            pay3.shapes + edge_shapes,
             "outer_image_of_residual",
         )
         received = pay3.exchange(payload)
-        high_z = lax.ppermute(flow_z, "slc", [(i + 1, i) for i in range(slc_count - 1)])
-        high_y = lax.ppermute(flow_y, "row", [(i + 1, i) for i in range(row_count - 1)])
-
-        def final_kernel(labels, strength, residual, image, inner, flow_z, flow_y, high_z, high_y, slot_tile, scalars, *refs):
-            arrived, (solution_field, out) = refs[: pay3.count], refs[pay3.count :]
+
+        def final_kernel(labels, strength, residual, image, inner, flow0, flow1, flow2, slot_tile, scalars, *refs):
+            place = whereabouts()
+            arrived, (solution_out, residual_out, solution_field, out, done) = refs[: pay3.count], refs[pay3.count :]
+            copies = []
             norm, whole, cross = unpacked_sums(pay3.get_spare(arrived), 3)
             square, power, step = scalars[0:1, :1], scalars[1:2, :1], scalars[2:3, :1]
             turn = norm / square
             second = norm / (whole + 2.0 * turn * cross + turn * turn * power)
             columns = slot_tile[...].T
-            line = lax.broadcasted_iota(jnp.int32, (lines, width), 0)
             for t in range(frames):
-                turned = []
-                for z in range(slices):
-                    cells = inner[t, z] + jnp.where(line == 0, flow_y[t, z : z + 1, :], 0.0)
-                    cells = cells - jnp.where(line == lines - 1, high_y[t, z : z + 1, :], 0.0)
-                    if z == 0:
-                        cells = cells + flow_z[t]
-                    if z == slices - 1:
-                        cells = cells - high_z[t]
-                    turned.append(cells)
-                turned = to_blocks(jnp.stack(turned))
+                turned = to_blocks(with_flows(inner[t], (flow0, flow1, flow2), place, t))
                 if t < links:
                     turned = turned - pick(scatter_matrix(columns[:, t : t + 1], slots), pay3.get(arrived, t))
                 residual_t = to_blocks(residual[t])
@@ -503,13 +549,20 @@
                 turned = turned + turn * to_blocks(image[t])
                 store_cells(solution_field, t, step * right + second * direction)
                 store_cells(out, t, residual_t - second * turned)
+                for k, (held, target) in enumerate(((solution_field, solution_out), (out, residual_out))):
+                    copies.append(pltpu.make_async_copy(held.at[t], target.at[t], done.at[t, k]))
+                    copies[-1].start()
+            for copy in copies:
+                copy.wait()
 
         return tuple(
             call(
                 final_kernel,
-                [labels, strength, residual, image, inner, flow_z, flow_y, high_z, high_y, slot_tile, scalars, *received],
+                [labels, strength, residual, image, inner, flow0, flow1, flow2, slot_tile, scalars, *received],
                 [field, field],
                 "solution_and_residual",
+                far_outputs=True,
+                scratch=[pltpu.VMEM(field.shape, F32)] * 2 + [pltpu.SemaphoreType.DMA((frames, 2))],
             )
         )
 

time: 86.9 us -> 83.8 us (0.964)
  starting transfers between devices: 31 us -> 14.7 us
  blocking collectives: 29.4 us -> 45.3 us
  waiting for transfers between devices: 16.6 us -> 15.4 us
  Pallas kernels: 8.36 us -> 7.28 us
    all_to_all x1 -> x2, blocking collectives: 29.4 us -> 45.3 us  [exchange(): lax.all_to_all(packed, AXES, split_axis=0, concat_axis=0, tiled=True)]
    ppermute x10 -> x9, starting transfers between devices: 18.9 us -> 7.21 us  [the longest x3 5.8 us: swap_faces(): lax.ppermute(along, AXES, ring)]
    all_to_all x2 -> x1, starting transfers between devices: 12 us -> 7.53 us  [exchange(): lax.all_to_all(packed, AXES, split_axis=0, concat_axis=0, tiled=True)]
    ppermute x10 -> x9, waiting for transfers between devices: 9.88 us -> 8.35 us  [the longest x3 6.77 us: swap_faces(): lax.ppermute(against, AXES, [(j, i) for i, j in ring])]
    pallas_call x7 -> x8, Pallas kernels: 8.36 us -> 7.28 us  [call(): pl.pallas_call(kernel, out_shape=outputs, in_specs=[away if far else near...]
    all_to_all x2 -> x1, waiting for transfers between devices: 6.75 us -> 7.01 us  [exchange(): lax.all_to_all(packed, AXES, split_axis=0, concat_axis=0, tiled=True)]
  transfers between devices with their start and end apart: 12 -> 10, of which waited for: 7 -> 7; matrix products, arithmetic and copies ran while one was open for 0% -> 0% of each run, Pallas kernels for 2% -> 2%
where the time goes in v4:
time: 83.8 us; the launch traced here: 83.5 us
  blocking collectives  45.3 us (54%)
  waiting for transfers between devices  15.4 us (18%)
  starting transfers between devices  14.7 us (18%)
  Pallas kernels  7.28 us (9%)
    all_to_all x2, blocking collectives, exchange(): lax.all_to_all(packed, AXES, split_axis=0, concat_axis=0, tiled=True)  45.3 us
    all_to_all x1, starting transfers between devices, exchange(): lax.all_to_all(packed, AXES, split_axis=0, concat_axis=0, tiled=True)  7.53 us
    pallas_call x8, Pallas kernels, call(): pl.pallas_call(kernel, out_shape=outputs, in_specs=[away if far else near...  7.28 us
    all_to_all x1, waiting for transfers between devices, exchange(): lax.all_to_all(packed, AXES, split_axis=0, concat_axis=0, tiled=True)  7.01 us
    ppermute x3, waiting for transfers between devices, swap_faces(): lax.ppermute(against, AXES, [(j, i) for i, j in ring])  6.77 us
    ppermute x3, starting transfers between devices, swap_faces(): lax.ppermute(along, AXES, ring)  5.8 us
  transfers between devices with their start and end apart: 10, of which 7 were waited for; matrix products, arithmetic and copies ran while one was open for 0% of the time, Pallas kernels for 2%

profile of v4, /device:TPU:0, one launch (start us, length us, event | category | flops | bytes accessed | tf_op | source)
XLA Modules:
  0.0 83.5 jit_solution(15970707831305531809)
XLA Ops:
  0.6 2.9 %send_blocks.1 = (f32[1552,128]{1,0:T(8,128)}, f32[8,128]{1,0:T(8,128)}, f32[4,8,512]{2,1,0:T(8,128)}, f32[4,8,512]{2,1,0:T(8,128)}, f32[4,4,512]{2,1,0:T(4,128)...) custom-call(s32[3,4,4,8]{3,2,1,0:T(4,128)} %bitcast.14, f32[4,4,8,512]{3,2,1,0:T(8,128)} %shade.5, ...), custom_call_target="tpu_custom_call" | custom-call | tf_op jit(solution)/shard_map/send_blocks/pallas_call | solution.py:141
  3.5 0.0 copy-start.7
  3.5 0.0 copy-start.4
  3.5 0.0 copy-start.3
  3.5 0.0 copy-start.6
  3.5 0.0 copy-start.5
  3.6 0.0 copy-start.8
  3.6 0.0 copy-start
  3.6 0.0 copy-start.1
  3.6 0.0 copy-start.2
  3.6 7.5 %all-to-all-start = ((f32[16,97,1,128]{3,2,1,0:T(1,128)}), f32[16,97,1,128]{3,2,1,0:T(1,128)S(1)}, u32[]{:S(2)}, u32[]{:S(2)}) async-start(f32[16,97,1,128]{3,2,1,0:T(1,128)} %bitcast.13), calls=%async_computation | async-start | bytes 1589248 | tf_op jit(solution)/shard_map/all_to_all | solution.py:131
  11.1 0.0 copy-done.7
  11.2 0.5 collective-permute-start.2
  11.6 0.0 copy-done.4
  11.6 0.1 collective-permute-start.1
  11.7 0.0 copy-done.3
  11.7 1.9 %collective-permute-start = (f32[4,8,512]{2,1,0:T(8,128)S(1)}, f32[4,8,512]{2,1,0:T(8,128)S(1)}, u32[]{:S(2)}, u32[]{:S(2)}) collective-permute-start(f32[4,8,512]{2,1,0:T(8,128)S(1)} %copy-done.3), channel_id=1, source_target_pairs={{0,2},{2,4},{4,6},{6,8},{8,10},{10,12},{12,14},{14,15},{3,1},{5,3}... | collective-permute-start | bytes 196616 | tf_op jit(solution)/shard_map/ppermute | solution.py:266
  13.7 0.0 copy-done.6
  13.7 0.0 collective-permute-start.4
  13.7 0.0 copy-done.5
  13.7 2.6 %collective-permute-start.3 = (f32[4,8,512]{2,1,0:T(8,128)S(1)}, f32[4,8,512]{2,1,0:T(8,128)S(1)}, u32[]{:S(2)}, u32[]{:S(2)}) collective-permute-start(f32[4,8,512]{2,1,0:T(8,128)S(1)} %copy-done.5), channel_id=1, source_target_pairs={{0,2},{2,4},{4,6},{6,8},{8,10},{10,12},{12,14},{14,15},{3,1},{5,3}... | collective-permute-start | bytes 196616 | tf_op jit(solution)/shard_map/ppermute | solution.py:266
  16.3 0.0 collective-permute-done.2.refs_5_
  16.3 0.0 copy-done.8
  16.3 0.0 collective-permute-start.5
  16.3 0.0 copy-done
  16.3 0.0 copy-done.1
  16.3 0.0 copy-done.2
  16.3 0.4 inner_image_of_right.1
  16.8 0.7 collective-permute-done.5.refs_11_
  17.5 3.7 %collective-permute-done.1.refs_4_ = f32[4,8,512]{2,1,0:T(8,128)S(1)} collective-permute-done((f32[4,8,512]{2,1,0:T(8,128)S(1)}, f32[4,8,512]{2,1,0:T(8,128)S(1)}, u32[]{:S(2)}, u32[]{:S(2)}) %collective-permute-start.1) | collective-permute-done | bytes 65568 | tf_op jit(solution)/shard_map/ppermute | solution.py:267
  21.2 0.0 collective-permute-done.refs_3_
  21.2 1.6 %collective-permute-done.4.refs_10_ = f32[4,8,512]{2,1,0:T(8,128)S(1)} collective-permute-done((f32[4,8,512]{2,1,0:T(8,128)S(1)}, f32[4,8,512]{2,1,0:T(8,128)S(1)}, u32[]{:S(2)}, u32[]{:S(2)}) %collective-permute-start.4) | collective-permute-done | bytes 65568 | tf_op jit(solution)/shard_map/ppermute | solution.py:267
  22.9 0.0 collective-permute-done.3.refs_9_
  22.9 0.1 outer_image_of_right.1
  23.0 7.0 %all-to-all-done = f32[16,97,1,128]{3,2,1,0:T(1,128)S(1)} async-done(((f32[16,97,1,128]{3,2,1,0:T(1,128)}), f32[16,97,1,128]{3,2,1,0:T(1,128)S(1)}, u32[]{:S(2)}, u32[]{:S(2)}) %all-to-all-start) | async-done | bytes 794656 | tf_op jit(solution)/shard_map/all_to_all | solution.py:131
  30.0 1.4 %flux_of_right.1 = (f32[1552,128]{1,0:T(8,128)S(1)}, f32[4,4,8,512]{3,2,1,0:T(8,128)S(1)}, f32[3,128,128]{2,1,0:T(8,128)S(1)}, f32[3,128,128]{2,1,0:T(8,128)S(1)...) custom-call(f32[4,4,8,512]{3,2,1,0:T(8,128)S(1)} %copy-done.2, s32[4,4,8,512]{3,2,1,0:T(8,128)S(1)} %copy-done, ...), custom_call_target="tpu_custom_call" | custom-call | tf_op jit(solution)/shard_map/flux_of_right/pallas_call | solution.py:141
  31.4 28.3 %all_to_all.15 = f32[16,97,1,128]{3,2,1,0:T(1,128)S(1)} all-to-all(f32[16,97,1,128]{3,2,1,0:T(1,128)S(1)} %bitcast.11), channel_id=1, replica_groups=mesh['grp'=2,'slc'=8,'row'=2] {'slc','row'}, dimensions={0} | all-to-all | bytes 1589248 | tf_op jit(solution)/shard_map/all_to_all | solution.py:131
  59.7 0.4 first_residual.1
  60.1 0.8 collective-permute-start.7
  60.9 1.3 %collective-permute-start.6 = (f32[4,8,512]{2,1,0:T(8,128)S(1)}, f32[4,8,512]{2,1,0:T(8,128)S(1)}, u32[]{:S(2)}, u32[]{:S(2)}) collective-permute-start(f32[4,8,512]{2,1,0:T(8,128)S(1)} %get-tuple-element.66.refs_1_), channel_id=1, source_target_pairs={{0,2},{2,4},{4,6},{6,8},{8,10},{10,12},{12,14},{14,15},{3,1},{5,3}... | collective-permute-start | bytes 196616 | tf_op jit(solution)/shard_map/ppermute | solution.py:266
  62.2 0.0 collective-permute-start.8
  62.2 0.8 inner_image_of_residual.1
  62.9 0.4 collective-permute-done.8.refs_5_
  63.4 1.4 %collective-permute-done.7.refs_4_ = f32[4,8,512]{2,1,0:T(8,128)S(1)} collective-permute-done((f32[4,8,512]{2,1,0:T(8,128)S(1)}, f32[4,8,512]{2,1,0:T(8,128)S(1)}, u32[]{:S(2)}, u32[]{:S(2)}) %collective-permute-start.7) | collective-permute-done | bytes 65568 | tf_op jit(solution)/shard_map/ppermute | solution.py:267
  64.8 0.4 collective-permute-done.6.refs_3_
  65.2 0.1 outer_image_of_residual.1
  65.3 17.0 %all_to_all.16 = f32[16,49,1,128]{3,2,1,0:T(1,128)S(1)} all-to-all(f32[16,49,1,128]{3,2,1,0:T(1,128)S(1)} %bitcast.12), channel_id=1, replica_groups=mesh['grp'=2,'slc'=8,'row'=2] {'slc','row'}, dimensions={0} | all-to-all | bytes 802816 | tf_op jit(solution)/shard_map/all_to_all | solution.py:131
  82.3 1.2 %solution_and_residual.1 = (f32[4,4,8,512]{3,2,1,0:T(8,128)}, f32[4,4,8,512]{3,2,1,0:T(8,128)}) custom-call(s32[4,4,8,512]{3,2,1,0:T(8,128)S(1)} %copy-done, f32[4,4,8,512]{3,2,1,0:T(8,128)S(1)} %copy-done.1, f32[4,4,8,512]{3,2,1,0:T(8,128)S(1)} %get-tuple-element.56.residual, f32[4,4,8,512]{3,2,1,0:T(8,128)S(1)} %get-tuple-element.57.image, ...), custom_call_target="tpu_custom_call" | custom-call | tf_op jit(solution)/shard_map/solution_and_residual/pallas_call | solution.py:141
  (2 shorter events, 0.0 us)
Async XLA Ops:
  3.5 7.6 %copy-start.7 = (f32[4,4,512]{2,1,0:T(4,128)S(1)}, f32[4,4,512]{2,1,0:T(4,128)}, u32[]{:S(2)}) copy-start(f32[4,4,512]{2,1,0:T(4,128)} %get-tuple-element.44.refs_2_) | copy-start | bytes 98308
  3.5 8.1 %copy-start.4 = (f32[4,8,512]{2,1,0:T(8,128)S(1)}, f32[4,8,512]{2,1,0:T(8,128)}, u32[]{:S(2)}) copy-start(f32[4,8,512]{2,1,0:T(8,128)} %get-tuple-element.42.refs_0_) | copy-start | bytes 196612
  3.5 8.2 %copy-start.3 = (f32[4,8,512]{2,1,0:T(8,128)S(1)}, f32[4,8,512]{2,1,0:T(8,128)}, u32[]{:S(2)}) copy-start(f32[4,8,512]{2,1,0:T(8,128)} %get-tuple-element.43.refs_1_) | copy-start | bytes 196612
  3.5 10.1 %copy-start.6 = (f32[4,8,512]{2,1,0:T(8,128)S(1)}, f32[4,8,512]{2,1,0:T(8,128)}, u32[]{:S(2)}) copy-start(f32[4,8,512]{2,1,0:T(8,128)} %get-tuple-element.45.refs_6_) | copy-start | bytes 196612
  3.5 10.1 %copy-start.5 = (f32[4,8,512]{2,1,0:T(8,128)S(1)}, f32[4,8,512]{2,1,0:T(8,128)}, u32[]{:S(2)}) copy-start(f32[4,8,512]{2,1,0:T(8,128)} %get-tuple-element.46.refs_7_) | copy-start | bytes 196612
  3.6 12.7 %copy-start.8 = (f32[4,4,512]{2,1,0:T(4,128)S(1)}, f32[4,4,512]{2,1,0:T(4,128)}, u32[]{:S(2)}) copy-start(f32[4,4,512]{2,1,0:T(4,128)} %get-tuple-element.47.refs_8_) | copy-start | bytes 98308
  3.6 12.7 %copy-start = (s32[4,4,8,512]{3,2,1,0:T(8,128)S(1)}, s32[4,4,8,512]{3,2,1,0:T(8,128)}, u32[]{:S(2)}) copy-start(s32[4,4,8,512]{3,2,1,0:T(8,128)} %labels.9) | copy-start | bytes 786436
  3.6 12.7 %copy-start.1 = (f32[4,4,8,512]{3,2,1,0:T(8,128)S(1)}, f32[4,4,8,512]{3,2,1,0:T(8,128)}, u32[]{:S(2)}) copy-start(f32[4,4,8,512]{3,2,1,0:T(8,128)} %strength.9) | copy-start | bytes 786436
  3.6 12.7 %copy-start.2 = (f32[4,4,8,512]{3,2,1,0:T(8,128)S(1)}, f32[4,4,8,512]{3,2,1,0:T(8,128)}, u32[]{:S(2)}) copy-start(f32[4,4,8,512]{3,2,1,0:T(8,128)} %shade.5) | copy-start | bytes 786436
  3.6 26.4 %all-to-all-start = ((f32[16,97,1,128]{3,2,1,0:T(1,128)}), f32[16,97,1,128]{3,2,1,0:T(1,128)S(1)}, u32[]{:S(2)}, u32[]{:S(2)}) async-start(f32[16,97,1,128]{3,2,1,0:T(1,128)} %bitcast.13), calls=%async_computation | async-start | bytes 1589248 | tf_op jit(solution)/shard_map/all_to_all | solution.py:131
  11.2 5.1 %collective-permute-start.2 = (f32[4,4,512]{2,1,0:T(4,128)S(1)}, f32[4,4,512]{2,1,0:T(4,128)S(1)}, u32[]{:S(2)}, u32[]{:S(2)}) collective-permute-start(f32[4,4,512]{2,1,0:T(4,128)S(1)} %copy-done.7), channel_id=1, source_target_pairs={{0,1},{1,0},{2,3},{3,2},{4,5},{5,4},{6,7},{7,6},{8,9},{9,8},{10,11... | collective-permute-start | bytes 98312 | tf_op jit(solution)/shard_map/ppermute | solution.py:268
  11.6 9.6 %collective-permute-start.1 = (f32[4,8,512]{2,1,0:T(8,128)S(1)}, f32[4,8,512]{2,1,0:T(8,128)S(1)}, u32[]{:S(2)}, u32[]{:S(2)}) collective-permute-start(f32[4,8,512]{2,1,0:T(8,128)S(1)} %copy-done.4), channel_id=1, source_target_pairs={{2,0},{4,2},{6,4},{8,6},{10,8},{12,10},{14,12},{15,14},{1,3},{3,5}... | collective-permute-start | bytes 196616 | tf_op jit(solution)/shard_map/ppermute | solution.py:267
  11.7 4.6 %copy-start.9 = (f32[8,128]{1,0:T(8,128)S(1)}, f32[8,128]{1,0:T(8,128)}, u32[]{:S(2)}) copy-start(f32[8,128]{1,0:T(8,128)} %get-tuple-element.39.slot_tile) | copy-start | bytes 12292
  11.7 9.5 %collective-permute-start = (f32[4,8,512]{2,1,0:T(8,128)S(1)}, f32[4,8,512]{2,1,0:T(8,128)S(1)}, u32[]{:S(2)}, u32[]{:S(2)}) collective-permute-start(f32[4,8,512]{2,1,0:T(8,128)S(1)} %copy-done.3), channel_id=1, source_target_pairs={{0,2},{2,4},{4,6},{6,8},{8,10},{10,12},{12,14},{14,15},{3,1},{5,3}... | collective-permute-start | bytes 196616 | tf_op jit(solution)/shard_map/ppermute | solution.py:266
  13.7 9.2 %collective-permute-start.4 = (f32[4,8,512]{2,1,0:T(8,128)S(1)}, f32[4,8,512]{2,1,0:T(8,128)S(1)}, u32[]{:S(2)}, u32[]{:S(2)}) collective-permute-start(f32[4,8,512]{2,1,0:T(8,128)S(1)} %copy-done.6), channel_id=1, source_target_pairs={{2,0},{4,2},{6,4},{8,6},{10,8},{12,10},{14,12},{15,14},{1,3},{3,5}... | collective-permute-start | bytes 196616 | tf_op jit(solution)/shard_map/ppermute | solution.py:267
  13.7 9.2 %collective-permute-start.3 = (f32[4,8,512]{2,1,0:T(8,128)S(1)}, f32[4,8,512]{2,1,0:T(8,128)S(1)}, u32[]{:S(2)}, u32[]{:S(2)}) collective-permute-start(f32[4,8,512]{2,1,0:T(8,128)S(1)} %copy-done.5), channel_id=1, source_target_pairs={{0,2},{2,4},{4,6},{6,8},{8,10},{10,12},{12,14},{14,15},{3,1},{5,3}... | collective-permute-start | bytes 196616 | tf_op jit(solution)/shard_map/ppermute | solution.py:266
  16.3 1.2 %collective-permute-start.5 = (f32[4,4,512]{2,1,0:T(4,128)S(1)}, f32[4,4,512]{2,1,0:T(4,128)S(1)}, u32[]{:S(2)}, u32[]{:S(2)}) collective-permute-start(f32[4,4,512]{2,1,0:T(4,128)S(1)} %copy-done.8), channel_id=1, source_target_pairs={{0,1},{1,0},{2,3},{3,2},{4,5},{5,4},{6,7},{7,6},{8,9},{9,8},{10,11... | collective-permute-start | bytes 98312 | tf_op jit(solution)/shard_map/ppermute | solution.py:268
  60.1 4.7 %collective-permute-start.7 = (f32[4,8,512]{2,1,0:T(8,128)S(1)}, f32[4,8,512]{2,1,0:T(8,128)S(1)}, u32[]{:S(2)}, u32[]{:S(2)}) collective-permute-start(f32[4,8,512]{2,1,0:T(8,128)S(1)} %get-tuple-element.65.refs_0_), channel_id=1, source_target_pairs={{2,0},{4,2},{6,4},{8,6},{10,8},{12,10},{14,12},{15,14},{1,3},{3,5}... | collective-permute-start | bytes 196616 | tf_op jit(solution)/shard_map/ppermute | solution.py:267
  60.9 4.3 %collective-permute-start.6 = (f32[4,8,512]{2,1,0:T(8,128)S(1)}, f32[4,8,512]{2,1,0:T(8,128)S(1)}, u32[]{:S(2)}, u32[]{:S(2)}) collective-permute-start(f32[4,8,512]{2,1,0:T(8,128)S(1)} %get-tuple-element.66.refs_1_), channel_id=1, source_target_pairs={{0,2},{2,4},{4,6},{6,8},{8,10},{10,12},{12,14},{14,15},{3,1},{5,3}... | collective-permute-start | bytes 196616 | tf_op jit(solution)/shard_map/ppermute | solution.py:266
  62.2 1.2 %collective-permute-start.8 = (f32[4,4,512]{2,1,0:T(4,128)S(1)}, f32[4,4,512]{2,1,0:T(4,128)S(1)}, u32[]{:S(2)}, u32[]{:S(2)}) collective-permute-start(f32[4,4,512]{2,1,0:T(4,128)S(1)} %get-tuple-element.67.refs_2_), channel_id=1, source_target_pairs={{0,1},{1,0},{2,3},{3,2},{4,5},{5,4},{6,7},{7,6},{8,9},{9,8},{10,11... | collective-permute-start | bytes 98312 | tf_op jit(solution)/shard_map/ppermute | solution.py:268

commit v5 on v4

--- a/solution.py
+++ b/solution.py
@@ -368,22 +368,6 @@
 
         edge_shapes = [face_z, face_z, face_y]
 
-        def edge_kernel(sums, *refs):
-            shade, shade_out, right, right_out = (refs[k : k + 3] for k in (0, 3, 6, 9))
-            total, weights, flows = refs[12], refs[13:16], refs[16:]
-            place = whereabouts()
-            line = place[1] == 0
-            ahead, behind = place[0] < slc_count - 1, place[0] > 0
-            inside = jnp.where(line, behind, ahead), jnp.where(line, ahead, behind), None
-            power = sums[1:2, :]
-            for k in range(3):
-                weight = edge_weight(shade[k][...], shade_out[k][...])
-                if inside[k] is not None:
-                    weight = jnp.where(inside[k], weight, 0.0)
-                weights[k][...] = weight
-                power = power + put_flow(flows[k], weight, right[k][...], right_out[k][...])
-            total[...] = tile_rows([sums[0:1, :], power])
-
         def put_flow(ref, weight, cells, outside):
             flow = weight * (cells - outside)
             ref[...] = flow
@@ -404,14 +388,6 @@
                 out.append(layer)
             return jnp.stack(out)
 
-        sums, *edges = call(
-            edge_kernel,
-            [sums, *facing(shade_faces), *shade_halo, *facing(right_faces), *right_halo],
-            [tile] + edge_shapes * 2,
-            "outer_image_of_right",
-        )
-        weights, flows = edges[:3], edges[3:]
-
         def target_rows(told):
             slot = lax.broadcasted_iota(jnp.int32, (owners, slots), 1)
             source = lax.broadcasted_iota(jnp.int32, (owners, slots), 0)
@@ -425,38 +401,65 @@
                 rows += [row[:, :LANES], row[:, LANES:]]
             return tile_rows(rows)
 
-        def flux_kernel(shade, labels, strength, own, flow0, flow1, flow2, sums, slot_tile, *refs):
+        def flux_kernel(shade, labels, strength, *refs):
             arrived, refs = refs[: pay1.count], refs[pay1.count :]
-            pay, (image, weight, flux, right_in, targets) = refs[: pay2.count], refs[pay2.count :]
-            place = whereabouts()
+            pay, (weight, flux, right_in, targets, joined) = refs[: pay2.count], refs[pay2.count :]
             rows = target_rows(pay1.get_spare(arrived))
             targets[...] = rows
             columns = rows.T
-            square, power = sums[0:1, :], sums[1:2, :]
+            power = jnp.zeros((1, LANES), F32)
+            for k in range(links):
+                t = k + 1
+                came = jnp.concatenate([pay1.get(arrived, k), pay1.get(arrived, links + k)], axis=1)
+                came = pick(landing_scatter(rows, k), came)
+                weight_t = edge_weight(came[:, :LANES], to_blocks(shade[t]))
+                gap = to_blocks(right_of(labels[t], strength[t])) - came[:, LANES:]
+                flux_t = weight_t * gap
+                power = power + row_sum(flux_t * gap)
+                weight[k], flux[k], right_in[k] = weight_t, flux_t, came[:, LANES:]
+                pay2.put(pay, k, pick(landing_gather(columns, k), flux_t))
+            joined[...] = tile_rows([power])
+
+        *payload, weight, flux, right_in, targets, joined = call(
+            flux_kernel,
+            [intensity, labels, strength, *received],
+            pay2.shapes + [by_link, by_link, by_link, tile, tile],
+            "flux_of_right",
+        )
+
+        def part_kernel(own, sums, joined, slot_tile, flux, *refs):
+            shade, shade_out, right, right_out = (refs[k : k + 3] for k in (0, 3, 6, 9))
+            rows, refs = refs[12 : 12 + pay2.count], refs[12 + pay2.count :]
+            pay, (image, *weights), flows = refs[: pay2.count], refs[pay2.count : pay2.count + 4], refs[pay2.count + 4 :]
+            place = whereabouts()
+            line = place[1] == 0
+            ahead, behind = place[0] < slc_count - 1, place[0] > 0
+            inside = jnp.where(line, behind, ahead), jnp.where(line, ahead, behind), None
+            power = sums[1:2, :] + joined[0:1, :]
+            for k in range(3):
+                weight = edge_weight(shade[k][...], shade_out[k][...])
+                if inside[k] is not None:
+                    weight = jnp.where(inside[k], weight, 0.0)
+                weights[k][...] = weight
+                power = power + put_flow(flows[k], weight, right[k][...], right_out[k][...])
+            pay[0][...] = rows[0][...]
             for t in range(frames):
-                part = to_blocks(with_flows(own[t], (flow0, flow1, flow2), place, t))
+                part = to_blocks(with_flows(own[t], flows, place, t))
                 if t > 0:
-                    k = t - 1
-                    came = jnp.concatenate([pay1.get(arrived, k), pay1.get(arrived, links + k)], axis=1)
-                    came = pick(landing_scatter(rows, k), came)
-                    weight_t = edge_weight(came[:, :LANES], to_blocks(shade[t]))
-                    gap = to_blocks(right_of(labels[t], strength[t])) - came[:, LANES:]
-                    flux_t = weight_t * gap
-                    power = power + row_sum(flux_t * gap)
-                    part = part + flux_t
-                    weight[k], flux[k], right_in[k] = weight_t, flux_t, came[:, LANES:]
-                    pay2.put(pay, k, pick(landing_gather(columns, k), flux_t))
+                    part = part + flux[t - 1]
                 if t < links:
                     pay2.put(pay, links + t, pick(gather_matrix(slot_tile[t : t + 1], slots), part))
                 store_cells(image, t, part)
-            pay2.put_spare(pay, packed_sums([square, power]))
-
-        *payload, part, weight, flux, right_in, targets = call(
-            flux_kernel,
-            [intensity, labels, strength, own, *flows, sums, slot_tile, *received],
-            pay2.shapes + [field, by_link, by_link, by_link, tile],
-            "flux_of_right",
-        )
+            pay2.put_spare(pay, packed_sums([sums[0:1, :], power]))
+
+        *payload, part, weight0, weight1, weight2 = call(
+            part_kernel,
+            [own, sums, joined, slot_tile, flux, *facing(shade_faces), *shade_halo, *facing(right_faces), *right_halo, *payload],
+            pay2.shapes + [field] + edge_shapes,
+            "image_of_right",
+            scratch=[pltpu.VMEM(leaf.shape, F32) for leaf in edge_shapes],
+        )
+        weights = weight0, weight1, weight2
         received = pay2.exchange(payload)
 
         def residual_kernel(labels, strength, part, slot_tile, *refs):

time: 83.8 us -> 82.7 us (0.987)
  blocking collectives: 45.3 us -> 43.8 us
    all_to_all x1, waiting for transfers between devices: 7.01 us -> 13.2 us  [exchange(): lax.all_to_all(packed, AXES, split_axis=0, concat_axis=0, tiled=True)]
    ppermute x3, waiting for transfers between devices: 6.77 us -> 1.39 us  [swap_faces(): lax.ppermute(against, AXES, [(j, i) for i, j in ring])]
    all_to_all x2, blocking collectives: 45.3 us -> 43.8 us  [exchange(): lax.all_to_all(packed, AXES, split_axis=0, concat_axis=0, tiled=True)]
  transfers between devices with their start and end apart: 10 -> 10, of which waited for: 7 -> 4; matrix products, arithmetic and copies ran while one was open for 0% -> 0% of each run, Pallas kernels for 2% -> 3%
where the time goes in v5:
time: 82.7 us; the launch traced here: 82.4 us
  blocking collectives  43.8 us (53%)
  waiting for transfers between devices  15.4 us (19%)
  starting transfers between devices  14.7 us (18%)
  Pallas kernels  7.52 us (9%)
  between operations  0.84 us (1%)
    all_to_all x2, blocking collectives, exchange(): lax.all_to_all(packed, AXES, split_axis=0, concat_axis=0, tiled=True)  43.8 us
    all_to_all x1, waiting for transfers between devices, exchange(): lax.all_to_all(packed, AXES, split_axis=0, concat_axis=0, tiled=True)  13.2 us
    all_to_all x1, starting transfers between devices, exchange(): lax.all_to_all(packed, AXES, split_axis=0, concat_axis=0, tiled=True)  7.53 us
    pallas_call x8, Pallas kernels, call(): pl.pallas_call(kernel, out_shape=outputs, in_specs=[away if far else near...  7.52 us
    ppermute x3, starting transfers between devices, swap_faces(): lax.ppermute(along, AXES, ring)  5.79 us
  transfers between devices with their start and end apart: 10, of which 4 were waited for; matrix products, arithmetic and copies ran while one was open for 0% of the time, Pallas kernels for 3%

profile of v5, /device:TPU:0, one launch (start us, length us, event | category | flops | bytes accessed | tf_op | source)
XLA Modules:
  0.0 82.4 jit_solution(15028838375946383372)
XLA Ops:
  0.6 2.9 %send_blocks.1 = (f32[1552,128]{1,0:T(8,128)}, f32[8,128]{1,0:T(8,128)}, f32[4,8,512]{2,1,0:T(8,128)}, f32[4,8,512]{2,1,0:T(8,128)}, f32[4,4,512]{2,1,0:T(4,128)...) custom-call(s32[3,4,4,8]{3,2,1,0:T(4,128)} %bitcast.14, f32[4,4,8,512]{3,2,1,0:T(8,128)} %shade.5, ...), custom_call_target="tpu_custom_call" | custom-call | tf_op jit(solution)/shard_map/send_blocks/pallas_call | solution.py:141
  3.5 0.0 copy-start.7
  3.5 0.0 copy-start.4
  3.5 0.0 copy-start.3
  3.5 0.0 copy-start.6
  3.5 0.0 copy-start.5
  3.6 0.0 copy-start.8
  3.6 0.0 copy-start
  3.6 0.0 copy-start.1
  3.6 0.0 copy-start.2
  3.6 7.5 %all-to-all-start = ((f32[16,97,1,128]{3,2,1,0:T(1,128)}), f32[16,97,1,128]{3,2,1,0:T(1,128)S(1)}, u32[]{:S(2)}, u32[]{:S(2)}) async-start(f32[16,97,1,128]{3,2,1,0:T(1,128)} %bitcast.13), calls=%async_computation | async-start | bytes 1589248 | tf_op jit(solution)/shard_map/all_to_all | solution.py:131
  11.1 0.0 copy-done.7
  11.2 0.5 collective-permute-start.2
  11.6 0.0 copy-done.4
  11.6 0.1 collective-permute-start.1
  11.7 0.0 copy-done.3
  11.7 1.9 %collective-permute-start = (f32[4,8,512]{2,1,0:T(8,128)S(1)}, f32[4,8,512]{2,1,0:T(8,128)S(1)}, u32[]{:S(2)}, u32[]{:S(2)}) collective-permute-start(f32[4,8,512]{2,1,0:T(8,128)S(1)} %copy-done.3), channel_id=1, source_target_pairs={{0,2},{2,4},{4,6},{6,8},{8,10},{10,12},{12,14},{14,15},{3,1},{5,3}... | collective-permute-start | bytes 196616 | tf_op jit(solution)/shard_map/ppermute | solution.py:266
  13.7 0.0 copy-done.6
  13.7 0.0 collective-permute-start.4
  13.7 0.0 copy-done.5
  13.7 2.6 %collective-permute-start.3 = (f32[4,8,512]{2,1,0:T(8,128)S(1)}, f32[4,8,512]{2,1,0:T(8,128)S(1)}, u32[]{:S(2)}, u32[]{:S(2)}) collective-permute-start(f32[4,8,512]{2,1,0:T(8,128)S(1)} %copy-done.5), channel_id=1, source_target_pairs={{0,2},{2,4},{4,6},{6,8},{8,10},{10,12},{12,14},{14,15},{3,1},{5,3}... | collective-permute-start | bytes 196616 | tf_op jit(solution)/shard_map/ppermute | solution.py:266
  16.3 0.0 collective-permute-done.2.refs_5_
  16.3 0.0 copy-done.8
  16.3 0.0 collective-permute-start.5
  16.3 0.0 copy-done
  16.3 0.0 copy-done.1
  16.3 0.0 copy-done.2
  16.3 0.4 inner_image_of_right.1
  16.8 13.2 %all-to-all-done = f32[16,97,1,128]{3,2,1,0:T(1,128)S(1)} async-done(((f32[16,97,1,128]{3,2,1,0:T(1,128)}), f32[16,97,1,128]{3,2,1,0:T(1,128)S(1)}, u32[]{:S(2)}, u32[]{:S(2)}) %all-to-all-start) | async-done | bytes 794656 | tf_op jit(solution)/shard_map/all_to_all | solution.py:131
  30.0 1.3 %flux_of_right.1 = (f32[1552,128]{1,0:T(8,128)S(1)}, f32[3,128,128]{2,1,0:T(8,128)S(1)}, f32[3,128,128]{2,1,0:T(8,128)S(1)}, f32[3,128,128]{2,1,0:T(8,128)S(1)},...) custom-call(f32[4,4,8,512]{3,2,1,0:T(8,128)S(1)} %copy-done.2, s32[4,4,8,512]{3,2,1,0:T(8,128)S(1)} %copy-done, ...), custom_call_target="tpu_custom_call" | custom-call | tf_op jit(solution)/shard_map/flux_of_right/pallas_call | solution.py:141
  31.3 0.0 collective-permute-done.5.refs_11_
  31.3 0.0 collective-permute-done.1.refs_4_
  31.3 0.0 collective-permute-done.refs_3_
  31.4 0.0 collective-permute-done.4.refs_10_
  31.4 0.0 collective-permute-done.3.refs_9_
  31.4 0.4 image_of_right.1
  31.8 26.8 %all_to_all.15 = f32[16,97,1,128]{3,2,1,0:T(1,128)S(1)} all-to-all(f32[16,97,1,128]{3,2,1,0:T(1,128)S(1)} %bitcast.11), channel_id=1, replica_groups=mesh['grp'=2,'slc'=8,'row'=2] {'slc','row'}, dimensions={0} | all-to-all | bytes 1589248 | tf_op jit(solution)/shard_map/all_to_all | solution.py:131
  58.5 0.4 first_residual.1
  58.9 0.8 %collective-permute-start.7 = (f32[4,8,512]{2,1,0:T(8,128)S(1)}, f32[4,8,512]{2,1,0:T(8,128)S(1)}, u32[]{:S(2)}, u32[]{:S(2)}) collective-permute-start(f32[4,8,512]{2,1,0:T(8,128)S(1)} %get-tuple-element.61.refs_0_), channel_id=1, source_target_pairs={{2,0},{4,2},{6,4},{8,6},{10,8},{12,10},{14,12},{15,14},{1,3},{3,5}... | collective-permute-start | bytes 196616 | tf_op jit(solution)/shard_map/ppermute | solution.py:267
  59.8 1.3 %collective-permute-start.6 = (f32[4,8,512]{2,1,0:T(8,128)S(1)}, f32[4,8,512]{2,1,0:T(8,128)S(1)}, u32[]{:S(2)}, u32[]{:S(2)}) collective-permute-start(f32[4,8,512]{2,1,0:T(8,128)S(1)} %get-tuple-element.62.refs_1_), channel_id=1, source_target_pairs={{0,2},{2,4},{4,6},{6,8},{8,10},{10,12},{12,14},{14,15},{3,1},{5,3}... | collective-permute-start | bytes 196616 | tf_op jit(solution)/shard_map/ppermute | solution.py:266
  61.0 0.0 collective-permute-start.8
  61.0 0.8 inner_image_of_residual.1
  61.8 0.4 collective-permute-done.8.refs_5_
  62.2 1.4 %collective-permute-done.7.refs_4_ = f32[4,8,512]{2,1,0:T(8,128)S(1)} collective-permute-done((f32[4,8,512]{2,1,0:T(8,128)S(1)}, f32[4,8,512]{2,1,0:T(8,128)S(1)}, u32[]{:S(2)}, u32[]{:S(2)}) %collective-permute-start.7) | collective-permute-done | bytes 65568 | tf_op jit(solution)/shard_map/ppermute | solution.py:267
  63.6 0.4 collective-permute-done.6.refs_3_
  64.0 0.1 outer_image_of_residual.1
  64.2 17.0 %all_to_all.16 = f32[16,49,1,128]{3,2,1,0:T(1,128)S(1)} all-to-all(f32[16,49,1,128]{3,2,1,0:T(1,128)S(1)} %bitcast.12), channel_id=1, replica_groups=mesh['grp'=2,'slc'=8,'row'=2] {'slc','row'}, dimensions={0} | all-to-all | bytes 802816 | tf_op jit(solution)/shard_map/all_to_all | solution.py:131
  81.2 1.2 %solution_and_residual.1 = (f32[4,4,8,512]{3,2,1,0:T(8,128)}, f32[4,4,8,512]{3,2,1,0:T(8,128)}) custom-call(s32[4,4,8,512]{3,2,1,0:T(8,128)S(1)} %copy-done, f32[4,4,8,512]{3,2,1,0:T(8,128)S(1)} %copy-done.1, f32[4,4,8,512]{3,2,1,0:T(8,128)S(1)} %get-tuple-element.53.residual, f32[4,4,8,512]{3,2,1,0:T(8,128)S(1)} %get-tuple-element.54.image, ...), custom_call_target="tpu_custom_call" | custom-call | tf_op jit(solution)/shard_map/solution_and_residual/pallas_call | solution.py:141
  (2 shorter events, 0.0 us)
Async XLA Ops:
  3.5 7.6 %copy-start.7 = (f32[4,4,512]{2,1,0:T(4,128)S(1)}, f32[4,4,512]{2,1,0:T(4,128)}, u32[]{:S(2)}) copy-start(f32[4,4,512]{2,1,0:T(4,128)} %get-tuple-element.46.refs_2_) | copy-start | bytes 98308
  3.5 8.1 %copy-start.4 = (f32[4,8,512]{2,1,0:T(8,128)S(1)}, f32[4,8,512]{2,1,0:T(8,128)}, u32[]{:S(2)}) copy-start(f32[4,8,512]{2,1,0:T(8,128)} %get-tuple-element.44.refs_0_) | copy-start | bytes 196612
  3.5 8.2 %copy-start.3 = (f32[4,8,512]{2,1,0:T(8,128)S(1)}, f32[4,8,512]{2,1,0:T(8,128)}, u32[]{:S(2)}) copy-start(f32[4,8,512]{2,1,0:T(8,128)} %get-tuple-element.45.refs_1_) | copy-start | bytes 196612
  3.5 10.1 %copy-start.6 = (f32[4,8,512]{2,1,0:T(8,128)S(1)}, f32[4,8,512]{2,1,0:T(8,128)}, u32[]{:S(2)}) copy-start(f32[4,8,512]{2,1,0:T(8,128)} %get-tuple-element.47.refs_6_) | copy-start | bytes 196612
  3.5 10.1 %copy-start.5 = (f32[4,8,512]{2,1,0:T(8,128)S(1)}, f32[4,8,512]{2,1,0:T(8,128)}, u32[]{:S(2)}) copy-start(f32[4,8,512]{2,1,0:T(8,128)} %get-tuple-element.48.refs_7_) | copy-start | bytes 196612
  3.6 12.7 %copy-start.8 = (f32[4,4,512]{2,1,0:T(4,128)S(1)}, f32[4,4,512]{2,1,0:T(4,128)}, u32[]{:S(2)}) copy-start(f32[4,4,512]{2,1,0:T(4,128)} %get-tuple-element.49.refs_8_) | copy-start | bytes 98308
  3.6 12.7 %copy-start = (s32[4,4,8,512]{3,2,1,0:T(8,128)S(1)}, s32[4,4,8,512]{3,2,1,0:T(8,128)}, u32[]{:S(2)}) copy-start(s32[4,4,8,512]{3,2,1,0:T(8,128)} %labels.9) | copy-start | bytes 786436
  3.6 12.7 %copy-start.1 = (f32[4,4,8,512]{3,2,1,0:T(8,128)S(1)}, f32[4,4,8,512]{3,2,1,0:T(8,128)}, u32[]{:S(2)}) copy-start(f32[4,4,8,512]{3,2,1,0:T(8,128)} %strength.9) | copy-start | bytes 786436
  3.6 12.7 %copy-start.2 = (f32[4,4,8,512]{3,2,1,0:T(8,128)S(1)}, f32[4,4,8,512]{3,2,1,0:T(8,128)}, u32[]{:S(2)}) copy-start(f32[4,4,8,512]{3,2,1,0:T(8,128)} %shade.5) | copy-start | bytes 786436
  3.6 26.4 %all-to-all-start = ((f32[16,97,1,128]{3,2,1,0:T(1,128)}), f32[16,97,1,128]{3,2,1,0:T(1,128)S(1)}, u32[]{:S(2)}, u32[]{:S(2)}) async-start(f32[16,97,1,128]{3,2,1,0:T(1,128)} %bitcast.13), calls=%async_computation | async-start | bytes 1589248 | tf_op jit(solution)/shard_map/all_to_all | solution.py:131
  11.2 5.1 %collective-permute-start.2 = (f32[4,4,512]{2,1,0:T(4,128)S(1)}, f32[4,4,512]{2,1,0:T(4,128)S(1)}, u32[]{:S(2)}, u32[]{:S(2)}) collective-permute-start(f32[4,4,512]{2,1,0:T(4,128)S(1)} %copy-done.7), channel_id=1, source_target_pairs={{0,1},{1,0},{2,3},{3,2},{4,5},{5,4},{6,7},{7,6},{8,9},{9,8},{10,11... | collective-permute-start | bytes 98312 | tf_op jit(solution)/shard_map/ppermute | solution.py:268
  11.6 19.7 %collective-permute-start.1 = (f32[4,8,512]{2,1,0:T(8,128)S(1)}, f32[4,8,512]{2,1,0:T(8,128)S(1)}, u32[]{:S(2)}, u32[]{:S(2)}) collective-permute-start(f32[4,8,512]{2,1,0:T(8,128)S(1)} %copy-done.4), channel_id=1, source_target_pairs={{2,0},{4,2},{6,4},{8,6},{10,8},{12,10},{14,12},{15,14},{1,3},{3,5}... | collective-permute-start | bytes 196616 | tf_op jit(solution)/shard_map/ppermute | solution.py:267
  11.7 4.6 %copy-start.9 = (f32[8,128]{1,0:T(8,128)S(1)}, f32[8,128]{1,0:T(8,128)}, u32[]{:S(2)}) copy-start(f32[8,128]{1,0:T(8,128)} %get-tuple-element.37.slot_tile) | copy-start | bytes 12292
  11.7 19.6 %collective-permute-start = (f32[4,8,512]{2,1,0:T(8,128)S(1)}, f32[4,8,512]{2,1,0:T(8,128)S(1)}, u32[]{:S(2)}, u32[]{:S(2)}) collective-permute-start(f32[4,8,512]{2,1,0:T(8,128)S(1)} %copy-done.3), channel_id=1, source_target_pairs={{0,2},{2,4},{4,6},{6,8},{8,10},{10,12},{12,14},{14,15},{3,1},{5,3}... | collective-permute-start | bytes 196616 | tf_op jit(solution)/shard_map/ppermute | solution.py:266
  13.7 17.7 %collective-permute-start.4 = (f32[4,8,512]{2,1,0:T(8,128)S(1)}, f32[4,8,512]{2,1,0:T(8,128)S(1)}, u32[]{:S(2)}, u32[]{:S(2)}) collective-permute-start(f32[4,8,512]{2,1,0:T(8,128)S(1)} %copy-done.6), channel_id=1, source_target_pairs={{2,0},{4,2},{6,4},{8,6},{10,8},{12,10},{14,12},{15,14},{1,3},{3,5}... | collective-permute-start | bytes 196616 | tf_op jit(solution)/shard_map/ppermute | solution.py:267
  13.7 17.7 %collective-permute-start.3 = (f32[4,8,512]{2,1,0:T(8,128)S(1)}, f32[4,8,512]{2,1,0:T(8,128)S(1)}, u32[]{:S(2)}, u32[]{:S(2)}) collective-permute-start(f32[4,8,512]{2,1,0:T(8,128)S(1)} %copy-done.5), channel_id=1, source_target_pairs={{0,2},{2,4},{4,6},{6,8},{8,10},{10,12},{12,14},{14,15},{3,1},{5,3}... | collective-permute-start | bytes 196616 | tf_op jit(solution)/shard_map/ppermute | solution.py:266
  16.3 15.0 %collective-permute-start.5 = (f32[4,4,512]{2,1,0:T(4,128)S(1)}, f32[4,4,512]{2,1,0:T(4,128)S(1)}, u32[]{:S(2)}, u32[]{:S(2)}) collective-permute-start(f32[4,4,512]{2,1,0:T(4,128)S(1)} %copy-done.8), channel_id=1, source_target_pairs={{0,1},{1,0},{2,3},{3,2},{4,5},{5,4},{6,7},{7,6},{8,9},{9,8},{10,11... | collective-permute-start | bytes 98312 | tf_op jit(solution)/shard_map/ppermute | solution.py:268
  58.9 4.7 %collective-permute-start.7 = (f32[4,8,512]{2,1,0:T(8,128)S(1)}, f32[4,8,512]{2,1,0:T(8,128)S(1)}, u32[]{:S(2)}, u32[]{:S(2)}) collective-permute-start(f32[4,8,512]{2,1,0:T(8,128)S(1)} %get-tuple-element.61.refs_0_), channel_id=1, source_target_pairs={{2,0},{4,2},{6,4},{8,6},{10,8},{12,10},{14,12},{15,14},{1,3},{3,5}... | collective-permute-start | bytes 196616 | tf_op jit(solution)/shard_map/ppermute | solution.py:267
  59.8 4.3 %collective-permute-start.6 = (f32[4,8,512]{2,1,0:T(8,128)S(1)}, f32[4,8,512]{2,1,0:T(8,128)S(1)}, u32[]{:S(2)}, u32[]{:S(2)}) collective-permute-start(f32[4,8,512]{2,1,0:T(8,128)S(1)} %get-tuple-element.62.refs_1_), channel_id=1, source_target_pairs={{0,2},{2,4},{4,6},{6,8},{8,10},{10,12},{12,14},{14,15},{3,1},{5,3}... | collective-permute-start | bytes 196616 | tf_op jit(solution)/shard_map/ppermute | solution.py:266
  61.0 1.2 %collective-permute-start.8 = (f32[4,4,512]{2,1,0:T(4,128)S(1)}, f32[4,4,512]{2,1,0:T(4,128)S(1)}, u32[]{:S(2)}, u32[]{:S(2)}) collective-permute-start(f32[4,4,512]{2,1,0:T(4,128)S(1)} %get-tuple-element.63.refs_2_), channel_id=1, source_target_pairs={{0,1},{1,0},{2,3},{3,2},{4,5},{5,4},{6,7},{7,6},{8,9},{9,8},{10,11... | collective-permute-start | bytes 98312 | tf_op jit(solution)/shard_map/ppermute | solution.py:268

commit v6 on v5

--- a/solution.py
+++ b/solution.py
@@ -353,7 +353,11 @@
         shade_halo, right_halo = swap_faces(*shade_faces), swap_faces(*right_faces)
         received = pay1.exchange(payload)
 
-        def own_kernel(shade, labels, strength, slot_tile, out, sums, slots_out):
+        def own_kernel(shade, labels, strength, slot_tile, out, sums, gathers, scatters):
+            columns = slot_tile[...].T
+            for t in range(links):
+                gathers[t] = gather_matrix(slot_tile[t : t + 1, :], slots)
+                scatters[t] = scatter_matrix(columns[:, t : t + 1], slots)
             square = power = jnp.zeros((1, LANES), F32)
             for t in range(frames):
                 right = right_of(labels[t], strength[t])
@@ -362,9 +366,18 @@
                 power = power + row_sum(right * part)
                 out[t] = part
             sums[...] = tile_rows([square, power])
-            slots_out[...] = slot_tile[...]
-
-        own, sums, slot_tile = call(own_kernel, [intensity, labels, strength, slot_tile], [field, tile, tile], "inner_image_of_right")
+
+        own, sums, gathers, scatters = call(
+            own_kernel,
+            [intensity, labels, strength, slot_tile],
+            [
+                field,
+                tile,
+                jax.ShapeDtypeStruct((links, slots, LANES), jnp.bfloat16),
+                jax.ShapeDtypeStruct((links, LANES, slots), jnp.bfloat16),
+            ],
+            "inner_image_of_right",
+        )
 
         edge_shapes = [face_z, face_z, face_y]
 
@@ -427,7 +440,7 @@
             "flux_of_right",
         )
 
-        def part_kernel(own, sums, joined, slot_tile, flux, *refs):
+        def part_kernel(own, sums, joined, gathers, flux, *refs):
             shade, shade_out, right, right_out = (refs[k : k + 3] for k in (0, 3, 6, 9))
             rows, refs = refs[12 : 12 + pay2.count], refs[12 + pay2.count :]
             pay, (image, *weights), flows = refs[: pay2.count], refs[pay2.count : pay2.count + 4], refs[pay2.count + 4 :]
@@ -448,13 +461,13 @@
                 if t > 0:
                     part = part + flux[t - 1]
                 if t < links:
-                    pay2.put(pay, links + t, pick(gather_matrix(slot_tile[t : t + 1], slots), part))
+                    pay2.put(pay, links + t, pick(gathers[t], part))
                 store_cells(image, t, part)
             pay2.put_spare(pay, packed_sums([sums[0:1, :], power]))
 
         *payload, part, weight0, weight1, weight2 = call(
             part_kernel,
-            [own, sums, joined, slot_tile, flux, *facing(shade_faces), *shade_halo, *facing(right_faces), *right_halo, *payload],
+            [own, sums, joined, gathers, flux, *facing(shade_faces), *shade_halo, *facing(right_faces), *right_halo, *payload],
             pay2.shapes + [field] + edge_shapes,
             "image_of_right",
             scratch=[pltpu.VMEM(leaf.shape, F32) for leaf in edge_shapes],
@@ -462,24 +475,23 @@
         weights = weight0, weight1, weight2
         received = pay2.exchange(payload)
 
-        def residual_kernel(labels, strength, part, slot_tile, *refs):
+        def residual_kernel(labels, strength, part, scatters, *refs):
             place = whereabouts()
             arrived, (image, residual, scalars, *faces) = refs[: pay2.count], refs[pay2.count :]
             square, power = unpacked_sums(pay2.get_spare(arrived), 2)
             step = square / power
             scalars[...] = tile_rows([jnp.broadcast_to(v, (1, LANES)) for v in (square, power, step)])
-            columns = slot_tile[...].T
             for t in range(frames):
                 image_t = to_blocks(part[t])
                 if t < links:
-                    image_t = image_t - pick(scatter_matrix(columns[:, t : t + 1], slots), pay2.get(arrived, t))
+                    image_t = image_t - pick(scatters[t], pay2.get(arrived, t))
                 store_cells(image, t, image_t)
                 store_cells(residual, t, to_blocks(right_of(labels[t], strength[t])) - step * image_t)
                 put_faces(faces, place, t, residual[t])
 
         image, residual, scalars, *faces = call(
             residual_kernel,
-            [labels, strength, part, slot_tile, *received],
+            [labels, strength, part, scatters, *received],
             [field, field, tile] + edge_shapes,
             "first_residual",
         )
@@ -533,7 +545,7 @@
         )
         received = pay3.exchange(payload)
 
-        def final_kernel(labels, strength, residual, image, inner, flow0, flow1, flow2, slot_tile, scalars, *refs):
+        def final_kernel(labels, strength, residual, image, inner, flow0, flow1, flow2, scatters, scalars, *refs):
             place = whereabouts()
             arrived, (solution_out, residual_out, solution_field, out, done) = refs[: pay3.count], refs[pay3.count :]
             copies = []
@@ -541,11 +553,10 @@
             square, power, step = scalars[0:1, :1], scalars[1:2, :1], scalars[2:3, :1]
             turn = norm / square
             second = norm / (whole + 2.0 * turn * cross + turn * turn * power)
-            columns = slot_tile[...].T
             for t in range(frames):
                 turned = to_blocks(with_flows(inner[t], (flow0, flow1, flow2), place, t))
                 if t < links:
-                    turned = turned - pick(scatter_matrix(columns[:, t : t + 1], slots), pay3.get(arrived, t))
+                    turned = turned - pick(scatters[t], pay3.get(arrived, t))
                 residual_t = to_blocks(residual[t])
                 right = to_blocks(right_of(labels[t], strength[t]))
                 direction = residual_t + turn * right
@@ -561,7 +572,7 @@
         return tuple(
             call(
                 final_kernel,
-                [labels, strength, residual, image, inner, flow0, flow1, flow2, slot_tile, scalars, *received],
+                [labels, strength, residual, image, inner, flow0, flow1, flow2, scatters, scalars, *received],
                 [field, field],
                 "solution_and_residual",
                 far_outputs=True,

time: 82.7 us -> 82.4 us (level)
  no operation moved by 1% of the time
where the time goes in v6:
time: 82.4 us; the launch traced here: 82.1 us
  blocking collectives  43.8 us (53%)
  waiting for transfers between devices  15.3 us (19%)
  starting transfers between devices  14.7 us (18%)
  Pallas kernels  7.43 us (9%)
  between operations  0.84 us (1%)
    all_to_all x2, blocking collectives, exchange(): lax.all_to_all(packed, AXES, split_axis=0, concat_axis=0, tiled=True)  43.8 us
    all_to_all x1, waiting for transfers between devices, exchange(): lax.all_to_all(packed, AXES, split_axis=0, concat_axis=0, tiled=True)  13 us
    all_to_all x1, starting transfers between devices, exchange(): lax.all_to_all(packed, AXES, split_axis=0, concat_axis=0, tiled=True)  7.53 us
    pallas_call x8, Pallas kernels, call(): pl.pallas_call(kernel, out_shape=outputs, in_specs=[away if far else near...  7.43 us
    ppermute x3, starting transfers between devices, swap_faces(): lax.ppermute(along, AXES, ring)  5.8 us
  transfers between devices with their start and end apart: 10, of which 4 were waited for; matrix products, arithmetic and copies ran while one was open for 0% of the time, Pallas kernels for 3%

profile of v6, /device:TPU:0, one launch (start us, length us, event | category | flops | bytes accessed | tf_op | source)
XLA Modules:
  0.0 82.1 jit_solution(2072450649412846693)
XLA Ops:
  0.6 2.9 %send_blocks.1 = (f32[1552,128]{1,0:T(8,128)}, f32[8,128]{1,0:T(8,128)}, f32[4,8,512]{2,1,0:T(8,128)}, f32[4,8,512]{2,1,0:T(8,128)}, f32[4,4,512]{2,1,0:T(4,128)...) custom-call(s32[3,4,4,8]{3,2,1,0:T(4,128)} %bitcast.14, f32[4,4,8,512]{3,2,1,0:T(8,128)} %shade.5, ...), custom_call_target="tpu_custom_call" | custom-call | tf_op jit(solution)/shard_map/send_blocks/pallas_call | solution.py:141
  3.5 0.0 copy-start.7
  3.5 0.0 copy-start.4
  3.5 0.0 copy-start.3
  3.5 0.0 copy-start.6
  3.5 0.0 copy-start.5
  3.6 0.0 copy-start.8
  3.6 0.0 copy-start
  3.6 0.0 copy-start.1
  3.6 0.0 copy-start.2
  3.6 7.5 %all-to-all-start = ((f32[16,97,1,128]{3,2,1,0:T(1,128)}), f32[16,97,1,128]{3,2,1,0:T(1,128)S(1)}, u32[]{:S(2)}, u32[]{:S(2)}) async-start(f32[16,97,1,128]{3,2,1,0:T(1,128)} %bitcast.13), calls=%async_computation | async-start | bytes 1589248 | tf_op jit(solution)/shard_map/all_to_all | solution.py:131
  11.1 0.0 copy-done.7
  11.2 0.5 collective-permute-start.2
  11.6 0.0 copy-done.4
  11.6 0.1 collective-permute-start.1
  11.7 0.0 copy-done.3
  11.7 1.9 %collective-permute-start = (f32[4,8,512]{2,1,0:T(8,128)S(1)}, f32[4,8,512]{2,1,0:T(8,128)S(1)}, u32[]{:S(2)}, u32[]{:S(2)}) collective-permute-start(f32[4,8,512]{2,1,0:T(8,128)S(1)} %copy-done.3), channel_id=1, source_target_pairs={{0,2},{2,4},{4,6},{6,8},{8,10},{10,12},{12,14},{14,15},{3,1},{5,3}... | collective-permute-start | bytes 196616 | tf_op jit(solution)/shard_map/ppermute | solution.py:266
  13.7 0.0 copy-done.6
  13.7 0.0 collective-permute-start.4
  13.7 0.0 copy-done.5
  13.7 2.6 %collective-permute-start.3 = (f32[4,8,512]{2,1,0:T(8,128)S(1)}, f32[4,8,512]{2,1,0:T(8,128)S(1)}, u32[]{:S(2)}, u32[]{:S(2)}) collective-permute-start(f32[4,8,512]{2,1,0:T(8,128)S(1)} %copy-done.5), channel_id=1, source_target_pairs={{0,2},{2,4},{4,6},{6,8},{8,10},{10,12},{12,14},{14,15},{3,1},{5,3}... | collective-permute-start | bytes 196616 | tf_op jit(solution)/shard_map/ppermute | solution.py:266
  16.3 0.0 collective-permute-done.2.refs_5_
  16.3 0.0 copy-done.8
  16.3 0.0 collective-permute-start.5
  16.3 0.0 copy-done
  16.3 0.0 copy-done.1
  16.3 0.0 copy-done.2
  16.3 0.6 inner_image_of_right.1
  17.0 13.0 %all-to-all-done = f32[16,97,1,128]{3,2,1,0:T(1,128)S(1)} async-done(((f32[16,97,1,128]{3,2,1,0:T(1,128)}), f32[16,97,1,128]{3,2,1,0:T(1,128)S(1)}, u32[]{:S(2)}, u32[]{:S(2)}) %all-to-all-start) | async-done | bytes 794656 | tf_op jit(solution)/shard_map/all_to_all | solution.py:131
  30.0 1.3 %flux_of_right.1 = (f32[1552,128]{1,0:T(8,128)S(1)}, f32[3,128,128]{2,1,0:T(8,128)S(1)}, f32[3,128,128]{2,1,0:T(8,128)S(1)}, f32[3,128,128]{2,1,0:T(8,128)S(1)},...) custom-call(f32[4,4,8,512]{3,2,1,0:T(8,128)S(1)} %copy-done.2, s32[4,4,8,512]{3,2,1,0:T(8,128)S(1)} %copy-done, ...), custom_call_target="tpu_custom_call" | custom-call | tf_op jit(solution)/shard_map/flux_of_right/pallas_call | solution.py:141
  31.3 0.0 collective-permute-done.5.refs_11_
  31.3 0.0 collective-permute-done.1.refs_4_
  31.3 0.0 collective-permute-done.refs_3_
  31.4 0.0 collective-permute-done.4.refs_10_
  31.4 0.0 collective-permute-done.3.refs_9_
  31.4 0.4 image_of_right.1
  31.8 26.8 %all_to_all.15 = f32[16,97,1,128]{3,2,1,0:T(1,128)S(1)} all-to-all(f32[16,97,1,128]{3,2,1,0:T(1,128)S(1)} %bitcast.11), channel_id=1, replica_groups=mesh['grp'=2,'slc'=8,'row'=2] {'slc','row'}, dimensions={0} | all-to-all | bytes 1589248 | tf_op jit(solution)/shard_map/all_to_all | solution.py:131
  58.5 0.3 first_residual.1
  58.8 0.8 %collective-permute-start.7 = (f32[4,8,512]{2,1,0:T(8,128)S(1)}, f32[4,8,512]{2,1,0:T(8,128)S(1)}, u32[]{:S(2)}, u32[]{:S(2)}) collective-permute-start(f32[4,8,512]{2,1,0:T(8,128)S(1)} %get-tuple-element.63.refs_0_), channel_id=1, source_target_pairs={{2,0},{4,2},{6,4},{8,6},{10,8},{12,10},{14,12},{15,14},{1,3},{3,5}... | collective-permute-start | bytes 196616 | tf_op jit(solution)/shard_map/ppermute | solution.py:267
  59.6 1.3 %collective-permute-start.6 = (f32[4,8,512]{2,1,0:T(8,128)S(1)}, f32[4,8,512]{2,1,0:T(8,128)S(1)}, u32[]{:S(2)}, u32[]{:S(2)}) collective-permute-start(f32[4,8,512]{2,1,0:T(8,128)S(1)} %get-tuple-element.64.refs_1_), channel_id=1, source_target_pairs={{0,2},{2,4},{4,6},{6,8},{8,10},{10,12},{12,14},{14,15},{3,1},{5,3}... | collective-permute-start | bytes 196616 | tf_op jit(solution)/shard_map/ppermute | solution.py:266
  60.9 0.0 collective-permute-start.8
  60.9 0.8 inner_image_of_residual.1
  61.7 0.4 collective-permute-done.8.refs_5_
  62.1 1.4 %collective-permute-done.7.refs_4_ = f32[4,8,512]{2,1,0:T(8,128)S(1)} collective-permute-done((f32[4,8,512]{2,1,0:T(8,128)S(1)}, f32[4,8,512]{2,1,0:T(8,128)S(1)}, u32[]{:S(2)}, u32[]{:S(2)}) %collective-permute-start.7) | collective-permute-done | bytes 65568 | tf_op jit(solution)/shard_map/ppermute | solution.py:267
  63.5 0.4 collective-permute-done.6.refs_3_
  63.9 0.1 outer_image_of_residual.1
  64.0 17.0 %all_to_all.16 = f32[16,49,1,128]{3,2,1,0:T(1,128)S(1)} all-to-all(f32[16,49,1,128]{3,2,1,0:T(1,128)S(1)} %bitcast.12), channel_id=1, replica_groups=mesh['grp'=2,'slc'=8,'row'=2] {'slc','row'}, dimensions={0} | all-to-all | bytes 802816 | tf_op jit(solution)/shard_map/all_to_all | solution.py:131
  81.0 1.1 %solution_and_residual.1 = (f32[4,4,8,512]{3,2,1,0:T(8,128)}, f32[4,4,8,512]{3,2,1,0:T(8,128)}) custom-call(s32[4,4,8,512]{3,2,1,0:T(8,128)S(1)} %copy-done, f32[4,4,8,512]{3,2,1,0:T(8,128)S(1)} %copy-done.1, f32[4,4,8,512]{3,2,1,0:T(8,128)S(1)} %get-tuple-element.55.residual, f32[4,4,8,512]{3,2,1,0:T(8,128)S(1)} %get-tuple-element.56.image, ...), custom_call_target="tpu_custom_call" | custom-call | tf_op jit(solution)/shard_map/solution_and_residual/pallas_call | solution.py:141
  (2 shorter events, 0.0 us)
Async XLA Ops:
  3.5 7.6 %copy-start.7 = (f32[4,4,512]{2,1,0:T(4,128)S(1)}, f32[4,4,512]{2,1,0:T(4,128)}, u32[]{:S(2)}) copy-start(f32[4,4,512]{2,1,0:T(4,128)} %get-tuple-element.47.refs_2_) | copy-start | bytes 98308
  3.5 8.1 %copy-start.4 = (f32[4,8,512]{2,1,0:T(8,128)S(1)}, f32[4,8,512]{2,1,0:T(8,128)}, u32[]{:S(2)}) copy-start(f32[4,8,512]{2,1,0:T(8,128)} %get-tuple-element.45.refs_0_) | copy-start | bytes 196612
  3.5 8.2 %copy-start.3 = (f32[4,8,512]{2,1,0:T(8,128)S(1)}, f32[4,8,512]{2,1,0:T(8,128)}, u32[]{:S(2)}) copy-start(f32[4,8,512]{2,1,0:T(8,128)} %get-tuple-element.46.refs_1_) | copy-start | bytes 196612
  3.5 10.1 %copy-start.6 = (f32[4,8,512]{2,1,0:T(8,128)S(1)}, f32[4,8,512]{2,1,0:T(8,128)}, u32[]{:S(2)}) copy-start(f32[4,8,512]{2,1,0:T(8,128)} %get-tuple-element.48.refs_6_) | copy-start | bytes 196612
  3.5 10.1 %copy-start.5 = (f32[4,8,512]{2,1,0:T(8,128)S(1)}, f32[4,8,512]{2,1,0:T(8,128)}, u32[]{:S(2)}) copy-start(f32[4,8,512]{2,1,0:T(8,128)} %get-tuple-element.49.refs_7_) | copy-start | bytes 196612
  3.6 12.7 %copy-start.8 = (f32[4,4,512]{2,1,0:T(4,128)S(1)}, f32[4,4,512]{2,1,0:T(4,128)}, u32[]{:S(2)}) copy-start(f32[4,4,512]{2,1,0:T(4,128)} %get-tuple-element.50.refs_8_) | copy-start | bytes 98308
  3.6 12.7 %copy-start = (s32[4,4,8,512]{3,2,1,0:T(8,128)S(1)}, s32[4,4,8,512]{3,2,1,0:T(8,128)}, u32[]{:S(2)}) copy-start(s32[4,4,8,512]{3,2,1,0:T(8,128)} %labels.9) | copy-start | bytes 786436
  3.6 12.7 %copy-start.1 = (f32[4,4,8,512]{3,2,1,0:T(8,128)S(1)}, f32[4,4,8,512]{3,2,1,0:T(8,128)}, u32[]{:S(2)}) copy-start(f32[4,4,8,512]{3,2,1,0:T(8,128)} %strength.9) | copy-start | bytes 786436
  3.6 12.7 %copy-start.2 = (f32[4,4,8,512]{3,2,1,0:T(8,128)S(1)}, f32[4,4,8,512]{3,2,1,0:T(8,128)}, u32[]{:S(2)}) copy-start(f32[4,4,8,512]{3,2,1,0:T(8,128)} %shade.5) | copy-start | bytes 786436
  3.6 26.4 %all-to-all-start = ((f32[16,97,1,128]{3,2,1,0:T(1,128)}), f32[16,97,1,128]{3,2,1,0:T(1,128)S(1)}, u32[]{:S(2)}, u32[]{:S(2)}) async-start(f32[16,97,1,128]{3,2,1,0:T(1,128)} %bitcast.13), calls=%async_computation | async-start | bytes 1589248 | tf_op jit(solution)/shard_map/all_to_all | solution.py:131
  11.2 5.1 %collective-permute-start.2 = (f32[4,4,512]{2,1,0:T(4,128)S(1)}, f32[4,4,512]{2,1,0:T(4,128)S(1)}, u32[]{:S(2)}, u32[]{:S(2)}) collective-permute-start(f32[4,4,512]{2,1,0:T(4,128)S(1)} %copy-done.7), channel_id=1, source_target_pairs={{0,1},{1,0},{2,3},{3,2},{4,5},{5,4},{6,7},{7,6},{8,9},{9,8},{10,11... | collective-permute-start | bytes 98312 | tf_op jit(solution)/shard_map/ppermute | solution.py:268
  11.6 19.7 %collective-permute-start.1 = (f32[4,8,512]{2,1,0:T(8,128)S(1)}, f32[4,8,512]{2,1,0:T(8,128)S(1)}, u32[]{:S(2)}, u32[]{:S(2)}) collective-permute-start(f32[4,8,512]{2,1,0:T(8,128)S(1)} %copy-done.4), channel_id=1, source_target_pairs={{2,0},{4,2},{6,4},{8,6},{10,8},{12,10},{14,12},{15,14},{1,3},{3,5}... | collective-permute-start | bytes 196616 | tf_op jit(solution)/shard_map/ppermute | solution.py:267
  11.7 4.6 %copy-start.9 = (f32[8,128]{1,0:T(8,128)S(1)}, f32[8,128]{1,0:T(8,128)}, u32[]{:S(2)}) copy-start(f32[8,128]{1,0:T(8,128)} %get-tuple-element.38.slot_tile) | copy-start | bytes 12292
  11.7 19.6 %collective-permute-start = (f32[4,8,512]{2,1,0:T(8,128)S(1)}, f32[4,8,512]{2,1,0:T(8,128)S(1)}, u32[]{:S(2)}, u32[]{:S(2)}) collective-permute-start(f32[4,8,512]{2,1,0:T(8,128)S(1)} %copy-done.3), channel_id=1, source_target_pairs={{0,2},{2,4},{4,6},{6,8},{8,10},{10,12},{12,14},{14,15},{3,1},{5,3}... | collective-permute-start | bytes 196616 | tf_op jit(solution)/shard_map/ppermute | solution.py:266
  13.7 17.7 %collective-permute-start.4 = (f32[4,8,512]{2,1,0:T(8,128)S(1)}, f32[4,8,512]{2,1,0:T(8,128)S(1)}, u32[]{:S(2)}, u32[]{:S(2)}) collective-permute-start(f32[4,8,512]{2,1,0:T(8,128)S(1)} %copy-done.6), channel_id=1, source_target_pairs={{2,0},{4,2},{6,4},{8,6},{10,8},{12,10},{14,12},{15,14},{1,3},{3,5}... | collective-permute-start | bytes 196616 | tf_op jit(solution)/shard_map/ppermute | solution.py:267
  13.7 17.7 %collective-permute-start.3 = (f32[4,8,512]{2,1,0:T(8,128)S(1)}, f32[4,8,512]{2,1,0:T(8,128)S(1)}, u32[]{:S(2)}, u32[]{:S(2)}) collective-permute-start(f32[4,8,512]{2,1,0:T(8,128)S(1)} %copy-done.5), channel_id=1, source_target_pairs={{0,2},{2,4},{4,6},{6,8},{8,10},{10,12},{12,14},{14,15},{3,1},{5,3}... | collective-permute-start | bytes 196616 | tf_op jit(solution)/shard_map/ppermute | solution.py:266
  16.3 15.0 %collective-permute-start.5 = (f32[4,4,512]{2,1,0:T(4,128)S(1)}, f32[4,4,512]{2,1,0:T(4,128)S(1)}, u32[]{:S(2)}, u32[]{:S(2)}) collective-permute-start(f32[4,4,512]{2,1,0:T(4,128)S(1)} %copy-done.8), channel_id=1, source_target_pairs={{0,1},{1,0},{2,3},{3,2},{4,5},{5,4},{6,7},{7,6},{8,9},{9,8},{10,11... | collective-permute-start | bytes 98312 | tf_op jit(solution)/shard_map/ppermute | solution.py:268
  58.8 4.7 %collective-permute-start.7 = (f32[4,8,512]{2,1,0:T(8,128)S(1)}, f32[4,8,512]{2,1,0:T(8,128)S(1)}, u32[]{:S(2)}, u32[]{:S(2)}) collective-permute-start(f32[4,8,512]{2,1,0:T(8,128)S(1)} %get-tuple-element.63.refs_0_), channel_id=1, source_target_pairs={{2,0},{4,2},{6,4},{8,6},{10,8},{12,10},{14,12},{15,14},{1,3},{3,5}... | collective-permute-start | bytes 196616 | tf_op jit(solution)/shard_map/ppermute | solution.py:267
  59.6 4.3 %collective-permute-start.6 = (f32[4,8,512]{2,1,0:T(8,128)S(1)}, f32[4,8,512]{2,1,0:T(8,128)S(1)}, u32[]{:S(2)}, u32[]{:S(2)}) collective-permute-start(f32[4,8,512]{2,1,0:T(8,128)S(1)} %get-tuple-element.64.refs_1_), channel_id=1, source_target_pairs={{0,2},{2,4},{4,6},{6,8},{8,10},{10,12},{12,14},{14,15},{3,1},{5,3}... | collective-permute-start | bytes 196616 | tf_op jit(solution)/shard_map/ppermute | solution.py:266
  60.9 1.2 %collective-permute-start.8 = (f32[4,4,512]{2,1,0:T(4,128)S(1)}, f32[4,4,512]{2,1,0:T(4,128)S(1)}, u32[]{:S(2)}, u32[]{:S(2)}) collective-permute-start(f32[4,4,512]{2,1,0:T(4,128)S(1)} %get-tuple-element.65.refs_2_), channel_id=1, source_target_pairs={{0,1},{1,0},{2,3},{3,2},{4,5},{5,4},{6,7},{7,6},{8,9},{9,8},{10,11... | collective-permute-start | bytes 98312 | tf_op jit(solution)/shard_map/ppermute | solution.py:268

commit v7 on v6

--- a/solution.py
+++ b/solution.py
@@ -528,26 +528,28 @@
             pay3.shapes + [field, tile],
             "inner_image_of_residual",
         )
-        def outer_kernel(sums, *refs):
-            faces, outside, weights = (refs[k : k + 3] for k in (0, 3, 6))
-            rows, pay, flows = refs[9 : 9 + pay3.count], refs[9 + pay3.count : 9 + 2 * pay3.count], refs[-3:]
+        def outer_kernel(sums, along, beside, face0, face2, weight0, weight2, *refs):
+            rows, pay, flows = refs[: pay3.count], refs[pay3.count : 2 * pay3.count], refs[2 * pay3.count :]
             pay[0][...] = rows[0][...]
-            power = sums[1:2, :]
-            for k in range(3):
-                power = power + put_flow(flows[k], weights[k][...], faces[k][...], outside[k][...])
+            gap = face0[...] - along[...]
+            flow = weight0[...] * gap
+            flows[0][...] = flow
+            power = sums[1:2, :] + row_sum(flow * gap) + put_flow(flows[1], weight2[...], face2[...], beside[...])
             pay3.put_spare(pay, packed_sums([sums[0:1, :], power, sums[2:3, :]]))
 
-        *payload, flow0, flow1, flow2 = call(
+        own0, own1, own2 = facing(faces)
+        *payload, flow0, flow2 = call(
             outer_kernel,
-            [sums, *facing(faces), *halo, *weights, *payload],
-            pay3.shapes + edge_shapes,
+            [sums, halo[0], halo[2], own0, own2, weights[0], weights[2], *payload],
+            pay3.shapes + [face_z, face_y],
             "outer_image_of_residual",
         )
         received = pay3.exchange(payload)
 
-        def final_kernel(labels, strength, residual, image, inner, flow0, flow1, flow2, scatters, scalars, *refs):
+        def final_kernel(labels, strength, residual, image, inner, flow0, own1, against, weight1, flow2, scatters, scalars, *refs):
             place = whereabouts()
-            arrived, (solution_out, residual_out, solution_field, out, done) = refs[: pay3.count], refs[pay3.count :]
+            arrived, (solution_out, residual_out, solution_field, out, flow1, done) = refs[: pay3.count], refs[pay3.count :]
+            flow1[...] = weight1[...] * (own1[...] - against[...])
             copies = []
             norm, whole, cross = unpacked_sums(pay3.get_spare(arrived), 3)
             square, power, step = scalars[0:1, :1], scalars[1:2, :1], scalars[2:3, :1]
@@ -572,11 +574,12 @@
         return tuple(
             call(
                 final_kernel,
-                [labels, strength, residual, image, inner, flow0, flow1, flow2, scatters, scalars, *received],
+                [labels, strength, residual, image, inner, flow0, own1, halo[1], weights[1], flow2, scatters, scalars, *received],
                 [field, field],
                 "solution_and_residual",
                 far_outputs=True,
-                scratch=[pltpu.VMEM(field.shape, F32)] * 2 + [pltpu.SemaphoreType.DMA((frames, 2))],
+                scratch=[pltpu.VMEM(field.shape, F32)] * 2
+                + [pltpu.VMEM(face_z.shape, F32), pltpu.SemaphoreType.DMA((frames, 2))],
             )
         )
 

time: 82.4 us -> 82.2 us (level)
  blocking collectives: 43.8 us -> 26.8 us
  waiting for transfers between devices: 15.3 us -> 26.1 us
  starting transfers between devices: 14.7 us -> 19.9 us
    all_to_all x2 -> x1, blocking collectives: 43.8 us -> 26.8 us  [exchange(): lax.all_to_all(packed, AXES, split_axis=0, concat_axis=0, tiled=True)]
    all_to_all x1 -> x2, waiting for transfers between devices: 13 us -> 19.1 us  [exchange(): lax.all_to_all(packed, AXES, split_axis=0, concat_axis=0, tiled=True)]
    all_to_all x1 -> x2, starting transfers between devices: 7.53 us -> 13.3 us  [exchange(): lax.all_to_all(packed, AXES, split_axis=0, concat_axis=0, tiled=True)]
    ppermute x3, waiting for transfers between devices: 1.4 us -> 5.84 us  [swap_faces(): lax.ppermute(against, AXES, [(j, i) for i, j in ring])]
  transfers between devices with their start and end apart: 10 -> 11, of which waited for: 4 -> 5; matrix products, arithmetic and copies ran while one was open for 0% -> 0% of each run, Pallas kernels for 3% -> 3%
where the time goes in v7:
time: 82.2 us; the launch traced here: 81.8 us
  blocking collectives  26.8 us (33%)
  waiting for transfers between devices  26.1 us (32%)
  starting transfers between devices  19.9 us (24%)
  Pallas kernels  8.16 us (10%)
  between operations  0.85 us (1%)
    all_to_all x1, blocking collectives, exchange(): lax.all_to_all(packed, AXES, split_axis=0, concat_axis=0, tiled=True)  26.8 us
    all_to_all x2, waiting for transfers between devices, exchange(): lax.all_to_all(packed, AXES, split_axis=0, concat_axis=0, tiled=True)  19.1 us
    all_to_all x2, starting transfers between devices, exchange(): lax.all_to_all(packed, AXES, split_axis=0, concat_axis=0, tiled=True)  13.3 us
    pallas_call x8, Pallas kernels, call(): pl.pallas_call(kernel, out_shape=outputs, in_specs=[away if far else near...  8.16 us
    ppermute x3, waiting for transfers between devices, swap_faces(): lax.ppermute(against, AXES, [(j, i) for i, j in ring])  5.84 us
    ppermute x3, starting transfers between devices, swap_faces(): lax.ppermute(along, AXES, ring)  5.52 us
  transfers between devices with their start and end apart: 11, of which 5 were waited for; matrix products, arithmetic and copies ran while one was open for 0% of the time, Pallas kernels for 3%

profile of v7, /device:TPU:0, one launch (start us, length us, event | category | flops | bytes accessed | tf_op | source)
XLA Modules:
  0.0 81.8 jit_solution(10413409581745101864)
XLA Ops:
  0.6 2.9 %send_blocks.1 = (f32[1552,128]{1,0:T(8,128)}, f32[8,128]{1,0:T(8,128)}, f32[4,8,512]{2,1,0:T(8,128)}, f32[4,8,512]{2,1,0:T(8,128)}, f32[4,4,512]{2,1,0:T(4,128)...) custom-call(s32[3,4,4,8]{3,2,1,0:T(4,128)} %bitcast.13, f32[4,4,8,512]{3,2,1,0:T(8,128)} %shade.5, ...), custom_call_target="tpu_custom_call" | custom-call | tf_op jit(solution)/shard_map/send_blocks/pallas_call | solution.py:141
  3.5 0.0 copy-start.7
  3.5 0.0 copy-start.4
  3.5 0.0 copy-start.3
  3.5 0.0 copy-start.6
  3.6 0.0 copy-start.5
  3.6 0.0 copy-start.8
  3.6 0.0 copy-start
  3.6 0.0 copy-start.1
  3.6 0.0 copy-start.2
  3.6 7.5 %all-to-all-start = ((f32[16,97,1,128]{3,2,1,0:T(1,128)}), f32[16,97,1,128]{3,2,1,0:T(1,128)S(1)}, u32[]{:S(2)}, u32[]{:S(2)}) async-start(f32[16,97,1,128]{3,2,1,0:T(1,128)} %bitcast.12), calls=%async_computation | async-start | bytes 1589248 | tf_op jit(solution)/shard_map/all_to_all | solution.py:131
  11.1 0.0 copy-done.7
  11.2 0.5 collective-permute-start.2
  11.6 0.0 copy-done.4
  11.6 0.1 collective-permute-start.1
  11.7 0.0 copy-done.3
  11.7 1.9 %collective-permute-start = (f32[4,8,512]{2,1,0:T(8,128)S(1)}, f32[4,8,512]{2,1,0:T(8,128)S(1)}, u32[]{:S(2)}, u32[]{:S(2)}) collective-permute-start(f32[4,8,512]{2,1,0:T(8,128)S(1)} %copy-done.3), channel_id=1, source_target_pairs={{0,2},{2,4},{4,6},{6,8},{8,10},{10,12},{12,14},{14,15},{3,1},{5,3}... | collective-permute-start | bytes 196616 | tf_op jit(solution)/shard_map/ppermute | solution.py:266
  13.7 0.0 copy-done.6
  13.7 0.0 collective-permute-start.4
  13.7 0.0 copy-done.5
  13.7 2.6 %collective-permute-start.3 = (f32[4,8,512]{2,1,0:T(8,128)S(1)}, f32[4,8,512]{2,1,0:T(8,128)S(1)}, u32[]{:S(2)}, u32[]{:S(2)}) collective-permute-start(f32[4,8,512]{2,1,0:T(8,128)S(1)} %copy-done.5), channel_id=1, source_target_pairs={{0,2},{2,4},{4,6},{6,8},{8,10},{10,12},{12,14},{14,15},{3,1},{5,3}... | collective-permute-start | bytes 196616 | tf_op jit(solution)/shard_map/ppermute | solution.py:266
  16.3 0.0 collective-permute-done.2.refs_5_
  16.3 0.0 copy-done.8
  16.3 0.0 collective-permute-start.5
  16.3 0.0 copy-done
  16.3 0.0 copy-done.1
  16.3 0.6 inner_image_of_right.1
  17.0 13.0 %all-to-all-done = f32[16,97,1,128]{3,2,1,0:T(1,128)S(1)} async-done(((f32[16,97,1,128]{3,2,1,0:T(1,128)}), f32[16,97,1,128]{3,2,1,0:T(1,128)S(1)}, u32[]{:S(2)}, u32[]{:S(2)}) %all-to-all-start) | async-done | bytes 794656 | tf_op jit(solution)/shard_map/all_to_all | solution.py:131
  30.0 1.3 %flux_of_right.1 = (f32[1552,128]{1,0:T(8,128)S(1)}, f32[3,128,128]{2,1,0:T(8,128)S(1)}, f32[3,128,128]{2,1,0:T(8,128)S(1)}, f32[3,128,128]{2,1,0:T(8,128)S(1)},...) custom-call(f32[4,4,8,512]{3,2,1,0:T(8,128)S(1)} %copy-done.2, s32[4,4,8,512]{3,2,1,0:T(8,128)S(1)} %copy-done, ...), custom_call_target="tpu_custom_call" | custom-call | tf_op jit(solution)/shard_map/flux_of_right/pallas_call | solution.py:141
  31.3 0.0 collective-permute-done.5.refs_11_
  31.3 0.0 collective-permute-done.1.refs_4_
  31.3 0.0 collective-permute-done.refs_3_
  31.4 0.0 collective-permute-done.4.refs_10_
  31.4 0.0 collective-permute-done.3.refs_9_
  31.4 0.4 image_of_right.1
  31.8 26.8 %all_to_all.15 = f32[16,97,1,128]{3,2,1,0:T(1,128)S(1)} all-to-all(f32[16,97,1,128]{3,2,1,0:T(1,128)S(1)} %bitcast.11), channel_id=1, replica_groups=mesh['grp'=2,'slc'=8,'row'=2] {'slc','row'}, dimensions={0} | all-to-all | bytes 1589248 | tf_op jit(solution)/shard_map/all_to_all | solution.py:131
  58.5 0.3 first_residual.1
  58.8 1.0 %collective-permute-start.6 = (f32[4,8,512]{2,1,0:T(8,128)S(1)}, f32[4,8,512]{2,1,0:T(8,128)S(1)}, u32[]{:S(2)}, u32[]{:S(2)}) collective-permute-start(f32[4,8,512]{2,1,0:T(8,128)S(1)} %get-tuple-element.62.own1), channel_id=1, source_target_pairs={{0,2},{2,4},{4,6},{6,8},{8,10},{10,12},{12,14},{14,15},{3,1},{5,3}... | collective-permute-start | bytes 196616 | tf_op jit(solution)/shard_map/ppermute | solution.py:266
  59.8 0.0 collective-permute-start.7
  59.8 0.7 inner_image_of_residual.1
  60.6 0.5 collective-permute-done.7.beside
  61.0 0.7 collective-permute-done.6.along
  61.7 0.9 %outer_image_of_residual.1 = (f32[784,128]{1,0:T(8,128)}, f32[4,8,512]{2,1,0:T(8,128)S(1)}, f32[4,4,512]{2,1,0:T(4,128)S(1)}) custom-call(f32[8,128]{1,0:T(8,128)S(1)} %get-tuple-element.61.sums, f32[4,8,512]{2,1,0:T(8,128)S(1)} %collective-permute-done.6.along, f32[4,4,512]{2,1,0:T(4,128)S(1)} %collective-permute-done.7.beside, ...), custom_call_target="tpu_custom_call" | custom-call | tf_op jit(solution)/shard_map/outer_image_of_residual/pallas_call | solution.py:141
  62.6 5.8 %all-to-all-start.2 = ((f32[16,49,1,128]{3,2,1,0:T(1,128)}), f32[16,49,1,128]{3,2,1,0:T(1,128)S(1)}, u32[]{:S(2)}, u32[]{:S(2)}) async-start(f32[16,49,1,128]{3,2,1,0:T(1,128)} %bitcast.5), calls=%async_computation.2 | async-start | bytes 802816 | tf_op jit(solution)/shard_map/all_to_all | solution.py:131
  68.4 0.4 collective-permute-start.8
  68.8 5.8 %collective-permute-done.8.against = f32[4,8,512]{2,1,0:T(8,128)S(1)} collective-permute-done((f32[4,8,512]{2,1,0:T(8,128)S(1)}, f32[4,8,512]{2,1,0:T(8,128)S(1)}, u32[]{:S(2)}, u32[]{:S(2)}) %collective-permute-start.8) | collective-permute-done | bytes 65568 | tf_op jit(solution)/shard_map/ppermute | solution.py:267
  74.7 6.1 %all-to-all-done.2 = f32[16,49,1,128]{3,2,1,0:T(1,128)S(1)} async-done(((f32[16,49,1,128]{3,2,1,0:T(1,128)}), f32[16,49,1,128]{3,2,1,0:T(1,128)S(1)}, u32[]{:S(2)}, u32[]{:S(2)}) %all-to-all-start.2) | async-done | bytes 401440 | tf_op jit(solution)/shard_map/all_to_all | solution.py:131
  80.8 1.1 %solution_and_residual.1 = (f32[4,4,8,512]{3,2,1,0:T(8,128)}, f32[4,4,8,512]{3,2,1,0:T(8,128)}) custom-call(s32[4,4,8,512]{3,2,1,0:T(8,128)S(1)} %copy-done, f32[4,4,8,512]{3,2,1,0:T(8,128)S(1)} %copy-done.1, f32[4,4,8,512]{3,2,1,0:T(8,128)S(1)} %get-tuple-element.54.residual, f32[4,4,8,512]{3,2,1,0:T(8,128)S(1)} %get-tuple-element.55.image, ...), custom_call_target="tpu_custom_call" | custom-call | tf_op jit(solution)/shard_map/solution_and_residual/pallas_call | solution.py:141
  (3 shorter events, 0.0 us)
Async XLA Ops:
  3.5 7.6 %copy-start.7 = (f32[4,4,512]{2,1,0:T(4,128)S(1)}, f32[4,4,512]{2,1,0:T(4,128)}, u32[]{:S(2)}) copy-start(f32[4,4,512]{2,1,0:T(4,128)} %get-tuple-element.46.refs_2_) | copy-start | bytes 98308
  3.5 8.1 %copy-start.4 = (f32[4,8,512]{2,1,0:T(8,128)S(1)}, f32[4,8,512]{2,1,0:T(8,128)}, u32[]{:S(2)}) copy-start(f32[4,8,512]{2,1,0:T(8,128)} %get-tuple-element.44.refs_0_) | copy-start | bytes 196612
  3.5 8.2 %copy-start.3 = (f32[4,8,512]{2,1,0:T(8,128)S(1)}, f32[4,8,512]{2,1,0:T(8,128)}, u32[]{:S(2)}) copy-start(f32[4,8,512]{2,1,0:T(8,128)} %get-tuple-element.45.refs_1_) | copy-start | bytes 196612
  3.5 10.1 %copy-start.6 = (f32[4,8,512]{2,1,0:T(8,128)S(1)}, f32[4,8,512]{2,1,0:T(8,128)}, u32[]{:S(2)}) copy-start(f32[4,8,512]{2,1,0:T(8,128)} %get-tuple-element.47.refs_6_) | copy-start | bytes 196612
  3.6 10.1 %copy-start.5 = (f32[4,8,512]{2,1,0:T(8,128)S(1)}, f32[4,8,512]{2,1,0:T(8,128)}, u32[]{:S(2)}) copy-start(f32[4,8,512]{2,1,0:T(8,128)} %get-tuple-element.48.refs_7_) | copy-start | bytes 196612
  3.6 12.7 %copy-start.8 = (f32[4,4,512]{2,1,0:T(4,128)S(1)}, f32[4,4,512]{2,1,0:T(4,128)}, u32[]{:S(2)}) copy-start(f32[4,4,512]{2,1,0:T(4,128)} %get-tuple-element.49.refs_8_) | copy-start | bytes 98308
  3.6 12.7 %copy-start = (s32[4,4,8,512]{3,2,1,0:T(8,128)S(1)}, s32[4,4,8,512]{3,2,1,0:T(8,128)}, u32[]{:S(2)}) copy-start(s32[4,4,8,512]{3,2,1,0:T(8,128)} %labels.9) | copy-start | bytes 786436
  3.6 12.7 %copy-start.1 = (f32[4,4,8,512]{3,2,1,0:T(8,128)S(1)}, f32[4,4,8,512]{3,2,1,0:T(8,128)}, u32[]{:S(2)}) copy-start(f32[4,4,8,512]{3,2,1,0:T(8,128)} %strength.9) | copy-start | bytes 786436
  3.6 12.7 %copy-start.2 = (f32[4,4,8,512]{3,2,1,0:T(8,128)S(1)}, f32[4,4,8,512]{3,2,1,0:T(8,128)}, u32[]{:S(2)}) copy-start(f32[4,4,8,512]{3,2,1,0:T(8,128)} %shade.5) | copy-start | bytes 786436
  3.6 26.4 %all-to-all-start = ((f32[16,97,1,128]{3,2,1,0:T(1,128)}), f32[16,97,1,128]{3,2,1,0:T(1,128)S(1)}, u32[]{:S(2)}, u32[]{:S(2)}) async-start(f32[16,97,1,128]{3,2,1,0:T(1,128)} %bitcast.12), calls=%async_computation | async-start | bytes 1589248 | tf_op jit(solution)/shard_map/all_to_all | solution.py:131
  11.2 5.1 %collective-permute-start.2 = (f32[4,4,512]{2,1,0:T(4,128)S(1)}, f32[4,4,512]{2,1,0:T(4,128)S(1)}, u32[]{:S(2)}, u32[]{:S(2)}) collective-permute-start(f32[4,4,512]{2,1,0:T(4,128)S(1)} %copy-done.7), channel_id=1, source_target_pairs={{0,1},{1,0},{2,3},{3,2},{4,5},{5,4},{6,7},{7,6},{8,9},{9,8},{10,11... | collective-permute-start | bytes 98312 | tf_op jit(solution)/shard_map/ppermute | solution.py:268
  11.6 19.7 %collective-permute-start.1 = (f32[4,8,512]{2,1,0:T(8,128)S(1)}, f32[4,8,512]{2,1,0:T(8,128)S(1)}, u32[]{:S(2)}, u32[]{:S(2)}) collective-permute-start(f32[4,8,512]{2,1,0:T(8,128)S(1)} %copy-done.4), channel_id=1, source_target_pairs={{2,0},{4,2},{6,4},{8,6},{10,8},{12,10},{14,12},{15,14},{1,3},{3,5}... | collective-permute-start | bytes 196616 | tf_op jit(solution)/shard_map/ppermute | solution.py:267
  11.7 4.6 %copy-start.9 = (f32[8,128]{1,0:T(8,128)S(1)}, f32[8,128]{1,0:T(8,128)}, u32[]{:S(2)}) copy-start(f32[8,128]{1,0:T(8,128)} %get-tuple-element.37.slot_tile) | copy-start | bytes 12292
  11.7 19.6 %collective-permute-start = (f32[4,8,512]{2,1,0:T(8,128)S(1)}, f32[4,8,512]{2,1,0:T(8,128)S(1)}, u32[]{:S(2)}, u32[]{:S(2)}) collective-permute-start(f32[4,8,512]{2,1,0:T(8,128)S(1)} %copy-done.3), channel_id=1, source_target_pairs={{0,2},{2,4},{4,6},{6,8},{8,10},{10,12},{12,14},{14,15},{3,1},{5,3}... | collective-permute-start | bytes 196616 | tf_op jit(solution)/shard_map/ppermute | solution.py:266
  13.7 17.7 %collective-permute-start.4 = (f32[4,8,512]{2,1,0:T(8,128)S(1)}, f32[4,8,512]{2,1,0:T(8,128)S(1)}, u32[]{:S(2)}, u32[]{:S(2)}) collective-permute-start(f32[4,8,512]{2,1,0:T(8,128)S(1)} %copy-done.6), channel_id=1, source_target_pairs={{2,0},{4,2},{6,4},{8,6},{10,8},{12,10},{14,12},{15,14},{1,3},{3,5}... | collective-permute-start | bytes 196616 | tf_op jit(solution)/shard_map/ppermute | solution.py:267
  13.7 17.7 %collective-permute-start.3 = (f32[4,8,512]{2,1,0:T(8,128)S(1)}, f32[4,8,512]{2,1,0:T(8,128)S(1)}, u32[]{:S(2)}, u32[]{:S(2)}) collective-permute-start(f32[4,8,512]{2,1,0:T(8,128)S(1)} %copy-done.5), channel_id=1, source_target_pairs={{0,2},{2,4},{4,6},{6,8},{8,10},{10,12},{12,14},{14,15},{3,1},{5,3}... | collective-permute-start | bytes 196616 | tf_op jit(solution)/shard_map/ppermute | solution.py:266
  16.3 15.0 %collective-permute-start.5 = (f32[4,4,512]{2,1,0:T(4,128)S(1)}, f32[4,4,512]{2,1,0:T(4,128)S(1)}, u32[]{:S(2)}, u32[]{:S(2)}) collective-permute-start(f32[4,4,512]{2,1,0:T(4,128)S(1)} %copy-done.8), channel_id=1, source_target_pairs={{0,1},{1,0},{2,3},{3,2},{4,5},{5,4},{6,7},{7,6},{8,9},{9,8},{10,11... | collective-permute-start | bytes 98312 | tf_op jit(solution)/shard_map/ppermute | solution.py:268
  58.8 2.9 %collective-permute-start.6 = (f32[4,8,512]{2,1,0:T(8,128)S(1)}, f32[4,8,512]{2,1,0:T(8,128)S(1)}, u32[]{:S(2)}, u32[]{:S(2)}) collective-permute-start(f32[4,8,512]{2,1,0:T(8,128)S(1)} %get-tuple-element.62.own1), channel_id=1, source_target_pairs={{0,2},{2,4},{4,6},{6,8},{8,10},{10,12},{12,14},{14,15},{3,1},{5,3}... | collective-permute-start | bytes 196616 | tf_op jit(solution)/shard_map/ppermute | solution.py:266
  59.8 1.2 %collective-permute-start.7 = (f32[4,4,512]{2,1,0:T(4,128)S(1)}, f32[4,4,512]{2,1,0:T(4,128)S(1)}, u32[]{:S(2)}, u32[]{:S(2)}) collective-permute-start(f32[4,4,512]{2,1,0:T(4,128)S(1)} %get-tuple-element.63.face2), channel_id=1, source_target_pairs={{0,1},{1,0},{2,3},{3,2},{4,5},{5,4},{6,7},{7,6},{8,9},{9,8},{10,11... | collective-permute-start | bytes 98312 | tf_op jit(solution)/shard_map/ppermute | solution.py:268
  62.6 18.2 %all-to-all-start.2 = ((f32[16,49,1,128]{3,2,1,0:T(1,128)}), f32[16,49,1,128]{3,2,1,0:T(1,128)S(1)}, u32[]{:S(2)}, u32[]{:S(2)}) async-start(f32[16,49,1,128]{3,2,1,0:T(1,128)} %bitcast.5), calls=%async_computation.2 | async-start | bytes 802816 | tf_op jit(solution)/shard_map/all_to_all | solution.py:131
  68.4 6.2 %collective-permute-start.8 = (f32[4,8,512]{2,1,0:T(8,128)S(1)}, f32[4,8,512]{2,1,0:T(8,128)S(1)}, u32[]{:S(2)}, u32[]{:S(2)}) collective-permute-start(f32[4,8,512]{2,1,0:T(8,128)S(1)} %get-tuple-element.64.face0), channel_id=1, source_target_pairs={{2,0},{4,2},{6,4},{8,6},{10,8},{12,10},{14,12},{15,14},{1,3},{3,5}... | collective-permute-start | bytes 196616 | tf_op jit(solution)/shard_map/ppermute | solution.py:267

commit v8 on v7

--- a/solution.py
+++ b/solution.py
@@ -538,18 +538,18 @@
             pay3.put_spare(pay, packed_sums([sums[0:1, :], power, sums[2:3, :]]))
 
         own0, own1, own2 = facing(faces)
-        *payload, flow0, flow2 = call(
+        *payload, flow1, flow2 = call(
             outer_kernel,
-            [sums, halo[0], halo[2], own0, own2, weights[0], weights[2], *payload],
+            [sums, halo[1], halo[2], own1, own2, weights[1], weights[2], *payload],
             pay3.shapes + [face_z, face_y],
             "outer_image_of_residual",
         )
         received = pay3.exchange(payload)
 
-        def final_kernel(labels, strength, residual, image, inner, flow0, own1, against, weight1, flow2, scatters, scalars, *refs):
+        def final_kernel(labels, strength, residual, image, inner, flow1, own0, along, weight0, flow2, scatters, scalars, *refs):
             place = whereabouts()
-            arrived, (solution_out, residual_out, solution_field, out, flow1, done) = refs[: pay3.count], refs[pay3.count :]
-            flow1[...] = weight1[...] * (own1[...] - against[...])
+            arrived, (solution_out, residual_out, solution_field, out, flow0, done) = refs[: pay3.count], refs[pay3.count :]
+            flow0[...] = weight0[...] * (own0[...] - along[...])
             copies = []
             norm, whole, cross = unpacked_sums(pay3.get_spare(arrived), 3)
             square, power, step = scalars[0:1, :1], scalars[1:2, :1], scalars[2:3, :1]
@@ -574,7 +574,7 @@
         return tuple(
             call(
                 final_kernel,
-                [labels, strength, residual, image, inner, flow0, own1, halo[1], weights[1], flow2, scatters, scalars, *received],
+                [labels, strength, residual, image, inner, flow1, own0, halo[0], weights[0], flow2, scatters, scalars, *received],
                 [field, field],
                 "solution_and_residual",
                 far_outputs=True,

time: 82.2 us -> 81.8 us (level)
    ppermute x3, waiting for transfers between devices: 5.84 us -> 2.1 us  [swap_faces(): lax.ppermute(against, AXES, [(j, i) for i, j in ring])]
    all_to_all x2, waiting for transfers between devices: 19.1 us -> 21.3 us  [exchange(): lax.all_to_all(packed, AXES, split_axis=0, concat_axis=0, tiled=True)]
    all_to_all x2, starting transfers between devices: 13.3 us -> 11.5 us  [exchange(): lax.all_to_all(packed, AXES, split_axis=0, concat_axis=0, tiled=True)]
    ppermute x3, waiting for transfers between devices: 0.7 us -> 2.09 us  [swap_faces(): lax.ppermute(along, AXES, ring)]
    ppermute x3, starting transfers between devices: 5.52 us -> 6.47 us  [swap_faces(): lax.ppermute(along, AXES, ring)]
where the time goes in v8:
time: 81.8 us; the launch traced here: 81.4 us
  blocking collectives  26.8 us (33%)
  waiting for transfers between devices  25.6 us (31%)
  starting transfers between devices  19.9 us (24%)
  Pallas kernels  8.16 us (10%)
  between operations  0.85 us (1%)
    all_to_all x1, blocking collectives, exchange(): lax.all_to_all(packed, AXES, split_axis=0, concat_axis=0, tiled=True)  26.8 us
    all_to_all x2, waiting for transfers between devices, exchange(): lax.all_to_all(packed, AXES, split_axis=0, concat_axis=0, tiled=True)  21.3 us
    all_to_all x2, starting transfers between devices, exchange(): lax.all_to_all(packed, AXES, split_axis=0, concat_axis=0, tiled=True)  11.5 us
    pallas_call x8, Pallas kernels, call(): pl.pallas_call(kernel, out_shape=outputs, in_specs=[away if far else near...  8.16 us
    ppermute x3, starting transfers between devices, swap_faces(): lax.ppermute(along, AXES, ring)  6.47 us
    ppermute x3, waiting for transfers between devices, swap_faces(): lax.ppermute(against, AXES, [(j, i) for i, j in ring])  2.1 us
    ppermute x3, waiting for transfers between devices, swap_faces(): lax.ppermute(along, AXES, ring)  2.09 us
  transfers between devices with their start and end apart: 11, of which 5 were waited for; matrix products, arithmetic and copies ran while one was open for 0% of the time, Pallas kernels for 3%

profile of v8, /device:TPU:0, one launch (start us, length us, event | category | flops | bytes accessed | tf_op | source)
XLA Modules:
  0.0 81.4 jit_solution(14120430661654039738)
XLA Ops:
  0.6 2.9 %send_blocks.1 = (f32[1552,128]{1,0:T(8,128)}, f32[8,128]{1,0:T(8,128)}, f32[4,8,512]{2,1,0:T(8,128)}, f32[4,8,512]{2,1,0:T(8,128)}, f32[4,4,512]{2,1,0:T(4,128)...) custom-call(s32[3,4,4,8]{3,2,1,0:T(4,128)} %bitcast.13, f32[4,4,8,512]{3,2,1,0:T(8,128)} %shade.5, ...), custom_call_target="tpu_custom_call" | custom-call | tf_op jit(solution)/shard_map/send_blocks/pallas_call | solution.py:141
  3.5 0.0 copy-start.7
  3.5 0.0 copy-start.4
  3.5 0.0 copy-start.3
  3.5 0.0 copy-start.6
  3.6 0.0 copy-start.5
  3.6 0.0 copy-start.8
  3.6 0.0 copy-start
  3.6 0.0 copy-start.1
  3.6 0.0 copy-start.2
  3.6 7.5 %all-to-all-start = ((f32[16,97,1,128]{3,2,1,0:T(1,128)}), f32[16,97,1,128]{3,2,1,0:T(1,128)S(1)}, u32[]{:S(2)}, u32[]{:S(2)}) async-start(f32[16,97,1,128]{3,2,1,0:T(1,128)} %bitcast.12), calls=%async_computation | async-start | bytes 1589248 | tf_op jit(solution)/shard_map/all_to_all | solution.py:131
  11.1 0.0 copy-done.7
  11.2 0.5 collective-permute-start.2
  11.6 0.0 copy-done.4
  11.6 0.1 collective-permute-start.1
  11.7 0.0 copy-done.3
  11.7 1.9 %collective-permute-start = (f32[4,8,512]{2,1,0:T(8,128)S(1)}, f32[4,8,512]{2,1,0:T(8,128)S(1)}, u32[]{:S(2)}, u32[]{:S(2)}) collective-permute-start(f32[4,8,512]{2,1,0:T(8,128)S(1)} %copy-done.3), channel_id=1, source_target_pairs={{0,2},{2,4},{4,6},{6,8},{8,10},{10,12},{12,14},{14,15},{3,1},{5,3}... | collective-permute-start | bytes 196616 | tf_op jit(solution)/shard_map/ppermute | solution.py:266
  13.7 0.0 copy-done.6
  13.7 0.0 collective-permute-start.4
  13.7 0.0 copy-done.5
  13.7 2.6 %collective-permute-start.3 = (f32[4,8,512]{2,1,0:T(8,128)S(1)}, f32[4,8,512]{2,1,0:T(8,128)S(1)}, u32[]{:S(2)}, u32[]{:S(2)}) collective-permute-start(f32[4,8,512]{2,1,0:T(8,128)S(1)} %copy-done.5), channel_id=1, source_target_pairs={{0,2},{2,4},{4,6},{6,8},{8,10},{10,12},{12,14},{14,15},{3,1},{5,3}... | collective-permute-start | bytes 196616 | tf_op jit(solution)/shard_map/ppermute | solution.py:266
  16.3 0.0 collective-permute-done.2.refs_5_
  16.3 0.0 copy-done.8
  16.3 0.0 collective-permute-start.5
  16.3 0.0 copy-done
  16.3 0.0 copy-done.1
  16.3 0.6 inner_image_of_right.1
  17.0 13.0 %all-to-all-done = f32[16,97,1,128]{3,2,1,0:T(1,128)S(1)} async-done(((f32[16,97,1,128]{3,2,1,0:T(1,128)}), f32[16,97,1,128]{3,2,1,0:T(1,128)S(1)}, u32[]{:S(2)}, u32[]{:S(2)}) %all-to-all-start) | async-done | bytes 794656 | tf_op jit(solution)/shard_map/all_to_all | solution.py:131
  30.0 1.3 %flux_of_right.1 = (f32[1552,128]{1,0:T(8,128)S(1)}, f32[3,128,128]{2,1,0:T(8,128)S(1)}, f32[3,128,128]{2,1,0:T(8,128)S(1)}, f32[3,128,128]{2,1,0:T(8,128)S(1)},...) custom-call(f32[4,4,8,512]{3,2,1,0:T(8,128)S(1)} %copy-done.2, s32[4,4,8,512]{3,2,1,0:T(8,128)S(1)} %copy-done, ...), custom_call_target="tpu_custom_call" | custom-call | tf_op jit(solution)/shard_map/flux_of_right/pallas_call | solution.py:141
  31.3 0.0 collective-permute-done.5.refs_11_
  31.3 0.0 collective-permute-done.1.refs_4_
  31.3 0.0 collective-permute-done.refs_3_
  31.4 0.0 collective-permute-done.4.refs_10_
  31.4 0.0 collective-permute-done.3.refs_9_
  31.4 0.4 image_of_right.1
  31.8 26.8 %all_to_all.15 = f32[16,97,1,128]{3,2,1,0:T(1,128)S(1)} all-to-all(f32[16,97,1,128]{3,2,1,0:T(1,128)S(1)} %bitcast.11), channel_id=1, replica_groups=mesh['grp'=2,'slc'=8,'row'=2] {'slc','row'}, dimensions={0} | all-to-all | bytes 1589248 | tf_op jit(solution)/shard_map/all_to_all | solution.py:131
  58.5 0.3 first_residual.1
  58.8 0.8 %collective-permute-start.6 = (f32[4,8,512]{2,1,0:T(8,128)S(1)}, f32[4,8,512]{2,1,0:T(8,128)S(1)}, u32[]{:S(2)}, u32[]{:S(2)}) collective-permute-start(f32[4,8,512]{2,1,0:T(8,128)S(1)} %get-tuple-element.62.own0), channel_id=1, source_target_pairs={{2,0},{4,2},{6,4},{8,6},{10,8},{12,10},{14,12},{15,14},{1,3},{3,5}... | collective-permute-start | bytes 196616 | tf_op jit(solution)/shard_map/ppermute | solution.py:267
  59.6 0.5 collective-permute-start.7
  60.2 0.7 inner_image_of_residual.1
  60.9 0.1 collective-permute-done.7.beside
  61.0 2.1 %collective-permute-done.6.along = f32[4,8,512]{2,1,0:T(8,128)S(1)} collective-permute-done((f32[4,8,512]{2,1,0:T(8,128)S(1)}, f32[4,8,512]{2,1,0:T(8,128)S(1)}, u32[]{:S(2)}, u32[]{:S(2)}) %collective-permute-start.6) | collective-permute-done | bytes 65568 | tf_op jit(solution)/shard_map/ppermute | solution.py:267
  63.1 0.9 %outer_image_of_residual.1 = (f32[784,128]{1,0:T(8,128)}, f32[4,8,512]{2,1,0:T(8,128)S(1)}, f32[4,4,512]{2,1,0:T(4,128)S(1)}) custom-call(f32[8,128]{1,0:T(8,128)S(1)} %get-tuple-element.61.sums, f32[4,8,512]{2,1,0:T(8,128)S(1)} %collective-permute-done.6.along, f32[4,4,512]{2,1,0:T(4,128)S(1)} %collective-permute-done.7.beside, ...), custom_call_target="tpu_custom_call" | custom-call | tf_op jit(solution)/shard_map/outer_image_of_residual/pallas_call | solution.py:141
  64.0 4.0 %all-to-all-start.2 = ((f32[16,49,1,128]{3,2,1,0:T(1,128)}), f32[16,49,1,128]{3,2,1,0:T(1,128)S(1)}, u32[]{:S(2)}, u32[]{:S(2)}) async-start(f32[16,49,1,128]{3,2,1,0:T(1,128)} %bitcast.5), calls=%async_computation.2 | async-start | bytes 802816 | tf_op jit(solution)/shard_map/all_to_all | solution.py:131
  68.0 1.9 %collective-permute-start.8 = (f32[4,8,512]{2,1,0:T(8,128)S(1)}, f32[4,8,512]{2,1,0:T(8,128)S(1)}, u32[]{:S(2)}, u32[]{:S(2)}) collective-permute-start(f32[4,8,512]{2,1,0:T(8,128)S(1)} %get-tuple-element.64.face0), channel_id=1, source_target_pairs={{0,2},{2,4},{4,6},{6,8},{8,10},{10,12},{12,14},{14,15},{3,1},{5,3}... | collective-permute-start | bytes 196616 | tf_op jit(solution)/shard_map/ppermute | solution.py:266
  69.9 2.1 %collective-permute-done.8.along = f32[4,8,512]{2,1,0:T(8,128)S(1)} collective-permute-done((f32[4,8,512]{2,1,0:T(8,128)S(1)}, f32[4,8,512]{2,1,0:T(8,128)S(1)}, u32[]{:S(2)}, u32[]{:S(2)}) %collective-permute-start.8) | collective-permute-done | bytes 65568 | tf_op jit(solution)/shard_map/ppermute | solution.py:266
  72.0 8.3 %all-to-all-done.2 = f32[16,49,1,128]{3,2,1,0:T(1,128)S(1)} async-done(((f32[16,49,1,128]{3,2,1,0:T(1,128)}), f32[16,49,1,128]{3,2,1,0:T(1,128)S(1)}, u32[]{:S(2)}, u32[]{:S(2)}) %all-to-all-start.2) | async-done | bytes 401440 | tf_op jit(solution)/shard_map/all_to_all | solution.py:131
  80.3 1.1 %solution_and_residual.1 = (f32[4,4,8,512]{3,2,1,0:T(8,128)}, f32[4,4,8,512]{3,2,1,0:T(8,128)}) custom-call(s32[4,4,8,512]{3,2,1,0:T(8,128)S(1)} %copy-done, f32[4,4,8,512]{3,2,1,0:T(8,128)S(1)} %copy-done.1, f32[4,4,8,512]{3,2,1,0:T(8,128)S(1)} %get-tuple-element.54.residual, f32[4,4,8,512]{3,2,1,0:T(8,128)S(1)} %get-tuple-element.55.image, ...), custom_call_target="tpu_custom_call" | custom-call | tf_op jit(solution)/shard_map/solution_and_residual/pallas_call | solution.py:141
  (3 shorter events, 0.0 us)
Async XLA Ops:
  3.5 7.6 %copy-start.7 = (f32[4,4,512]{2,1,0:T(4,128)S(1)}, f32[4,4,512]{2,1,0:T(4,128)}, u32[]{:S(2)}) copy-start(f32[4,4,512]{2,1,0:T(4,128)} %get-tuple-element.46.refs_2_) | copy-start | bytes 98308
  3.5 8.1 %copy-start.4 = (f32[4,8,512]{2,1,0:T(8,128)S(1)}, f32[4,8,512]{2,1,0:T(8,128)}, u32[]{:S(2)}) copy-start(f32[4,8,512]{2,1,0:T(8,128)} %get-tuple-element.44.refs_0_) | copy-start | bytes 196612
  3.5 8.2 %copy-start.3 = (f32[4,8,512]{2,1,0:T(8,128)S(1)}, f32[4,8,512]{2,1,0:T(8,128)}, u32[]{:S(2)}) copy-start(f32[4,8,512]{2,1,0:T(8,128)} %get-tuple-element.45.refs_1_) | copy-start | bytes 196612
  3.5 10.1 %copy-start.6 = (f32[4,8,512]{2,1,0:T(8,128)S(1)}, f32[4,8,512]{2,1,0:T(8,128)}, u32[]{:S(2)}) copy-start(f32[4,8,512]{2,1,0:T(8,128)} %get-tuple-element.47.refs_6_) | copy-start | bytes 196612
  3.6 10.1 %copy-start.5 = (f32[4,8,512]{2,1,0:T(8,128)S(1)}, f32[4,8,512]{2,1,0:T(8,128)}, u32[]{:S(2)}) copy-start(f32[4,8,512]{2,1,0:T(8,128)} %get-tuple-element.48.refs_7_) | copy-start | bytes 196612
  3.6 12.7 %copy-start.8 = (f32[4,4,512]{2,1,0:T(4,128)S(1)}, f32[4,4,512]{2,1,0:T(4,128)}, u32[]{:S(2)}) copy-start(f32[4,4,512]{2,1,0:T(4,128)} %get-tuple-element.49.refs_8_) | copy-start | bytes 98308
  3.6 12.7 %copy-start = (s32[4,4,8,512]{3,2,1,0:T(8,128)S(1)}, s32[4,4,8,512]{3,2,1,0:T(8,128)}, u32[]{:S(2)}) copy-start(s32[4,4,8,512]{3,2,1,0:T(8,128)} %labels.9) | copy-start | bytes 786436
  3.6 12.7 %copy-start.1 = (f32[4,4,8,512]{3,2,1,0:T(8,128)S(1)}, f32[4,4,8,512]{3,2,1,0:T(8,128)}, u32[]{:S(2)}) copy-start(f32[4,4,8,512]{3,2,1,0:T(8,128)} %strength.9) | copy-start | bytes 786436
  3.6 12.7 %copy-start.2 = (f32[4,4,8,512]{3,2,1,0:T(8,128)S(1)}, f32[4,4,8,512]{3,2,1,0:T(8,128)}, u32[]{:S(2)}) copy-start(f32[4,4,8,512]{3,2,1,0:T(8,128)} %shade.5) | copy-start | bytes 786436
  3.6 26.4 %all-to-all-start = ((f32[16,97,1,128]{3,2,1,0:T(1,128)}), f32[16,97,1,128]{3,2,1,0:T(1,128)S(1)}, u32[]{:S(2)}, u32[]{:S(2)}) async-start(f32[16,97,1,128]{3,2,1,0:T(1,128)} %bitcast.12), calls=%async_computation | async-start | bytes 1589248 | tf_op jit(solution)/shard_map/all_to_all | solution.py:131
  11.2 5.1 %collective-permute-start.2 = (f32[4,4,512]{2,1,0:T(4,128)S(1)}, f32[4,4,512]{2,1,0:T(4,128)S(1)}, u32[]{:S(2)}, u32[]{:S(2)}) collective-permute-start(f32[4,4,512]{2,1,0:T(4,128)S(1)} %copy-done.7), channel_id=1, source_target_pairs={{0,1},{1,0},{2,3},{3,2},{4,5},{5,4},{6,7},{7,6},{8,9},{9,8},{10,11... | collective-permute-start | bytes 98312 | tf_op jit(solution)/shard_map/ppermute | solution.py:268
  11.6 19.7 %collective-permute-start.1 = (f32[4,8,512]{2,1,0:T(8,128)S(1)}, f32[4,8,512]{2,1,0:T(8,128)S(1)}, u32[]{:S(2)}, u32[]{:S(2)}) collective-permute-start(f32[4,8,512]{2,1,0:T(8,128)S(1)} %copy-done.4), channel_id=1, source_target_pairs={{2,0},{4,2},{6,4},{8,6},{10,8},{12,10},{14,12},{15,14},{1,3},{3,5}... | collective-permute-start | bytes 196616 | tf_op jit(solution)/shard_map/ppermute | solution.py:267
  11.7 4.6 %copy-start.9 = (f32[8,128]{1,0:T(8,128)S(1)}, f32[8,128]{1,0:T(8,128)}, u32[]{:S(2)}) copy-start(f32[8,128]{1,0:T(8,128)} %get-tuple-element.37.slot_tile) | copy-start | bytes 12292
  11.7 19.6 %collective-permute-start = (f32[4,8,512]{2,1,0:T(8,128)S(1)}, f32[4,8,512]{2,1,0:T(8,128)S(1)}, u32[]{:S(2)}, u32[]{:S(2)}) collective-permute-start(f32[4,8,512]{2,1,0:T(8,128)S(1)} %copy-done.3), channel_id=1, source_target_pairs={{0,2},{2,4},{4,6},{6,8},{8,10},{10,12},{12,14},{14,15},{3,1},{5,3}... | collective-permute-start | bytes 196616 | tf_op jit(solution)/shard_map/ppermute | solution.py:266
  13.7 17.7 %collective-permute-start.4 = (f32[4,8,512]{2,1,0:T(8,128)S(1)}, f32[4,8,512]{2,1,0:T(8,128)S(1)}, u32[]{:S(2)}, u32[]{:S(2)}) collective-permute-start(f32[4,8,512]{2,1,0:T(8,128)S(1)} %copy-done.6), channel_id=1, source_target_pairs={{2,0},{4,2},{6,4},{8,6},{10,8},{12,10},{14,12},{15,14},{1,3},{3,5}... | collective-permute-start | bytes 196616 | tf_op jit(solution)/shard_map/ppermute | solution.py:267
  13.7 17.7 %collective-permute-start.3 = (f32[4,8,512]{2,1,0:T(8,128)S(1)}, f32[4,8,512]{2,1,0:T(8,128)S(1)}, u32[]{:S(2)}, u32[]{:S(2)}) collective-permute-start(f32[4,8,512]{2,1,0:T(8,128)S(1)} %copy-done.5), channel_id=1, source_target_pairs={{0,2},{2,4},{4,6},{6,8},{8,10},{10,12},{12,14},{14,15},{3,1},{5,3}... | collective-permute-start | bytes 196616 | tf_op jit(solution)/shard_map/ppermute | solution.py:266
  16.3 15.0 %collective-permute-start.5 = (f32[4,4,512]{2,1,0:T(4,128)S(1)}, f32[4,4,512]{2,1,0:T(4,128)S(1)}, u32[]{:S(2)}, u32[]{:S(2)}) collective-permute-start(f32[4,4,512]{2,1,0:T(4,128)S(1)} %copy-done.8), channel_id=1, source_target_pairs={{0,1},{1,0},{2,3},{3,2},{4,5},{5,4},{6,7},{7,6},{8,9},{9,8},{10,11... | collective-permute-start | bytes 98312 | tf_op jit(solution)/shard_map/ppermute | solution.py:268
  58.8 4.3 %collective-permute-start.6 = (f32[4,8,512]{2,1,0:T(8,128)S(1)}, f32[4,8,512]{2,1,0:T(8,128)S(1)}, u32[]{:S(2)}, u32[]{:S(2)}) collective-permute-start(f32[4,8,512]{2,1,0:T(8,128)S(1)} %get-tuple-element.62.own0), channel_id=1, source_target_pairs={{2,0},{4,2},{6,4},{8,6},{10,8},{12,10},{14,12},{15,14},{1,3},{3,5}... | collective-permute-start | bytes 196616 | tf_op jit(solution)/shard_map/ppermute | solution.py:267
  59.6 1.4 %collective-permute-start.7 = (f32[4,4,512]{2,1,0:T(4,128)S(1)}, f32[4,4,512]{2,1,0:T(4,128)S(1)}, u32[]{:S(2)}, u32[]{:S(2)}) collective-permute-start(f32[4,4,512]{2,1,0:T(4,128)S(1)} %get-tuple-element.63.face2), channel_id=1, source_target_pairs={{0,1},{1,0},{2,3},{3,2},{4,5},{5,4},{6,7},{7,6},{8,9},{9,8},{10,11... | collective-permute-start | bytes 98312 | tf_op jit(solution)/shard_map/ppermute | solution.py:268
  64.0 16.3 %all-to-all-start.2 = ((f32[16,49,1,128]{3,2,1,0:T(1,128)}), f32[16,49,1,128]{3,2,1,0:T(1,128)S(1)}, u32[]{:S(2)}, u32[]{:S(2)}) async-start(f32[16,49,1,128]{3,2,1,0:T(1,128)} %bitcast.5), calls=%async_computation.2 | async-start | bytes 802816 | tf_op jit(solution)/shard_map/all_to_all | solution.py:131
  68.0 4.0 %collective-permute-start.8 = (f32[4,8,512]{2,1,0:T(8,128)S(1)}, f32[4,8,512]{2,1,0:T(8,128)S(1)}, u32[]{:S(2)}, u32[]{:S(2)}) collective-permute-start(f32[4,8,512]{2,1,0:T(8,128)S(1)} %get-tuple-element.64.face0), channel_id=1, source_target_pairs={{0,2},{2,4},{4,6},{6,8},{8,10},{10,12},{12,14},{14,15},{3,1},{5,3}... | collective-permute-start | bytes 196616 | tf_op jit(solution)/shard_map/ppermute | solution.py:266

commit v9 on v8

--- a/solution.py
+++ b/solution.py
@@ -84,6 +84,7 @@
         self.owners, self.capacity, self.pieces = owners, capacity, pieces
         self.fused = capacity % SUBLANES == 0
         self.rows = pieces * capacity
+        self.pitch = self.rows + 1
         if self.fused:
             self.shapes = [jax.ShapeDtypeStruct((owners * (self.rows + 1), LANES), F32)]
         else:
@@ -93,12 +94,12 @@
             ]
         self.count = len(self.shapes)
 
-    def put(self, refs, piece, values):
+    def put(self, refs, piece, values, start=0, some=None):
         if not self.fused:
             refs[0][piece] = values
             return
-        for owner in range(self.owners):
-            first = owner * (self.rows + 1) + piece * self.capacity
+        for owner in range(self.owners if some is None else some):
+            first = (start + owner) * self.pitch + piece * self.capacity
             refs[0][first : first + self.capacity, :] = values[owner * self.capacity : (owner + 1) * self.capacity]
 
     def get(self, refs, piece):
@@ -328,12 +329,20 @@
             gone = Sender(sent)
             for k in range(pay1.count, count):
                 gone.start(held[k], targets[k])
-            for t in range(links):
-                both = pick(gather_matrix(slot_rows[t], slots), jnp.concatenate([to_blocks(shade[t]), to_blocks(rights[t])], axis=1))
-                pay1.put(pay, t, both[:, :LANES])
-                pay1.put(pay, links + t, both[:, LANES:])
-            for k in range(pay1.count):
-                gone.start(held[k], targets[k], 8)
+            pieces = [jnp.concatenate([to_blocks(shade[t]), to_blocks(rights[t])], axis=1) for t in range(links)]
+            parts = 2 if pay1.fused and owners // 2 * pay1.pitch % SUBLANES == 0 else 1
+            some = owners // parts
+            for first in range(0, owners, some):
+                for t in range(links):
+                    both = pick(same(iota((some * capacity, LANES), 0) + first * capacity, slot_rows[t]), pieces[t])
+                    pay1.put(pay, t, both[:, :LANES], first, some)
+                    pay1.put(pay, links + t, both[:, LANES:], first, some)
+                if parts > 1:
+                    rows = pl.ds(first * pay1.pitch, some * pay1.pitch)
+                    gone.start(pay[0].at[rows], targets[0].at[rows], 4)
+            if parts == 1:
+                for k in range(pay1.count):
+                    gone.start(held[k], targets[k], 8)
             gone.wait()
 
         send_outputs = pay1.shapes + [tile] + [face_z, face_z, face_y] * 2

time: 81.8 us -> 81.7 us (level)
  no operation moved by 1% of the time
where the time goes in v9:
time: 81.7 us; the launch traced here: 81.3 us
  blocking collectives  26.8 us (33%)
  waiting for transfers between devices  25.6 us (31%)
  starting transfers between devices  19.9 us (24%)
  Pallas kernels  8.08 us (10%)
  between operations  0.85 us (1%)
    all_to_all x1, blocking collectives, exchange(): lax.all_to_all(packed, AXES, split_axis=0, concat_axis=0, tiled=True)  26.8 us
    all_to_all x2, waiting for transfers between devices, exchange(): lax.all_to_all(packed, AXES, split_axis=0, concat_axis=0, tiled=True)  21.3 us
    all_to_all x2, starting transfers between devices, exchange(): lax.all_to_all(packed, AXES, split_axis=0, concat_axis=0, tiled=True)  11.5 us
    pallas_call x8, Pallas kernels, call(): pl.pallas_call(kernel, out_shape=outputs, in_specs=[away if far else near...  8.08 us
    ppermute x3, starting transfers between devices, swap_faces(): lax.ppermute(along, AXES, ring)  6.47 us
    ppermute x3, waiting for transfers between devices, swap_faces(): lax.ppermute(against, AXES, [(j, i) for i, j in ring])  2.1 us
    ppermute x3, waiting for transfers between devices, swap_faces(): lax.ppermute(along, AXES, ring)  2.09 us
  transfers between devices with their start and end apart: 11, of which 5 were waited for; matrix products, arithmetic and copies ran while one was open for 0% of the time, Pallas kernels for 3%

profile of v9, /device:TPU:0, one launch (start us, length us, event | category | flops | bytes accessed | tf_op | source)
XLA Modules:
  0.0 81.3 jit_solution(2432850102117100738)
XLA Ops:
  0.6 2.8 %send_blocks.1 = (f32[1552,128]{1,0:T(8,128)}, f32[8,128]{1,0:T(8,128)}, f32[4,8,512]{2,1,0:T(8,128)}, f32[4,8,512]{2,1,0:T(8,128)}, f32[4,4,512]{2,1,0:T(4,128)...) custom-call(s32[3,4,4,8]{3,2,1,0:T(4,128)} %bitcast.13, f32[4,4,8,512]{3,2,1,0:T(8,128)} %shade.5, ...), custom_call_target="tpu_custom_call" | custom-call | tf_op jit(solution)/shard_map/send_blocks/pallas_call | solution.py:142
  3.4 0.0 copy-start.7
  3.4 0.0 copy-start.4
  3.4 0.0 copy-start.3
  3.5 0.0 copy-start.6
  3.5 0.0 copy-start.5
  3.5 0.0 copy-start.8
  3.5 0.0 copy-start
  3.5 0.0 copy-start.1
  3.5 0.0 copy-start.2
  3.5 7.5 %all-to-all-start = ((f32[16,97,1,128]{3,2,1,0:T(1,128)}), f32[16,97,1,128]{3,2,1,0:T(1,128)S(1)}, u32[]{:S(2)}, u32[]{:S(2)}) async-start(f32[16,97,1,128]{3,2,1,0:T(1,128)} %bitcast.12), calls=%async_computation | async-start | bytes 1589248 | tf_op jit(solution)/shard_map/all_to_all | solution.py:132
  11.1 0.0 copy-done.7
  11.1 0.5 collective-permute-start.2
  11.5 0.0 copy-done.4
  11.5 0.1 collective-permute-start.1
  11.6 0.0 copy-done.3
  11.6 1.9 %collective-permute-start = (f32[4,8,512]{2,1,0:T(8,128)S(1)}, f32[4,8,512]{2,1,0:T(8,128)S(1)}, u32[]{:S(2)}, u32[]{:S(2)}) collective-permute-start(f32[4,8,512]{2,1,0:T(8,128)S(1)} %copy-done.3), channel_id=1, source_target_pairs={{0,2},{2,4},{4,6},{6,8},{8,10},{10,12},{12,14},{14,15},{3,1},{5,3}... | collective-permute-start | bytes 196616 | tf_op jit(solution)/shard_map/ppermute | solution.py:267
  13.6 0.0 copy-done.6
  13.6 0.0 collective-permute-start.4
  13.6 0.0 copy-done.5
  13.6 2.6 %collective-permute-start.3 = (f32[4,8,512]{2,1,0:T(8,128)S(1)}, f32[4,8,512]{2,1,0:T(8,128)S(1)}, u32[]{:S(2)}, u32[]{:S(2)}) collective-permute-start(f32[4,8,512]{2,1,0:T(8,128)S(1)} %copy-done.5), channel_id=1, source_target_pairs={{0,2},{2,4},{4,6},{6,8},{8,10},{10,12},{12,14},{14,15},{3,1},{5,3}... | collective-permute-start | bytes 196616 | tf_op jit(solution)/shard_map/ppermute | solution.py:267
  16.2 0.0 collective-permute-done.2.refs_5_
  16.2 0.0 copy-done.8
  16.2 0.0 collective-permute-start.5
  16.2 0.0 copy-done
  16.2 0.0 copy-done.1
  16.3 0.6 inner_image_of_right.1
  16.9 13.0 %all-to-all-done = f32[16,97,1,128]{3,2,1,0:T(1,128)S(1)} async-done(((f32[16,97,1,128]{3,2,1,0:T(1,128)}), f32[16,97,1,128]{3,2,1,0:T(1,128)S(1)}, u32[]{:S(2)}, u32[]{:S(2)}) %all-to-all-start) | async-done | bytes 794656 | tf_op jit(solution)/shard_map/all_to_all | solution.py:132
  29.9 1.3 %flux_of_right.1 = (f32[1552,128]{1,0:T(8,128)S(1)}, f32[3,128,128]{2,1,0:T(8,128)S(1)}, f32[3,128,128]{2,1,0:T(8,128)S(1)}, f32[3,128,128]{2,1,0:T(8,128)S(1)},...) custom-call(f32[4,4,8,512]{3,2,1,0:T(8,128)S(1)} %copy-done.2, s32[4,4,8,512]{3,2,1,0:T(8,128)S(1)} %copy-done, ...), custom_call_target="tpu_custom_call" | custom-call | tf_op jit(solution)/shard_map/flux_of_right/pallas_call | solution.py:142
  31.2 0.0 collective-permute-done.5.refs_11_
  31.2 0.0 collective-permute-done.1.refs_4_
  31.2 0.0 collective-permute-done.refs_3_
  31.3 0.0 collective-permute-done.4.refs_10_
  31.3 0.0 collective-permute-done.3.refs_9_
  31.3 0.4 image_of_right.1
  31.7 26.8 %all_to_all.15 = f32[16,97,1,128]{3,2,1,0:T(1,128)S(1)} all-to-all(f32[16,97,1,128]{3,2,1,0:T(1,128)S(1)} %bitcast.11), channel_id=1, replica_groups=mesh['grp'=2,'slc'=8,'row'=2] {'slc','row'}, dimensions={0} | all-to-all | bytes 1589248 | tf_op jit(solution)/shard_map/all_to_all | solution.py:132
  58.4 0.3 first_residual.1
  58.7 0.8 %collective-permute-start.6 = (f32[4,8,512]{2,1,0:T(8,128)S(1)}, f32[4,8,512]{2,1,0:T(8,128)S(1)}, u32[]{:S(2)}, u32[]{:S(2)}) collective-permute-start(f32[4,8,512]{2,1,0:T(8,128)S(1)} %get-tuple-element.62.own0), channel_id=1, source_target_pairs={{2,0},{4,2},{6,4},{8,6},{10,8},{12,10},{14,12},{15,14},{1,3},{3,5}... | collective-permute-start | bytes 196616 | tf_op jit(solution)/shard_map/ppermute | solution.py:268
  59.5 0.5 collective-permute-start.7
  60.1 0.7 inner_image_of_residual.1
  60.8 0.1 collective-permute-done.7.beside
  60.9 2.1 %collective-permute-done.6.along = f32[4,8,512]{2,1,0:T(8,128)S(1)} collective-permute-done((f32[4,8,512]{2,1,0:T(8,128)S(1)}, f32[4,8,512]{2,1,0:T(8,128)S(1)}, u32[]{:S(2)}, u32[]{:S(2)}) %collective-permute-start.6) | collective-permute-done | bytes 65568 | tf_op jit(solution)/shard_map/ppermute | solution.py:268
  63.0 0.9 %outer_image_of_residual.1 = (f32[784,128]{1,0:T(8,128)}, f32[4,8,512]{2,1,0:T(8,128)S(1)}, f32[4,4,512]{2,1,0:T(4,128)S(1)}) custom-call(f32[8,128]{1,0:T(8,128)S(1)} %get-tuple-element.61.sums, f32[4,8,512]{2,1,0:T(8,128)S(1)} %collective-permute-done.6.along, f32[4,4,512]{2,1,0:T(4,128)S(1)} %collective-permute-done.7.beside, ...), custom_call_target="tpu_custom_call" | custom-call | tf_op jit(solution)/shard_map/outer_image_of_residual/pallas_call | solution.py:142
  63.9 4.0 %all-to-all-start.2 = ((f32[16,49,1,128]{3,2,1,0:T(1,128)}), f32[16,49,1,128]{3,2,1,0:T(1,128)S(1)}, u32[]{:S(2)}, u32[]{:S(2)}) async-start(f32[16,49,1,128]{3,2,1,0:T(1,128)} %bitcast.5), calls=%async_computation.2 | async-start | bytes 802816 | tf_op jit(solution)/shard_map/all_to_all | solution.py:132
  67.9 1.9 %collective-permute-start.8 = (f32[4,8,512]{2,1,0:T(8,128)S(1)}, f32[4,8,512]{2,1,0:T(8,128)S(1)}, u32[]{:S(2)}, u32[]{:S(2)}) collective-permute-start(f32[4,8,512]{2,1,0:T(8,128)S(1)} %get-tuple-element.64.face0), channel_id=1, source_target_pairs={{0,2},{2,4},{4,6},{6,8},{8,10},{10,12},{12,14},{14,15},{3,1},{5,3}... | collective-permute-start | bytes 196616 | tf_op jit(solution)/shard_map/ppermute | solution.py:267
  69.8 2.1 %collective-permute-done.8.along = f32[4,8,512]{2,1,0:T(8,128)S(1)} collective-permute-done((f32[4,8,512]{2,1,0:T(8,128)S(1)}, f32[4,8,512]{2,1,0:T(8,128)S(1)}, u32[]{:S(2)}, u32[]{:S(2)}) %collective-permute-start.8) | collective-permute-done | bytes 65568 | tf_op jit(solution)/shard_map/ppermute | solution.py:267
  71.9 8.3 %all-to-all-done.2 = f32[16,49,1,128]{3,2,1,0:T(1,128)S(1)} async-done(((f32[16,49,1,128]{3,2,1,0:T(1,128)}), f32[16,49,1,128]{3,2,1,0:T(1,128)S(1)}, u32[]{:S(2)}, u32[]{:S(2)}) %all-to-all-start.2) | async-done | bytes 401440 | tf_op jit(solution)/shard_map/all_to_all | solution.py:132
  80.2 1.1 %solution_and_residual.1 = (f32[4,4,8,512]{3,2,1,0:T(8,128)}, f32[4,4,8,512]{3,2,1,0:T(8,128)}) custom-call(s32[4,4,8,512]{3,2,1,0:T(8,128)S(1)} %copy-done, f32[4,4,8,512]{3,2,1,0:T(8,128)S(1)} %copy-done.1, f32[4,4,8,512]{3,2,1,0:T(8,128)S(1)} %get-tuple-element.54.residual, f32[4,4,8,512]{3,2,1,0:T(8,128)S(1)} %get-tuple-element.55.image, ...), custom_call_target="tpu_custom_call" | custom-call | tf_op jit(solution)/shard_map/solution_and_residual/pallas_call | solution.py:142
  (3 shorter events, 0.0 us)
Async XLA Ops:
  3.4 7.6 %copy-start.7 = (f32[4,4,512]{2,1,0:T(4,128)S(1)}, f32[4,4,512]{2,1,0:T(4,128)}, u32[]{:S(2)}) copy-start(f32[4,4,512]{2,1,0:T(4,128)} %get-tuple-element.46.refs_2_) | copy-start | bytes 98308
  3.4 8.1 %copy-start.4 = (f32[4,8,512]{2,1,0:T(8,128)S(1)}, f32[4,8,512]{2,1,0:T(8,128)}, u32[]{:S(2)}) copy-start(f32[4,8,512]{2,1,0:T(8,128)} %get-tuple-element.44.refs_0_) | copy-start | bytes 196612
  3.4 8.2 %copy-start.3 = (f32[4,8,512]{2,1,0:T(8,128)S(1)}, f32[4,8,512]{2,1,0:T(8,128)}, u32[]{:S(2)}) copy-start(f32[4,8,512]{2,1,0:T(8,128)} %get-tuple-element.45.refs_1_) | copy-start | bytes 196612
  3.5 10.1 %copy-start.6 = (f32[4,8,512]{2,1,0:T(8,128)S(1)}, f32[4,8,512]{2,1,0:T(8,128)}, u32[]{:S(2)}) copy-start(f32[4,8,512]{2,1,0:T(8,128)} %get-tuple-element.47.refs_6_) | copy-start | bytes 196612
  3.5 10.1 %copy-start.5 = (f32[4,8,512]{2,1,0:T(8,128)S(1)}, f32[4,8,512]{2,1,0:T(8,128)}, u32[]{:S(2)}) copy-start(f32[4,8,512]{2,1,0:T(8,128)} %get-tuple-element.48.refs_7_) | copy-start | bytes 196612
  3.5 12.7 %copy-start.8 = (f32[4,4,512]{2,1,0:T(4,128)S(1)}, f32[4,4,512]{2,1,0:T(4,128)}, u32[]{:S(2)}) copy-start(f32[4,4,512]{2,1,0:T(4,128)} %get-tuple-element.49.refs_8_) | copy-start | bytes 98308
  3.5 12.7 %copy-start = (s32[4,4,8,512]{3,2,1,0:T(8,128)S(1)}, s32[4,4,8,512]{3,2,1,0:T(8,128)}, u32[]{:S(2)}) copy-start(s32[4,4,8,512]{3,2,1,0:T(8,128)} %labels.9) | copy-start | bytes 786436
  3.5 12.7 %copy-start.1 = (f32[4,4,8,512]{3,2,1,0:T(8,128)S(1)}, f32[4,4,8,512]{3,2,1,0:T(8,128)}, u32[]{:S(2)}) copy-start(f32[4,4,8,512]{3,2,1,0:T(8,128)} %strength.9) | copy-start | bytes 786436
  3.5 12.7 %copy-start.2 = (f32[4,4,8,512]{3,2,1,0:T(8,128)S(1)}, f32[4,4,8,512]{3,2,1,0:T(8,128)}, u32[]{:S(2)}) copy-start(f32[4,4,8,512]{3,2,1,0:T(8,128)} %shade.5) | copy-start | bytes 786436
  3.5 26.4 %all-to-all-start = ((f32[16,97,1,128]{3,2,1,0:T(1,128)}), f32[16,97,1,128]{3,2,1,0:T(1,128)S(1)}, u32[]{:S(2)}, u32[]{:S(2)}) async-start(f32[16,97,1,128]{3,2,1,0:T(1,128)} %bitcast.12), calls=%async_computation | async-start | bytes 1589248 | tf_op jit(solution)/shard_map/all_to_all | solution.py:132
  11.1 5.1 %collective-permute-start.2 = (f32[4,4,512]{2,1,0:T(4,128)S(1)}, f32[4,4,512]{2,1,0:T(4,128)S(1)}, u32[]{:S(2)}, u32[]{:S(2)}) collective-permute-start(f32[4,4,512]{2,1,0:T(4,128)S(1)} %copy-done.7), channel_id=1, source_target_pairs={{0,1},{1,0},{2,3},{3,2},{4,5},{5,4},{6,7},{7,6},{8,9},{9,8},{10,11... | collective-permute-start | bytes 98312 | tf_op jit(solution)/shard_map/ppermute | solution.py:269
  11.5 19.7 %collective-permute-start.1 = (f32[4,8,512]{2,1,0:T(8,128)S(1)}, f32[4,8,512]{2,1,0:T(8,128)S(1)}, u32[]{:S(2)}, u32[]{:S(2)}) collective-permute-start(f32[4,8,512]{2,1,0:T(8,128)S(1)} %copy-done.4), channel_id=1, source_target_pairs={{2,0},{4,2},{6,4},{8,6},{10,8},{12,10},{14,12},{15,14},{1,3},{3,5}... | collective-permute-start | bytes 196616 | tf_op jit(solution)/shard_map/ppermute | solution.py:268
  11.6 4.6 %copy-start.9 = (f32[8,128]{1,0:T(8,128)S(1)}, f32[8,128]{1,0:T(8,128)}, u32[]{:S(2)}) copy-start(f32[8,128]{1,0:T(8,128)} %get-tuple-element.37.slot_tile) | copy-start | bytes 12292
  11.6 19.6 %collective-permute-start = (f32[4,8,512]{2,1,0:T(8,128)S(1)}, f32[4,8,512]{2,1,0:T(8,128)S(1)}, u32[]{:S(2)}, u32[]{:S(2)}) collective-permute-start(f32[4,8,512]{2,1,0:T(8,128)S(1)} %copy-done.3), channel_id=1, source_target_pairs={{0,2},{2,4},{4,6},{6,8},{8,10},{10,12},{12,14},{14,15},{3,1},{5,3}... | collective-permute-start | bytes 196616 | tf_op jit(solution)/shard_map/ppermute | solution.py:267
  13.6 17.7 %collective-permute-start.4 = (f32[4,8,512]{2,1,0:T(8,128)S(1)}, f32[4,8,512]{2,1,0:T(8,128)S(1)}, u32[]{:S(2)}, u32[]{:S(2)}) collective-permute-start(f32[4,8,512]{2,1,0:T(8,128)S(1)} %copy-done.6), channel_id=1, source_target_pairs={{2,0},{4,2},{6,4},{8,6},{10,8},{12,10},{14,12},{15,14},{1,3},{3,5}... | collective-permute-start | bytes 196616 | tf_op jit(solution)/shard_map/ppermute | solution.py:268
  13.6 17.7 %collective-permute-start.3 = (f32[4,8,512]{2,1,0:T(8,128)S(1)}, f32[4,8,512]{2,1,0:T(8,128)S(1)}, u32[]{:S(2)}, u32[]{:S(2)}) collective-permute-start(f32[4,8,512]{2,1,0:T(8,128)S(1)} %copy-done.5), channel_id=1, source_target_pairs={{0,2},{2,4},{4,6},{6,8},{8,10},{10,12},{12,14},{14,15},{3,1},{5,3}... | collective-permute-start | bytes 196616 | tf_op jit(solution)/shard_map/ppermute | solution.py:267
  16.2 15.0 %collective-permute-start.5 = (f32[4,4,512]{2,1,0:T(4,128)S(1)}, f32[4,4,512]{2,1,0:T(4,128)S(1)}, u32[]{:S(2)}, u32[]{:S(2)}) collective-permute-start(f32[4,4,512]{2,1,0:T(4,128)S(1)} %copy-done.8), channel_id=1, source_target_pairs={{0,1},{1,0},{2,3},{3,2},{4,5},{5,4},{6,7},{7,6},{8,9},{9,8},{10,11... | collective-permute-start | bytes 98312 | tf_op jit(solution)/shard_map/ppermute | solution.py:269
  58.7 4.3 %collective-permute-start.6 = (f32[4,8,512]{2,1,0:T(8,128)S(1)}, f32[4,8,512]{2,1,0:T(8,128)S(1)}, u32[]{:S(2)}, u32[]{:S(2)}) collective-permute-start(f32[4,8,512]{2,1,0:T(8,128)S(1)} %get-tuple-element.62.own0), channel_id=1, source_target_pairs={{2,0},{4,2},{6,4},{8,6},{10,8},{12,10},{14,12},{15,14},{1,3},{3,5}... | collective-permute-start | bytes 196616 | tf_op jit(solution)/shard_map/ppermute | solution.py:268
  59.5 1.4 %collective-permute-start.7 = (f32[4,4,512]{2,1,0:T(4,128)S(1)}, f32[4,4,512]{2,1,0:T(4,128)S(1)}, u32[]{:S(2)}, u32[]{:S(2)}) collective-permute-start(f32[4,4,512]{2,1,0:T(4,128)S(1)} %get-tuple-element.63.face2), channel_id=1, source_target_pairs={{0,1},{1,0},{2,3},{3,2},{4,5},{5,4},{6,7},{7,6},{8,9},{9,8},{10,11... | collective-permute-start | bytes 98312 | tf_op jit(solution)/shard_map/ppermute | solution.py:269
  63.9 16.3 %all-to-all-start.2 = ((f32[16,49,1,128]{3,2,1,0:T(1,128)}), f32[16,49,1,128]{3,2,1,0:T(1,128)S(1)}, u32[]{:S(2)}, u32[]{:S(2)}) async-start(f32[16,49,1,128]{3,2,1,0:T(1,128)} %bitcast.5), calls=%async_computation.2 | async-start | bytes 802816 | tf_op jit(solution)/shard_map/all_to_all | solution.py:132
  67.9 4.0 %collective-permute-start.8 = (f32[4,8,512]{2,1,0:T(8,128)S(1)}, f32[4,8,512]{2,1,0:T(8,128)S(1)}, u32[]{:S(2)}, u32[]{:S(2)}) collective-permute-start(f32[4,8,512]{2,1,0:T(8,128)S(1)} %get-tuple-element.64.face0), channel_id=1, source_target_pairs={{0,2},{2,4},{4,6},{6,8},{8,10},{10,12},{12,14},{14,15},{3,1},{5,3}... | collective-permute-start | bytes 196616 | tf_op jit(solution)/shard_map/ppermute | solution.py:267
